TPU v7x, 32 devices: a whole 2x2x4 slice. The times are simulated.
32 devices in a mesh: fsdp: 8 (over y, x, core), tp: 4 (over z).
Axes of the slice: x: 2, y: 2, z: 4, core: 2. Of those that a mesh axis runs over, the one named last changes fastest.
Arguments:
- tokens: bfloat16 [1024, 16, 2048], P('tp', 'fsdp'), may hold values from -6 to 6
- lengths: int32 [16], P('fsdp'), may hold values from 512 to 1024, as said below
- routes: int32 [1024, 16, 8], P('tp', 'fsdp'), may hold values from 0 to 15, all different within a row
- slot_order: int32 [1024, 16, 8], P('tp', 'fsdp'), may hold values from 0 to 16383, as said below
- attn_gain: float32 [2048], replicated, may hold values from 0.5 to 1.5
- query_gain: float32 [128], replicated, may hold values from 0.5 to 1.5
- key_gain: float32 [128], replicated, may hold values from 0.5 to 1.5
- query_weight: bfloat16 [2048, 2048], P('fsdp', 'tp'), may hold values from -0.125 to 0.125
- key_weight: bfloat16 [2048, 2048], P('fsdp', 'tp'), may hold values from -0.125 to 0.125
- value_weight: bfloat16 [2048, 2048], P('fsdp', 'tp'), may hold values from -0.125 to 0.125
- out_weight: bfloat16 [2048, 2048], P('tp', 'fsdp'), may hold values from -0.5 to 0.5
- moe_gain: float32 [2048], replicated, may hold values from 0.5 to 1.5
- router_weight: bfloat16 [2048, 16], P('fsdp'), may hold values from -0.0625 to 0.0625
- gate_weight: bfloat16 [16, 2048, 1024], P(None, 'fsdp', 'tp'), may hold values from -0.125 to 0.125
- up_weight: bfloat16 [16, 2048, 1024], P(None, 'fsdp', 'tp'), may hold values from -0.125 to 0.125
- down_weight: bfloat16 [16, 1024, 2048], P(None, 'tp', 'fsdp'), may hold values from -1.5 to 1.5
- cotangent: bfloat16 [1024, 16, 2048], P('tp', 'fsdp'), may hold values from -6 to 6
Outputs:
- layer_out: bfloat16 [1024, 16, 2048], P('tp', 'fsdp')
- tokens_grad: float32 [1024, 16, 2048], P('tp', 'fsdp')
- attn_gain_grad: float32 [2048], replicated
- query_gain_grad: float32 [128], replicated
- key_gain_grad: float32 [128], replicated
- query_weight_grad: float32 [2048, 2048], P('fsdp', 'tp')
- key_weight_grad: float32 [2048, 2048], P('fsdp', 'tp')
- value_weight_grad: float32 [2048, 2048], P('fsdp', 'tp')
- out_weight_grad: float32 [2048, 2048], P('tp', 'fsdp')
- moe_gain_grad: float32 [2048], replicated
- router_grad: float32 [2048, 16], P('fsdp')
- gate_grad: float32 [16, 2048, 1024], P(None, 'fsdp', 'tp')
- up_grad: float32 [16, 2048, 1024], P(None, 'fsdp', 'tp')
- down_grad: float32 [16, 1024, 2048], P(None, 'tp', 'fsdp')
Inputs may be any that keep to these rules, and one draw needn't show every extreme that they name: `lengths`: in each group of 2 consecutive sequences one sequence has length 1024. `slot_order`: within each group of 2 consecutive sequences the values over all positions, sequences and choices are a permutation of 0 to 16383.
All inputs are finite; a program needn't handle non-finite values.
Results may differ from a plain program's by a relative error of at most 0.02.
Values may be sent and summed in bfloat16 or wider, within the bound.
A program may use at most 576 MiB of HBM per device.

v0:
```python
import jax
import jax.numpy as jnp
from jax import lax
from jax.sharding import PartitionSpec as P

EXPERTS = 16
TOP = 8
CAP = 1280


EPS = 1e-06
ROPE_BASE = 10000.0
NEG_FILL = -1e30


def rms_scale(values):
    return lax.rsqrt(jnp.mean(values * values, axis=-1, keepdims=True) + EPS)


def rope_tables(length, head_width):
    half_width = head_width // 2
    frequency = ROPE_BASE ** (-(jnp.arange(half_width, dtype=jnp.float32) * 2.0 / head_width))
    angles = jnp.arange(length, dtype=jnp.float32)[:, None] * frequency[None, :]
    return (jnp.cos(angles)[:, None, None, :], jnp.sin(angles)[:, None, None, :])


def rotate(values, cosine_table, sine_table):
    half_width = values.shape[-1] // 2
    lower_half = values[..., :half_width]
    upper_half = values[..., half_width:]
    return jnp.concatenate(
        [
            lower_half * cosine_table - upper_half * sine_table,
            lower_half * sine_table + upper_half * cosine_table,
        ],
        axis=-1,
    )


def norm_back(grad_in, raw_values, gain_values):
    scale_rows = rms_scale(raw_values)
    normed = raw_values * scale_rows
    scaled = grad_in * gain_values
    grad_raw = scale_rows * (scaled - normed * jnp.mean(scaled * normed, axis=-1, keepdims=True))
    grad_gain = jnp.sum(grad_in * normed, axis=tuple(range(grad_in.ndim - 1)))
    return (grad_raw, grad_gain)


def assign_slots(route_ids, order_ids, valid_rows):
    pair_count = route_ids.size
    route_flat = route_ids.reshape(-1)
    order_flat = order_ids.reshape(-1)
    valid_flat = jnp.broadcast_to(valid_rows[:, :, None], route_ids.shape).reshape(-1)
    positions = jnp.arange(pair_count, dtype=jnp.int32)
    inverse = jnp.zeros((pair_count,), jnp.int32).at[order_flat].set(positions)
    sorted_expert = route_flat[inverse]
    sorted_valid = valid_flat[inverse]
    expert_ids = jnp.arange(EXPERTS, dtype=jnp.int32)
    onehot = ((sorted_expert[:, None] == expert_ids[None, :]) & sorted_valid[:, None]).astype(
        jnp.int32
    )
    running = jnp.cumsum(onehot, axis=0)
    sorted_slot = jnp.sum((running - 1) * onehot, axis=1)
    slot_index = sorted_slot[order_flat]
    kept_pair = valid_flat & (slot_index < CAP)
    target = jnp.where(kept_pair, route_flat * CAP + slot_index, EXPERTS * CAP)
    token_rows = positions // TOP
    slot_rows = (
        jnp.full((EXPERTS * CAP,), pair_count // TOP, jnp.int32)
        .at[target]
        .set(token_rows, mode="drop")
    )
    return (target, slot_rows.reshape(EXPERTS, CAP))


def block_scores(query_rows, key_rows, key_valid, score_scale):
    raw_scores = (
        jnp.einsum("qhd,khd->hqk", query_rows, key_rows, preferred_element_type=jnp.float32)
        * score_scale
    )
    return jnp.where(key_valid[None, None, :], raw_scores, NEG_FILL)


def grouped(values, per_step):
    return values.reshape((values.shape[0] // per_step, per_step) + values.shape[1:])


def ungrouped(values):
    return values.reshape((values.shape[0] * values.shape[1],) + values.shape[2:])


def per_device(
    tokens,
    lengths,
    routes,
    slot_order,
    attn_gain,
    query_gain,
    key_gain,
    query_weight,
    key_weight,
    value_weight,
    out_weight,
    moe_gain,
    router_weight,
    gate_weight,
    up_weight,
    down_weight,
    cotangent,
):
    shard_len, seq_count, model_width = tokens.shape
    length = shard_len * lax.axis_size("tp")
    row_count = length * seq_count
    head_width = query_gain.shape[0]
    local_width = query_weight.shape[1]
    local_heads = local_width // head_width
    block_rows = min(512, length)
    score_scale = head_width ** (-0.5)
    per_step = 4
    own_positions = lax.axis_index("tp") * shard_len + jnp.arange(shard_len, dtype=jnp.int32)
    valid_own = own_positions[:, None] < lengths[None, :]
    valid_all = jnp.arange(length, dtype=jnp.int32)[:, None] < lengths[None, :]
    tokens_float = tokens.astype(jnp.float32)
    normed_own = (tokens_float * rms_scale(tokens_float) * attn_gain).astype(jnp.bfloat16)
    cot_own = cotangent.astype(jnp.float32) * valid_own[:, :, None].astype(jnp.float32)
    normed_all, cot_all = (
        lax.all_gather(normed_own, "tp", axis=0, tiled=True),
        lax.all_gather(cot_own.astype(jnp.bfloat16), "tp", axis=0, tiled=True),
    )
    routes_all, order_all = (
        lax.all_gather(routes, "tp", axis=0, tiled=True),
        lax.all_gather(slot_order, "tp", axis=0, tiled=True),
    )
    query_full, key_full, value_full, out_full = (
        lax.all_gather(query_weight, "fsdp", axis=0, tiled=True),
        lax.all_gather(key_weight, "fsdp", axis=0, tiled=True),
        lax.all_gather(value_weight, "fsdp", axis=0, tiled=True),
        lax.all_gather(out_weight, "fsdp", axis=1, tiled=True),
    )
    query_raw = jnp.einsum(
        "psd,dh->psh", normed_all, query_full, preferred_element_type=jnp.float32
    ).reshape(length, seq_count, local_heads, head_width)
    key_raw = jnp.einsum(
        "psd,dh->psh", normed_all, key_full, preferred_element_type=jnp.float32
    ).reshape(length, seq_count, local_heads, head_width)
    value_all = (
        jnp.einsum("psd,dh->psh", normed_all, value_full, preferred_element_type=jnp.float32)
        .astype(jnp.bfloat16)
        .reshape(length, seq_count, local_heads, head_width)
    )
    cosine_table, sine_table = rope_tables(length, head_width)
    query_all = rotate(
        query_raw * rms_scale(query_raw) * query_gain, cosine_table, sine_table
    ).astype(jnp.bfloat16)
    key_all = rotate(key_raw * rms_scale(key_raw) * key_gain, cosine_table, sine_table).astype(
        jnp.bfloat16
    )
    query_seq = jnp.moveaxis(query_all, 1, 0)
    key_seq = jnp.moveaxis(key_all, 1, 0)
    value_seq = jnp.moveaxis(value_all, 1, 0)
    key_valid_seq = jnp.transpose(valid_all)

    def attend(inputs_seq):
        query_rows, key_rows, value_rows, key_valid = inputs_seq
        out_parts = []
        total_parts = []
        for block_start in range(0, length, block_rows):
            scores = block_scores(
                query_rows[block_start : block_start + block_rows], key_rows, key_valid, score_scale
            )
            row_max = jnp.max(scores, axis=-1, keepdims=True)
            log_total = row_max + jnp.log(
                jnp.sum(jnp.exp(scores - row_max), axis=-1, keepdims=True)
            )
            probs_block = jnp.exp(scores - log_total).astype(jnp.bfloat16)
            out_parts.append(
                jnp.einsum(
                    "hqk,khd->qhd", probs_block, value_rows, preferred_element_type=jnp.float32
                )
            )
            total_parts.append(log_total[..., 0])
        return (jnp.concatenate(out_parts, axis=0), jnp.concatenate(total_parts, axis=1))

    attended_seq, log_seq = lax.map(attend, (query_seq, key_seq, value_seq, key_valid_seq))
    attended_low = (
        jnp.moveaxis(attended_seq, 0, 1)
        .astype(jnp.bfloat16)
        .reshape(length, seq_count, local_width)
    )
    branch_own = lax.psum_scatter(
        jnp.einsum("psh,hd->psd", attended_low, out_full, preferred_element_type=jnp.float32),
        "tp",
        scatter_dimension=0,
        tiled=True,
    )
    residual_own = tokens_float + branch_own
    moe_normed_own = (residual_own * rms_scale(residual_own) * moe_gain).astype(jnp.bfloat16)
    moe_normed_all = lax.all_gather(moe_normed_own, "tp", axis=0, tiled=True)
    gate_full, up_full, down_full, router_full = (
        lax.all_gather(gate_weight, "fsdp", axis=1, tiled=True),
        lax.all_gather(up_weight, "fsdp", axis=1, tiled=True),
        lax.all_gather(down_weight, "fsdp", axis=2, tiled=True),
        lax.all_gather(router_weight, "fsdp", axis=0, tiled=True),
    )
    gate_probs = jax.nn.softmax(
        jnp.einsum("psd,de->pse", moe_normed_all, router_full, preferred_element_type=jnp.float32),
        axis=-1,
    )
    target, slot_rows = assign_slots(routes_all, order_all, valid_all)
    pair_probs = jnp.take_along_axis(gate_probs, routes_all, axis=2).reshape(-1)
    slot_probs = (
        jnp.zeros((EXPERTS * CAP,), jnp.float32)
        .at[target]
        .set(pair_probs, mode="drop")
        .reshape(EXPERTS, CAP)
    )
    tokens_flat = moe_normed_all.reshape(row_count, model_width)
    cot_flat = cot_all.reshape(row_count, model_width)

    def expert_forward(accumulated, expert_in):
        gate_mat, up_mat, down_mat, row_ids, slot_gates = expert_in
        inputs = tokens_flat.at[row_ids].get(mode="fill", fill_value=0)
        gate_pre = jnp.einsum("ecd,edf->ecf", inputs, gate_mat, preferred_element_type=jnp.float32)
        up_pre = jnp.einsum("ecd,edf->ecf", inputs, up_mat, preferred_element_type=jnp.float32)
        hidden = (jax.nn.silu(gate_pre) * up_pre).astype(jnp.bfloat16)
        result = jnp.einsum("ecf,efd->ecd", hidden, down_mat, preferred_element_type=jnp.float32)
        cot_rows = cot_flat.at[row_ids].get(mode="fill", fill_value=0)
        slot_grad = jnp.sum(cot_rows.astype(jnp.float32) * result, axis=2)
        weighted = (slot_gates[:, :, None] * result).reshape(-1, model_width)
        accumulated = accumulated.at[row_ids.reshape(-1)].add(weighted, mode="drop")
        return (accumulated, (gate_pre, up_pre, slot_grad))

    forward_in = tuple(
        (grouped(item, per_step) for item in (gate_full, up_full, down_full, slot_rows, slot_probs))
    )
    moe_sum, (gate_kept, up_kept, slot_grads) = lax.scan(
        expert_forward, jnp.zeros((row_count, model_width), jnp.float32), forward_in
    )
    moe_own = lax.psum_scatter(
        moe_sum.reshape(length, seq_count, model_width).astype(jnp.bfloat16),
        "tp",
        scatter_dimension=0,
        tiled=True,
    ).astype(jnp.float32)
    layer_out = (residual_own + moe_own).astype(jnp.bfloat16)
    gate_back, up_back, down_back = (
        lax.all_gather(gate_weight, "fsdp", axis=1, tiled=True),
        lax.all_gather(up_weight, "fsdp", axis=1, tiled=True),
        lax.all_gather(down_weight, "fsdp", axis=2, tiled=True),
    )

    def expert_backward(accumulated, expert_in):
        gate_mat, up_mat, down_mat, row_ids, slot_gates, gate_pre, up_pre = expert_in
        inputs = tokens_flat.at[row_ids].get(mode="fill", fill_value=0)
        cot_rows = cot_flat.at[row_ids].get(mode="fill", fill_value=0)
        d_result = (slot_gates[:, :, None] * cot_rows.astype(jnp.float32)).astype(jnp.bfloat16)
        sigmoid_gate = jax.nn.sigmoid(gate_pre)
        activated = gate_pre * sigmoid_gate
        hidden = (activated * up_pre).astype(jnp.bfloat16)
        d_down = jnp.einsum("ecf,ecd->efd", hidden, d_result, preferred_element_type=jnp.float32)
        d_hidden = jnp.einsum(
            "ecd,efd->ecf", d_result, down_mat, preferred_element_type=jnp.float32
        )
        d_gate_pre = (
            d_hidden * up_pre * sigmoid_gate * (1.0 + gate_pre * (1.0 - sigmoid_gate))
        ).astype(jnp.bfloat16)
        d_up_pre = (d_hidden * activated).astype(jnp.bfloat16)
        d_gate_mat = jnp.einsum(
            "ecd,ecf->edf", inputs, d_gate_pre, preferred_element_type=jnp.float32
        )
        d_up_mat = jnp.einsum("ecd,ecf->edf", inputs, d_up_pre, preferred_element_type=jnp.float32)
        d_inputs = jnp.einsum(
            "ecf,edf->ecd", d_gate_pre, gate_mat, preferred_element_type=jnp.float32
        ) + jnp.einsum("ecf,edf->ecd", d_up_pre, up_mat, preferred_element_type=jnp.float32)
        accumulated = accumulated.at[row_ids.reshape(-1)].add(
            d_inputs.reshape(-1, model_width), mode="drop"
        )
        return (accumulated, (d_gate_mat, d_up_mat, d_down))

    backward_in = tuple(
        (grouped(item, per_step) for item in (gate_back, up_back, down_back, slot_rows, slot_probs))
    ) + (gate_kept, up_kept)
    moe_input_sum, (gate_grads, up_grads, down_grads) = lax.scan(
        expert_backward, jnp.zeros((row_count, model_width), jnp.float32), backward_in
    )
    gate_grad, up_grad, down_grad = (
        lax.psum_scatter(
            ungrouped(gate_grads).astype(jnp.bfloat16), "fsdp", scatter_dimension=1, tiled=True
        ).astype(jnp.float32),
        lax.psum_scatter(
            ungrouped(up_grads).astype(jnp.bfloat16), "fsdp", scatter_dimension=1, tiled=True
        ).astype(jnp.float32),
        lax.psum_scatter(
            ungrouped(down_grads).astype(jnp.bfloat16), "fsdp", scatter_dimension=2, tiled=True
        ).astype(jnp.float32),
    )
    pair_grads = (
        slot_grads.reshape(-1)
        .at[target]
        .get(mode="fill", fill_value=0.0)
        .reshape(length, seq_count, TOP)
    )
    moe_input_own, pair_grads_own = (
        lax.psum_scatter(
            moe_input_sum.reshape(length, seq_count, model_width),
            "tp",
            scatter_dimension=0,
            tiled=True,
        ),
        lax.psum_scatter(pair_grads, "tp", scatter_dimension=0, tiled=True),
    )
    probs_own = jax.nn.softmax(
        jnp.einsum("psd,de->pse", moe_normed_own, router_full, preferred_element_type=jnp.float32),
        axis=-1,
    )
    picked = (routes[..., None] == jnp.arange(EXPERTS, dtype=jnp.int32)).astype(jnp.float32)
    gate_dense = jnp.sum(pair_grads_own[..., None] * picked, axis=2)
    d_logits = (
        probs_own * (gate_dense - jnp.sum(probs_own * gate_dense, axis=-1, keepdims=True))
    ).astype(jnp.bfloat16)
    router_term = jnp.einsum(
        "psd,pse->de", moe_normed_own, d_logits, preferred_element_type=jnp.float32
    )
    moe_input_own = moe_input_own + jnp.einsum(
        "pse,de->psd", d_logits, router_full, preferred_element_type=jnp.float32
    )
    residual_grad, moe_gain_term = norm_back(moe_input_own, residual_own, moe_gain)
    residual_grad = residual_grad + cot_own
    piece_rows = lax.all_gather(residual_grad.astype(jnp.bfloat16), "tp", axis=0, tiled=True)
    out_grad_acc = jnp.einsum(
        "psh,psd->hd", attended_low, piece_rows, preferred_element_type=jnp.float32
    )
    grad_rows = jnp.einsum("psd,hd->psh", piece_rows, out_full, preferred_element_type=jnp.float32)
    attended_grad_acc = grad_rows
    attended_grad_seq = jnp.moveaxis(
        attended_grad_acc.astype(jnp.bfloat16).reshape(length, seq_count, local_heads, head_width),
        1,
        0,
    )

    def attend_back(inputs_seq):
        query_rows, key_rows, value_rows, key_valid, log_rows, grad_rows = inputs_seq
        query_parts = []
        key_grad = jnp.zeros(key_rows.shape, jnp.float32)
        value_grad = jnp.zeros(value_rows.shape, jnp.float32)
        for block_start in range(0, length, block_rows):
            query_block = query_rows[block_start : block_start + block_rows]
            grad_block = grad_rows[block_start : block_start + block_rows]
            scores = block_scores(query_block, key_rows, key_valid, score_scale)
            probs_block = jnp.exp(
                scores - log_rows[:, block_start : block_start + block_rows, None]
            )
            value_grad = value_grad + jnp.einsum(
                "hqk,qhd->khd",
                probs_block.astype(jnp.bfloat16),
                grad_block,
                preferred_element_type=jnp.float32,
            )
            d_probs = jnp.einsum(
                "qhd,khd->hqk", grad_block, value_rows, preferred_element_type=jnp.float32
            )
            d_scores = (
                probs_block * (d_probs - jnp.sum(probs_block * d_probs, axis=-1, keepdims=True))
            ).astype(jnp.bfloat16)
            query_parts.append(
                jnp.einsum("hqk,khd->qhd", d_scores, key_rows, preferred_element_type=jnp.float32)
                * score_scale
            )
            key_grad = (
                key_grad
                + jnp.einsum(
                    "hqk,qhd->khd", d_scores, query_block, preferred_element_type=jnp.float32
                )
                * score_scale
            )
        return (jnp.concatenate(query_parts, axis=0), key_grad, value_grad)

    query_grad_seq, key_grad_seq, value_grad_seq = lax.map(
        attend_back, (query_seq, key_seq, value_seq, key_valid_seq, log_seq, attended_grad_seq)
    )
    query_turned = rotate(jnp.moveaxis(query_grad_seq, 0, 1), cosine_table, -sine_table)
    key_turned = rotate(jnp.moveaxis(key_grad_seq, 0, 1), cosine_table, -sine_table)
    query_raw_grad, query_gain_term = norm_back(query_turned, query_raw, query_gain)
    key_raw_grad, key_gain_term = norm_back(key_turned, key_raw, key_gain)
    query_low = query_raw_grad.astype(jnp.bfloat16).reshape(length, seq_count, local_width)
    key_low = key_raw_grad.astype(jnp.bfloat16).reshape(length, seq_count, local_width)
    value_low = (
        jnp.moveaxis(value_grad_seq, 0, 1)
        .astype(jnp.bfloat16)
        .reshape(length, seq_count, local_width)
    )
    query_grads = jnp.einsum(
        "psd,psh->dh", normed_all, query_low, preferred_element_type=jnp.float32
    )
    key_grads = jnp.einsum("psd,psh->dh", normed_all, key_low, preferred_element_type=jnp.float32)
    value_grads = jnp.einsum(
        "psd,psh->dh", normed_all, value_low, preferred_element_type=jnp.float32
    )
    query_weight_grad, key_weight_grad, value_weight_grad, out_weight_grad = (
        lax.psum_scatter(
            query_grads.astype(jnp.bfloat16), "fsdp", scatter_dimension=0, tiled=True
        ).astype(jnp.float32),
        lax.psum_scatter(
            key_grads.astype(jnp.bfloat16), "fsdp", scatter_dimension=0, tiled=True
        ).astype(jnp.float32),
        lax.psum_scatter(
            value_grads.astype(jnp.bfloat16), "fsdp", scatter_dimension=0, tiled=True
        ).astype(jnp.float32),
        lax.psum_scatter(
            out_grad_acc.astype(jnp.bfloat16), "fsdp", scatter_dimension=1, tiled=True
        ).astype(jnp.float32),
    )
    summed = jnp.zeros((shard_len * lax.axis_size("tp"), seq_count, model_width), jnp.float32)
    for grad_low, weight_full in (
        (query_low, query_full),
        (key_low, key_full),
        (value_low, value_full),
    ):
        grad_rows = grad_low
        summed = summed + jnp.einsum(
            "psh,dh->psd", grad_rows, weight_full, preferred_element_type=jnp.float32
        )
    normed_grad_own = lax.psum_scatter(
        summed.astype(jnp.bfloat16), "tp", scatter_dimension=0, tiled=True
    ).astype(jnp.float32)
    tokens_grad, attn_gain_term = norm_back(normed_grad_own, tokens_float, attn_gain)
    tokens_grad = tokens_grad + residual_grad
    small_sums = lax.psum(
        (attn_gain_term, query_gain_term, key_gain_term, moe_gain_term, router_term), ("fsdp", "tp")
    )
    router_rows = model_width // lax.axis_size("fsdp")
    router_grad = lax.dynamic_slice_in_dim(
        small_sums[4], lax.axis_index("fsdp") * router_rows, router_rows, 0
    )
    return (
        layer_out,
        tokens_grad,
        small_sums[0],
        small_sums[1],
        small_sums[2],
        query_weight_grad,
        key_weight_grad,
        value_weight_grad,
        out_weight_grad,
        small_sums[3],
        router_grad,
        gate_grad,
        up_grad,
        down_grad,
    )


def solution(mesh):
    return jax.shard_map(
        per_device,
        mesh=mesh,
        in_specs=(
            P("tp", "fsdp", None),
            P("fsdp"),
            P("tp", "fsdp", None),
            P("tp", "fsdp", None),
            P(),
            P(),
            P(),
            P("fsdp", "tp"),
            P("fsdp", "tp"),
            P("fsdp", "tp"),
            P("tp", "fsdp"),
            P(),
            P("fsdp", None),
            P(None, "fsdp", "tp"),
            P(None, "fsdp", "tp"),
            P(None, "tp", "fsdp"),
            P("tp", "fsdp", None),
        ),
        out_specs=(
            P("tp", "fsdp", None),
            P("tp", "fsdp", None),
            P(),
            P(),
            P(),
            P("fsdp", "tp"),
            P("fsdp", "tp"),
            P("fsdp", "tp"),
            P("tp", "fsdp"),
            P(),
            P("fsdp", None),
            P(None, "fsdp", "tp"),
            P(None, "fsdp", "tp"),
            P(None, "tp", "fsdp"),
        ),
        check_vma=False,
    )
```

profile of v0, /device:TPU:0, one launch (start us, length us, event | category | flops | bytes accessed | tf_op | source)
XLA Modules:
  0.0 4958.3 jit_solution(10807798498983442579)
XLA Ops:
  41.4 151.8 %all-gather.12.cloned.1.call-done = bf16[1024,2,2048]{2,0,1:T(8,128)(2,1)} async-done(((bf16[256,2,2048]{2,0,1:T(8,128)(2,1)}), bf16[1024,2,2048]{2,0,1:T(8,128)(2,1)}) %all-gather.12.cloned.1.call-update) | async-done | bytes 8388624 | tf_op jit(solution)/shard_map/all_gather | solution.py:127
  311.5 275.1 %reduce-scatter.12.cloned.1.call-done = f32[256,2,2048]{2,0,1:T(8,128)} async-done(((f32[1024,2,2048]{2,0,1:T(8,128)}), f32[256,2,2048]{2,0,1:T(8,128)}) %reduce-scatter.12.cloned.1.call-update) | async-done | bytes 4194320 | tf_op jit(solution)/shard_map/reduce_scatter | solution.py:190
  680.4 100.9 %gather_fusion.5 = pred[16384]{0:T(1024)(128)(4,1)S(1)} fusion(pred[16384]{0:T(1024)(128)(4,1)S(1)} %reshape.572, s32[16384]{0:T(1024)S(1)} %fusion.190), kind=kCustom, calls=%fused_computation.5 | custom fusion | bytes 98304 | tf_op jit(solution)/shard_map/gather | solution.py:57
  809.1 90.5 %gather_fusion.4 = s32[16384]{0:T(1024)S(1)} fusion(s32[16384]{0:T(1024)S(1)} %reshape.570, s32[16384]{0:T(1024)S(1)} %fusion.190), kind=kCustom, calls=%fused_computation.4 | custom fusion | bytes 196608 | tf_op jit(solution)/shard_map/gather | solution.py:56
  901.7 90.5 %gather_fusion.6 = s32[16384]{0:T(1024)S(1)} fusion(s32[16384]{0:T(1024)S(1)} %fusion.177, s32[16384]{0:T(1024)S(1)} %broadcast_clamp_fusion.3), kind=kCustom, calls=%fused_computation.6 | custom fusion | bytes 196608 | tf_op jit(solution)/shard_map/gather | solution.py:64
  1132.0 157.0 %gather_fusion.8 = f32[16384]{0:T(1024)S(1)} fusion(f32[1024,2,16]{0,2,1:T(8,128)S(1)} %fusion.172, s32[16384]{0:T(1024)S(1)} %reshape.648), kind=kCustom, calls=%fused_computation.8 | custom fusion | bytes 327680 | tf_op jit(solution)/shard_map/jit(take_along_axis)/gather | solution.py:210
  1362.1 886.9 %while.63 = (s32[]{:T(128)}, f32[2048,2048]{1,0:T(8,128)}, f32[4,4,1280,256]{3,2,1,0:T(8,128)}, f32[4,4,1280,256]{3,2,1,0:T(8,128)}, f32[4,4,1280]{2,1,0:T(4,128...) while((s32[]{:T(128)}, f32[2048,2048]{1,0:T(8,128)}, ...), condition=%wide.region_22.23_spmd.clone, body=%wide.region_19.22_spmd.sunk.clone | while | flops 16197939200 | bytes 359250112 | solution.py:236
  1507.1 75.9 %scatter_fusion = f32[2048,2048]{1,0:T(8,128)} fusion(f32[2048,2048]{1,0:T(8,128)} %get-tuple-element.1028, s32[5120]{0:T(1024)S(1)} %bitcast.633, f32[5120,2048]{1,0:T(8,128)} %bitcast.608), kind=kCustom, calls=%fused_computation.9.clone.1.clone | custom fusion | flops 10485760 | bytes 125849600 | tf_op jit(solution)/shard_map/while/body/eval_jaxpr/scatter-add | solution.py:230
  1728.7 75.9 %scatter_fusion = f32[2048,2048]{1,0:T(8,128)} fusion(f32[2048,2048]{1,0:T(8,128)} %get-tuple-element.1028, s32[5120]{0:T(1024)S(1)} %bitcast.633, f32[5120,2048]{1,0:T(8,128)} %bitcast.608), kind=kCustom, calls=%fused_computation.9.clone.1.clone | custom fusion | flops 10485760 | bytes 125849600 | tf_op jit(solution)/shard_map/while/body/eval_jaxpr/scatter-add | solution.py:230
  1950.4 75.9 %scatter_fusion = f32[2048,2048]{1,0:T(8,128)} fusion(f32[2048,2048]{1,0:T(8,128)} %get-tuple-element.1028, s32[5120]{0:T(1024)S(1)} %bitcast.633, f32[5120,2048]{1,0:T(8,128)} %bitcast.608), kind=kCustom, calls=%fused_computation.9.clone.1.clone | custom fusion | flops 10485760 | bytes 125849600 | tf_op jit(solution)/shard_map/while/body/eval_jaxpr/scatter-add | solution.py:230
  2172.1 75.9 %scatter_fusion = f32[2048,2048]{1,0:T(8,128)} fusion(f32[2048,2048]{1,0:T(8,128)} %get-tuple-element.1028, s32[5120]{0:T(1024)S(1)} %bitcast.633, f32[5120,2048]{1,0:T(8,128)} %bitcast.608), kind=kCustom, calls=%fused_computation.9.clone.1.clone | custom fusion | flops 10485760 | bytes 125849600 | tf_op jit(solution)/shard_map/while/body/eval_jaxpr/scatter-add | solution.py:230
  2250.0 90.5 %gather_fusion.7 = f32[16384]{0:T(1024)S(1)} fusion(f32[20480]{0:T(1024)S(1)} %reshape.581, s32[16384]{0:T(1024)S(1)} %copy-done.55), kind=kCustom, calls=%fused_computation.7 | custom fusion | bytes 196608 | tf_op jit(solution)/shard_map/gather | solution.py:300
  2351.9 1105.1 %while.64 = (s32[]{:T(128)}, f32[2048,2048]{1,0:T(8,128)}, bf16[4,4,2048,256]{3,2,1,0:T(8,128)(2,1)}, bf16[4,4,2048,256]{3,2,1,0:T(8,128)(2,1)}, bf16[4,4,256,20...) while((s32[]{:T(128)}, f32[2048,2048]{1,0:T(8,128)}, ...), condition=%wide.region_26.27_spmd.clone, body=%wide.region_24.26_spmd.sunk.clone | while | flops 32363053056 | bytes 494398656 | solution.py:283
  2550.9 76.0 %scatter_fusion.1 = f32[2048,2048]{1,0:T(8,128)} fusion(f32[2048,2048]{1,0:T(8,128)} %get-tuple-element.1066, s32[5120]{0:T(1024)S(1)} %bitcast.634, f32[5120,2048]{1,0:T(8,128)} %bitcast.607), kind=kCustom, calls=%fused_computation.10.clone.1.clone | custom fusion | flops 10485760 | bytes 125849600 | tf_op jit(solution)/shard_map/while/body/eval_jaxpr/scatter-add | solution.py:275
  2825.8 76.0 %scatter_fusion.1 = f32[2048,2048]{1,0:T(8,128)} fusion(f32[2048,2048]{1,0:T(8,128)} %get-tuple-element.1066, s32[5120]{0:T(1024)S(1)} %bitcast.634, f32[5120,2048]{1,0:T(8,128)} %bitcast.607), kind=kCustom, calls=%fused_computation.10.clone.1.clone | custom fusion | flops 10485760 | bytes 125849600 | tf_op jit(solution)/shard_map/while/body/eval_jaxpr/scatter-add | solution.py:275
  3100.5 76.0 %scatter_fusion.1 = f32[2048,2048]{1,0:T(8,128)} fusion(f32[2048,2048]{1,0:T(8,128)} %get-tuple-element.1066, s32[5120]{0:T(1024)S(1)} %bitcast.634, f32[5120,2048]{1,0:T(8,128)} %bitcast.607), kind=kCustom, calls=%fused_computation.10.clone.1.clone | custom fusion | flops 10485760 | bytes 125849600 | tf_op jit(solution)/shard_map/while/body/eval_jaxpr/scatter-add | solution.py:275
  3375.2 76.0 %scatter_fusion.1 = f32[2048,2048]{1,0:T(8,128)} fusion(f32[2048,2048]{1,0:T(8,128)} %get-tuple-element.1066, s32[5120]{0:T(1024)S(1)} %bitcast.634, f32[5120,2048]{1,0:T(8,128)} %bitcast.607), kind=kCustom, calls=%fused_computation.10.clone.1.clone | custom fusion | flops 10485760 | bytes 125849600 | tf_op jit(solution)/shard_map/while/body/eval_jaxpr/scatter-add | solution.py:275
  3498.6 274.4 %reduce-scatter.16.cloned.1.call-done = f32[256,2,2048]{2,0,1:T(8,128)} async-done(((f32[1024,2,2048]{2,0,1:T(8,128)}), f32[256,2,2048]{2,0,1:T(8,128)}) %reduce-scatter.16.cloned.1.call-update) | async-done | bytes 4194320 | tf_op jit(solution)/shard_map/reduce_scatter | solution.py:304
  3789.9 143.8 %all-gather.32.cloned.1.call-done = bf16[1024,2,2048]{2,0,1:T(8,128)(2,1)} async-done(((bf16[256,2,2048]{2,0,1:T(8,128)(2,1)}), bf16[1024,2,2048]{2,0,1:T(8,128)(2,1)}) %all-gather.32.cloned.1.call-update) | async-done | bytes 8388624 | tf_op jit(solution)/shard_map/all_gather | solution.py:329
  3956.9 91.2 %while.65 = (s32[]{:T(128)}, f32[2,1024,4,128]{1,3,2,0:T(8,128)}, f32[2,1024,4,128]{1,3,2,0:T(8,128)}, bf16[2,1024,4,128]{1,3,2,0:T(8,128)(2,1)}, bf16[2,1024,4,...) while((s32[]{:T(128)}, f32[2,1024,4,128]{1,3,2,0:T(8,128)}, ...), condition=%wide.region_37.38_spmd.clone, body=%wide.region_34.37_spmd.sunk.clone | while | flops 5434241024 | bytes 289568704 | solution.py:378
  4184.3 115.7 %reduce-scatter.28.cloned.1.call-done = bf16[16,256,256]{2,1,0:T(8,128)(2,1)} async-done(((bf16[16,2048,256]{2,1,0:T(8,128)(2,1)}), bf16[16,256,256]{2,1,0:T(8,128)(2,1)}) %reduce-scatter.28.cloned.1.call-update) | async-done | bytes 2097168 | tf_op jit(solution)/shard_map/reduce_scatter | solution.py:287
  4304.1 115.7 %reduce-scatter.32.cloned.1.call-done = bf16[16,256,256]{2,1,0:T(8,128)(2,1)} async-done(((bf16[16,256,2048]{2,1,0:T(8,128)(2,1)}), bf16[16,256,256]{2,1,0:T(8,128)(2,1)}) %reduce-scatter.32.cloned.1.call-update) | async-done | bytes 2097168 | tf_op jit(solution)/shard_map/reduce_scatter | solution.py:293
  4600.9 145.2 %reduce-scatter.18.cloned.1.call-done = bf16[256,2,2048]{2,0,1:T(8,128)(2,1)} async-done(((bf16[1024,2,2048]{2,0,1:T(8,128)(2,1)}), bf16[256,2,2048]{2,0,1:T(8,128)(2,1)}) %reduce-scatter.18.cloned.1.call-update) | async-done | bytes 2097168 | tf_op jit(solution)/shard_map/reduce_scatter | solution.py:423
  4750.2 143.5 %reduce-scatter.14.cloned.1.call-done = bf16[256,2,2048]{2,0,1:T(8,128)(2,1)} async-done(((bf16[1024,2,2048]{2,0,1:T(8,128)(2,1)}), bf16[256,2,2048]{2,0,1:T(8,128)(2,1)}) %reduce-scatter.14.cloned.1.call-update) | async-done | bytes 2097168 | tf_op jit(solution)/shard_map/reduce_scatter | solution.py:239
  (609 shorter events, 2461.7 us)
Async XLA Ops:
  7.2 34.2 all-gather.18.cloned.1.call-start
  9.2 184.0 %all-gather.12.cloned.1.call-start = ((), (), s32[]{:S(2)}) async-start(), calls=%async_computation.11 | async-start | bytes 10485760 | tf_op jit(solution)/shard_map/all_gather | solution.py:127
  15.9 206.2 %all-gather.16.cloned.1.call-start = ((), (), s32[]{:S(2)}) async-start(), calls=%async_computation.13 | async-start | bytes 2359296 | tf_op jit(solution)/shard_map/all_gather | solution.py:135
  16.8 235.8 %all-gather.14.cloned.1.call-start = ((), (), s32[]{:S(2)}) async-start(), calls=%async_computation.12 | async-start | bytes 2359296 | tf_op jit(solution)/shard_map/all_gather | solution.py:137
  17.7 275.1 %all-gather.20.cloned.1.call-start = ((), (), s32[]{:S(2)}) async-start(), calls=%async_computation.15 | async-start | bytes 2359296 | tf_op jit(solution)/shard_map/all_gather | solution.py:138
  18.3 568.3 %reduce-scatter.12.cloned.1.call-start = ((), (), s32[]{:S(2)}) async-start(), calls=%async_computation.16 | async-start | bytes 20971520 | tf_op jit(solution)/shard_map/reduce_scatter | solution.py:190
  306.1 760.5 %all-gather.30.cloned.1.call-start = ((), (), s32[]{:S(2)}) async-start(), calls=%async_computation.21 | async-start | bytes 10485760 | tf_op jit(solution)/shard_map/all_gather | solution.py:128
  311.4 785.0 %all-gather.22.cloned.1.call-start = ((), (), s32[]{:S(2)}) async-start(), calls=%async_computation.17 | async-start | bytes 10485760 | tf_op jit(solution)/shard_map/all_gather | solution.py:198
  594.0 760.2 %all-gather.24.cloned.1.call-start = ((), (), s32[]{:S(2)}) async-start(), calls=%async_computation.18 | async-start | bytes 18874368 | tf_op jit(solution)/shard_map/all_gather | solution.py:200
  594.7 759.5 %all-gather.26.cloned.1.call-start = ((), (), s32[]{:S(2)}) async-start(), calls=%async_computation.19 | async-start | bytes 18874368 | tf_op jit(solution)/shard_map/all_gather | solution.py:201
  595.3 758.9 %all-gather.28.cloned.1.call-start = ((), (), s32[]{:S(2)}) async-start(), calls=%async_computation.20 | async-start | bytes 18874368 | tf_op jit(solution)/shard_map/all_gather | solution.py:202
  596.1 2901.3 %all-reduce.7.cloned.1.call-start = ((), (), s32[]{:S(2)}) async-start(), calls=%async_computation.34 | async-start | bytes 2097152
  2343.9 1429.1 %reduce-scatter.16.cloned.1.call-start = ((), (), s32[]{:S(2)}) async-start(), calls=%async_computation.23 | async-start | bytes 20971520 | tf_op jit(solution)/shard_map/reduce_scatter | solution.py:304
  3494.8 438.9 %all-gather.32.cloned.1.call-start = ((), (), s32[]{:S(2)}) async-start(), calls=%async_computation.24 | async-start | bytes 10485760 | tf_op jit(solution)/shard_map/all_gather | solution.py:329
  3783.2 387.5 %all-reduce.5.cloned.1.call-start = ((), (), s32[]{:S(2)}) async-start(), calls=%async_computation.30 | async-start | bytes 262144 | tf_op jit(solution)/shard_map/psum | solution.py:428
  3784.3 395.9 %reduce-scatter.30.cloned.1.call-start = ((), (), s32[]{:S(2)}) async-start(), calls=%async_computation.32 | async-start | bytes 18874368 | tf_op jit(solution)/shard_map/reduce_scatter | solution.py:290
  3784.9 515.1 %reduce-scatter.28.cloned.1.call-start = ((), (), s32[]{:S(2)}) async-start(), calls=%async_computation.31 | async-start | bytes 18874368 | tf_op jit(solution)/shard_map/reduce_scatter | solution.py:287
  3785.5 634.4 %reduce-scatter.32.cloned.1.call-start = ((), (), s32[]{:S(2)}) async-start(), calls=%async_computation.33 | async-start | bytes 18874368 | tf_op jit(solution)/shard_map/reduce_scatter | solution.py:293
  3786.1 678.7 %reduce-scatter.26.cloned.1.call-start = ((), (), s32[]{:S(2)}) async-start(), calls=%async_computation.29 | async-start | bytes 2359296 | tf_op jit(solution)/shard_map/reduce_scatter | solution.py:409
  3956.8 552.4 %reduce-scatter.22.cloned.1.call-start = ((), (), s32[]{:S(2)}) async-start(), calls=%async_computation.27 | async-start | bytes 2359296 | tf_op jit(solution)/shard_map/reduce_scatter | solution.py:403
  4065.8 488.3 %reduce-scatter.24.cloned.1.call-start = ((), (), s32[]{:S(2)}) async-start(), calls=%async_computation.28 | async-start | bytes 2359296 | tf_op jit(solution)/shard_map/reduce_scatter | solution.py:406
  4075.4 523.8 %reduce-scatter.20.cloned.1.call-start = ((), (), s32[]{:S(2)}) async-start(), calls=%async_computation.26 | async-start | bytes 2359296 | tf_op jit(solution)/shard_map/reduce_scatter | solution.py:400
  4096.1 650.0 %reduce-scatter.18.cloned.1.call-start = ((), (), s32[]{:S(2)}) async-start(), calls=%async_computation.25 | async-start | bytes 10485760 | tf_op jit(solution)/shard_map/reduce_scatter | solution.py:423
  4135.8 757.9 %reduce-scatter.14.cloned.1.call-start = ((), (), s32[]{:S(2)}) async-start(), calls=%async_computation.22 | async-start | bytes 10485760 | tf_op jit(solution)/shard_map/reduce_scatter | solution.py:239
  (114 other events, 7819.2 us)
Sparse Core Ops, SparseCore 0:
  10.5 30.8 all-gather.17
  43.5 149.6 all-gather.11
  195.7 26.3 all-gather.15
  224.4 28.1 all-gather.13
  254.3 28.1 all-gather.19
  306.2 280.3 reduce-scatter.11
  588.8 151.3 all-gather.29
  742.4 148.8 all-gather.21
  893.4 87.9 all-gather.23
  983.3 90.0 all-gather.25
  1075.5 93.0 all-gather.27
  2344.0 49.3 all-reduce.6
  3495.0 277.9 reduce-scatter.15
  3783.3 150.3 all-gather.31
  3940.6 120.6 all-reduce.4
  4065.2 115.0 reduce-scatter.29
  4184.1 115.9 reduce-scatter.27
  4303.9 115.9 reduce-scatter.31
  4423.5 41.2 reduce-scatter.25
  4467.9 41.1 reduce-scatter.21
  4512.8 41.2 reduce-scatter.23
  4557.9 41.1 reduce-scatter.19
  4601.6 144.4 reduce-scatter.17
  4748.4 145.1 reduce-scatter.13
where the time goes:
time: 4970 us; the launch traced here: 4960 us
  local copies, waits for them, and re-layouts  1640 us (33%)
  waiting for transfers between devices  1590 us (32%)
  matrix products  873 us (18%)
  other arithmetic  734 us (15%)
  blocking collectives  88.1 us (2%)
    gather x16, local copies, waits for them, and re-layouts, expert_forward(): inputs = tokens_flat.at[row_ids].get(mode='fill', fill_value=0)  693 us
    scatter-add x4, other arithmetic, expert_backward(): accumulated.at[row_ids.reshape(-1)]  304 us
    scatter-add x4, other arithmetic, expert_forward(): accumulated = accumulated.at[row_ids.reshape(-1)].add(weighted, mode='drop')  304 us
    reduce_scatter x1, waiting for transfers between devices, per_device(): lax.psum_scatter(jnp.einsum('psh,hd->psd', attended_low, out_full, prefer...  275 us
    reduce_scatter x1, waiting for transfers between devices, per_device(): lax.psum_scatter(moe_input_sum.reshape(length, seq_count, model_width), '...  274 us
    gather x5, local copies, waits for them, and re-layouts, per_device(): pair_probs = jnp.take_along_axis(gate_probs, routes_all, axis=2).reshape(-1)  161 us
    all_gather x1, waiting for transfers between devices, per_device(): lax.all_gather(normed_own, 'tp', axis=0, tiled=True)  152 us
    reduce_scatter x1, waiting for transfers between devices, per_device(): lax.psum_scatter(summed.astype(jnp.bfloat16), 'tp', scatter_dimension=0,...  145 us
  transfers between devices with their start and end apart: 24, of which 16 were waited for; matrix products, arithmetic and copies ran while one was open for 44% of the time, Pallas kernels for 0%

commit v1 on v0

v1 whole, which is shorter than its diff:
```python
import functools

import jax
import jax.numpy as jnp
from jax import lax
from jax.experimental import pallas as pl
from jax.experimental.pallas import tpu as pltpu
from jax.sharding import PartitionSpec as P

EXPERTS = 16
TOP = 8
CAP = 1280
LANES = 128

EPS = 1e-06
ROPE_BASE = 10000.0
NEG_FILL = -1e30
FAR = 1 << 20
BF = jnp.bfloat16
F32 = jnp.float32
VMEM_BYTES = 58 * 1024 * 1024


def dot_nn(a, b):
    return lax.dot_general(a, b, (((1,), (0,)), ((), ())), preferred_element_type=F32)


def dot_nt(a, b):
    return lax.dot_general(a, b, (((1,), (1,)), ((), ())), preferred_element_type=F32)


def dot_tn(a, b):
    return lax.dot_general(a, b, (((0,), (0,)), ((), ())), preferred_element_type=F32)


def params(steps):
    return pltpu.CompilerParams(
        dimension_semantics=("arbitrary",) * steps, vmem_limit_bytes=VMEM_BYTES
    )


def cost(macs, nbytes, exps=0):
    return pl.CostEstimate(flops=2 * macs, bytes_accessed=nbytes, transcendentals=exps)


def struct(shape, dtype):
    return jax.ShapeDtypeStruct(shape, dtype)


def rms_scale(values):
    return lax.rsqrt(jnp.mean(values * values, axis=-1, keepdims=True) + EPS)


def norm_back(grad_in, raw_values, gain_values):
    scale_rows = rms_scale(raw_values)
    normed = raw_values * scale_rows
    scaled = grad_in * gain_values
    grad_raw = scale_rows * (scaled - normed * jnp.mean(scaled * normed, axis=-1, keepdims=True))
    grad_gain = jnp.sum(grad_in * normed, axis=tuple(range(grad_in.ndim - 1)))
    return (grad_raw, grad_gain)


def shift(value, count, step):
    return lax.ppermute(value, "tp", [(i, (i + step) % count) for i in range(count)])


def ring_gather(value, count, step=1):
    held = [value]
    for _ in range(count - 1):
        held.append(shift(held[-1], count, step))
    return held


def ring_scatter(parts, step=1):
    count = len(parts)
    total = parts[1]
    for k in range(2, count + 1):
        arrived = shift(total, count, step)
        if k < count:
            total = (arrived.astype(F32) + parts[k].astype(F32)).astype(BF)
    return arrived.astype(F32) + parts[0].astype(F32)


def keep_kernel(bits, order_ref, keep_ref):
    count, experts, rows = order_ref.shape

    def below(limit):
        found = jnp.zeros((experts, 1), jnp.int32)
        for k in range(count):
            found = found + jnp.sum(
                (order_ref[k] < limit).astype(jnp.int32), axis=1, keepdims=True
            )
        return found

    last = jnp.zeros((experts, 1), jnp.int32)
    for bit in range(bits - 1, -1, -1):
        trial = last + (1 << bit)
        last = jnp.where(below(trial) < CAP, trial, last)
    for k in range(count):
        keep = (order_ref[k] <= last).astype(F32)
        wide = jnp.concatenate([keep, jnp.zeros((LANES - experts, rows), F32)], axis=0)
        keep_ref[k] = wide.T


def keep_rows(order_all, pair_count):
    count, experts, rows = order_all.shape
    return pl.pallas_call(
        functools.partial(keep_kernel, pair_count.bit_length() + 1),
        out_shape=struct((count, rows, LANES), F32),
        compiler_params=pltpu.CompilerParams(vmem_limit_bytes=VMEM_BYTES),
        cost_estimate=cost(16 * count * experts * rows, count * rows * LANES * 4),
        name="keep_rows",
    )(order_all)


def qkv_kernel(seqs, x_ref, wq_ref, wk_ref, wv_ref, cos_ref, sin_ref, gq_ref, gk_ref, *rest):
    qr_ref, kr_ref, q_ref, k_ref, v_ref = rest[-5:]
    rows = x_ref.shape[0] // seqs
    width = wq_ref.shape[1]
    heads = width // LANES
    x = x_ref[...]
    for w_ref, raw_ref, low_ref, gain_ref in (
        (wq_ref, qr_ref, q_ref, gq_ref),
        (wk_ref, kr_ref, k_ref, gk_ref),
    ):
        raw = dot_nn(x, w_ref[...])
        for s in range(seqs):
            for h in range(heads):
                part = raw[s * rows : (s + 1) * rows, h * LANES : (h + 1) * LANES]
                raw_ref[0, s, :, h * LANES : (h + 1) * LANES] = part
                normed = part * rms_scale(part) * gain_ref[...]
                turned = normed * cos_ref[0] + pltpu.roll(normed, LANES // 2, 1) * sin_ref[0]
                low_ref[0, s, :, h * LANES : (h + 1) * LANES] = turned.astype(BF)
    value = dot_nn(x, wv_ref[...]).astype(BF)
    for s in range(seqs):
        v_ref[0, s] = value[s * rows : (s + 1) * rows]


def project(k, count, seqs, x, weights, cos, sin, gain_q, gain_k, kept):
    rows, depth = x.shape
    local = (weights.shape[1] - LANES) // 3
    group = min(256, local)
    groups = local // group
    per = rows // seqs
    const = lambda *shape: pl.BlockSpec(shape, lambda g: (0,) * len(shape))
    table = pl.BlockSpec((1, per, LANES), lambda g: (k, 0, 0))
    out = pl.BlockSpec((1, seqs, per, group), lambda g: (k, 0, 0, g))
    shapes = [struct((count, seqs, per, local), d) for d in (F32, F32, BF, BF, BF)]
    aliased = list(kept or ())
    return pl.pallas_call(
        functools.partial(qkv_kernel, seqs),
        grid=(groups,),
        in_specs=[
            const(rows, depth),
            pl.BlockSpec((depth, group), lambda g: (0, g)),
            pl.BlockSpec((depth, group), lambda g: (0, groups + g)),
            pl.BlockSpec((depth, group), lambda g: (0, 2 * groups + g)),
            table,
            table,
            const(1, LANES),
            const(1, LANES),
        ]
        + [pl.BlockSpec(memory_space=pl.ANY)] * len(aliased),
        out_specs=[out] * 5,
        out_shape=shapes,
        input_output_aliases={8 + i: i for i in range(len(aliased))},
        compiler_params=params(1),
        cost_estimate=cost(rows * depth * local * 3, rows * depth * 2 + depth * local * 6),
        name="project",
    )(x, weights, weights, weights, cos, sin, gain_q, gain_k, *aliased)


def attend_kernel(scale, q_ref, k_ref, v_ref, valid_ref, o_ref, lse_ref):
    count, _, rows, width = q_ref.shape
    length = count * rows
    keys = k_ref[...].reshape(length, width)
    values_t = v_ref[...].reshape(length, width).astype(F32).T.astype(BF)
    valid = valid_ref[0][:, :1] > 0
    for i in range(count):
        scores = dot_nt(keys, q_ref[i, 0]) * scale
        weights = jnp.exp(jnp.where(valid, scores, NEG_FILL))
        total = jnp.sum(weights, axis=0, keepdims=True)
        out_t = dot_nn(values_t, weights.astype(BF)) / total
        o_ref[i, 0] = out_t.T.astype(BF)
        lse_ref[0, i : i + 1, :] = jnp.log(total)


def attend(q, k, v, valid, scale):
    count, seqs, rows, local = q.shape
    heads = local // LANES
    head = pl.BlockSpec((count, 1, rows, LANES), lambda s, h: (0, s, 0, h))
    return pl.pallas_call(
        functools.partial(attend_kernel, scale),
        grid=(seqs, heads),
        in_specs=[head, head, head, pl.BlockSpec((1, count * rows, LANES), lambda s, h: (s, 0, 0))],
        out_specs=[head, pl.BlockSpec((1, count, rows), lambda s, h: (s * heads + h, 0, 0))],
        out_shape=[struct(q.shape, BF), struct((seqs * heads, count, rows), F32)],
        compiler_params=params(2),
        cost_estimate=cost(
            2 * seqs * local * (count * rows) ** 2,
            4 * count * seqs * rows * local * 2,
            seqs * heads * (count * rows) ** 2,
        ),
        name="attend",
    )(q, k, v, valid)


def attend_back_kernel(scale, *refs):
    q_ref, k_ref, v_ref, o_ref, do_ref, lse_ref, valid_ref = refs[:7]
    qr_ref, kr_ref, cos_ref, sin_ref, gq_ref, gk_ref = refs[7:13]
    dq_ref, dk_ref, dv_ref, gains_ref = refs[13:17]
    dk_acc, dv_acc = refs[17:]
    count, _, rows, width = q_ref.shape
    length = count * rows
    first = jnp.logical_and(pl.program_id(0) == 0, pl.program_id(1) == 0)

    @pl.when(first)
    def _():
        gains_ref[...] = jnp.zeros_like(gains_ref)

    keys = k_ref[...].reshape(length, width)
    keys_t = keys.astype(F32).T.astype(BF)
    values = v_ref[...].reshape(length, width)
    valid = valid_ref[0][:, :1] > 0
    ones = jnp.ones((8, width), F32)

    def back(grad, raw, cos, sin, gain):
        turned = grad * cos - pltpu.roll(grad, LANES // 2, 1) * sin
        scale_rows = rms_scale(raw)
        normed = raw * scale_rows
        scaled = turned * gain
        mean = jnp.mean(scaled * normed, axis=-1, keepdims=True)
        return scale_rows * (scaled - normed * mean), jnp.sum(
            turned * normed, axis=0, keepdims=True
        )

    gain_q = jnp.zeros((1, width), F32)
    gain_k = jnp.zeros((1, width), F32)
    for i in range(count):
        query = q_ref[i, 0]
        grad = do_ref[i, 0]
        scores = dot_nt(keys, query) * scale
        weights = jnp.exp(jnp.where(valid, scores, NEG_FILL) - lse_ref[0, i : i + 1, :])
        delta = jnp.sum(
            (grad.astype(F32) * o_ref[i, 0].astype(F32)).T, axis=0, keepdims=True
        )
        d_weights = dot_nt(values, grad)
        d_scores = (weights * (d_weights - delta)).astype(BF)
        dv_part = dot_nn(weights.astype(BF), grad)
        dk_part = dot_nn(d_scores, query)
        if i == 0:
            dv_acc[...] = dv_part
            dk_acc[...] = dk_part
        else:
            dv_acc[...] += dv_part
            dk_acc[...] += dk_part
        dq = (dot_nn(keys_t, d_scores) * scale).T
        d_raw, d_gain = back(dq, qr_ref[i, 0], cos_ref[i], sin_ref[i], gq_ref[...])
        gain_q = gain_q + d_gain
        dq_ref[i, 0] = d_raw.astype(BF)
    for i in range(count):
        dv_ref[i, 0] = dv_acc[i * rows : (i + 1) * rows].astype(BF)
        dk = dk_acc[i * rows : (i + 1) * rows] * scale
        d_raw, d_gain = back(dk, kr_ref[i, 0], cos_ref[i], sin_ref[i], gk_ref[...])
        gain_k = gain_k + d_gain
        dk_ref[i, 0] = d_raw.astype(BF)
    gains_ref[0:1, :] += gain_q
    gains_ref[1:2, :] += gain_k


def attend_back(q, k, v, o, do, lse, valid, q_raw, k_raw, cos, sin, gain_q, gain_k, scale):
    count, seqs, rows, local = q.shape
    heads = local // LANES
    head = pl.BlockSpec((count, 1, rows, LANES), lambda s, h: (0, s, 0, h))
    const = lambda *shape: pl.BlockSpec(shape, lambda s, h: (0,) * len(shape))
    return pl.pallas_call(
        functools.partial(attend_back_kernel, scale),
        grid=(seqs, heads),
        in_specs=[
            head,
            head,
            head,
            head,
            head,
            pl.BlockSpec((1, count, rows), lambda s, h: (s * heads + h, 0, 0)),
            pl.BlockSpec((1, count * rows, LANES), lambda s, h: (s, 0, 0)),
            head,
            head,
            const(count, rows, LANES),
            const(count, rows, LANES),
            const(1, LANES),
            const(1, LANES),
        ],
        out_specs=[head, head, head, const(8, LANES)],
        out_shape=[struct(q.shape, BF)] * 3 + [struct((8, LANES), F32)],
        scratch_shapes=[pltpu.VMEM((count * rows, LANES), F32)] * 2,
        compiler_params=params(2),
        cost_estimate=cost(
            5 * seqs * local * (count * rows) ** 2,
            12 * count * seqs * rows * local * 2,
            seqs * heads * (count * rows) ** 2,
        ),
        name="attend_back",
    )(q, k, v, o, do, lse, valid, q_raw, k_raw, cos, sin, gain_q, gain_k)


def input_back_kernel(dq_ref, dk_ref, dv_ref, wq_ref, wk_ref, wv_ref, out_ref):
    total = None
    for d_ref, w_ref in ((dq_ref, wq_ref), (dk_ref, wk_ref), (dv_ref, wv_ref)):
        grad = d_ref[0].reshape(out_ref.shape[0], w_ref.shape[1])
        part = dot_nt(grad, w_ref[...])
        total = part if total is None else total + part
    out_ref[...] = total.astype(BF)


def input_back(k, dq, dk, dv, weights):
    _, seqs, per, local = dq.shape
    depth = weights.shape[0]
    rows = seqs * per
    tile = min(512, depth)
    grad = pl.BlockSpec((1, seqs, per, local), lambda t: (k, 0, 0, 0))
    return pl.pallas_call(
        input_back_kernel,
        grid=(depth // tile,),
        in_specs=[grad] * 3
        + [pl.BlockSpec((tile, local), lambda t, j=j: (t, j)) for j in range(3)],
        out_specs=pl.BlockSpec((rows, tile), lambda t: (0, t)),
        out_shape=struct((rows, depth), BF),
        compiler_params=params(1),
        cost_estimate=cost(rows * depth * local * 3, rows * depth * 2 + depth * local * 6),
        name="input_back",
    )(dq, dk, dv, weights, weights, weights)


def out_kernel(count, tok_ref, *refs):
    ob_refs = refs[:count]
    w_ref, x1_ref = refs[count:]
    local = ob_refs[0].shape[1]
    total = tok_ref[...].astype(F32)
    for s in range(count):
        total = total + dot_nn(ob_refs[s][...], w_ref[0, s * local : (s + 1) * local, :])
    x1_ref[...] = total


def out_project(tok, parts, weights):
    rows, depth = tok.shape
    blocks, full, tile = weights.shape
    count = len(parts)
    return pl.pallas_call(
        functools.partial(out_kernel, count),
        grid=(blocks,),
        in_specs=[pl.BlockSpec((rows, tile), lambda j: (0, j))]
        + [pl.BlockSpec(parts[0].shape, lambda j: (0, 0))] * count
        + [pl.BlockSpec((1, full, tile), lambda j: (j, 0, 0))],
        out_specs=pl.BlockSpec((rows, tile), lambda j: (0, j)),
        out_shape=struct((rows, depth), F32),
        compiler_params=params(1),
        cost_estimate=cost(rows * depth * full, rows * depth * 8 + full * depth * 2),
        name="out_project",
    )(tok, *parts, weights)


def out_back_kernel(db_ref, w_ref, out_ref):
    blocks, _, tile = w_ref.shape
    total = None
    for j in range(blocks):
        part = dot_nt(db_ref[:, j * tile : (j + 1) * tile], w_ref[j])
        total = part if total is None else total + part
    out_ref[0] = total.astype(BF)


def out_back(db, weights, count):
    rows, depth = db.shape
    blocks, full, tile = weights.shape
    local = full // count
    return pl.pallas_call(
        out_back_kernel,
        grid=(count,),
        in_specs=[
            pl.BlockSpec((rows, depth), lambda s: (0, 0)),
            pl.BlockSpec((blocks, local, tile), lambda s: (0, s, 0)),
        ],
        out_specs=pl.BlockSpec((1, rows, local), lambda s: (s, 0, 0)),
        out_shape=struct((count, rows, local), BF),
        compiler_params=params(1),
        cost_estimate=cost(rows * depth * full, rows * depth * 2 + full * depth * 2),
        name="out_back",
    )(db, weights)


def expert_kernel(n2_ref, c_ref, keep_ref, router_ref, g_ref, u_ref, d_ref, *rest):
    hp_ref, da_ref, du_ref, y_ref, dn_ref, dl_ref = rest[-12:-6]
    probs, gates, grads, y_acc, dn_acc, d_full = rest[-6:]
    e = pl.program_id(0)
    experts = pl.num_programs(0)
    blocks, _, _, tile = d_ref.shape
    rows = n2_ref.shape[0]
    lane = lax.broadcasted_iota(jnp.int32, (rows, LANES), 1)

    @pl.when(e == 0)
    def _():
        logits = jnp.where(lane < EXPERTS, dot_nn(n2_ref[...], router_ref[...]), NEG_FILL)
        raised = jnp.exp(logits - jnp.max(logits, axis=-1, keepdims=True))
        soft = raised / jnp.sum(raised, axis=-1, keepdims=True)
        probs[...] = soft
        gates[...] = soft * keep_ref[0]
        grads[...] = jnp.zeros_like(grads)

    for j in range(blocks):
        d_full[:, j * tile : (j + 1) * tile] = d_ref[j, 0]
    here = lane == e
    gate = jnp.sum(jnp.where(here, gates[...], 0.0), axis=-1, keepdims=True)
    x = n2_ref[...]
    pre = dot_nn(x, g_ref[0])
    up = dot_nn(x, u_ref[0])
    back = dot_nt(c_ref[...], d_full[...])
    sig = 1.0 / (1.0 + jnp.exp(-pre))
    act = pre * sig
    hid = act * up
    hp = (hid * gate).astype(BF)
    column = jnp.sum(back * hid, axis=-1, keepdims=True)
    grads[...] += jnp.where(here, column * keep_ref[0], 0.0)
    dh = back * gate
    du = (dh * act).astype(BF)
    da = (dh * up * (sig + act * (1.0 - sig))).astype(BF)
    hp_ref[0] = hp
    da_ref[0] = da
    du_ref[0] = du
    y_part = dot_nn(hp, d_full[...])
    dn_part = dot_nt(da, g_ref[0]) + dot_nt(du, u_ref[0])

    @pl.when(e == 0)
    def _():
        y_acc[...] = y_part
        dn_acc[...] = dn_part

    @pl.when(e > 0)
    def _():
        y_acc[...] += y_part
        dn_acc[...] += dn_part

    @pl.when(e == experts - 1)
    def _():
        soft = probs[...]
        gd = grads[...]
        dl = (soft * (gd - jnp.sum(soft * gd, axis=-1, keepdims=True))).astype(BF)
        dl_ref[0] = dl
        y_ref[...] = y_acc[...].astype(BF)
        dn_ref[...] = (dn_acc[...] + dot_nt(dl, router_ref[...])).astype(BF)


def experts_pass(k, count, n2, cot, keep, weights_all, gate_w, up_w, down_w, kept):
    rows, depth = n2.shape
    experts, _, ff = gate_w.shape
    blocks, _, _, tile = down_w.shape
    router_col = weights_all.shape[1] // LANES - 1
    const = lambda *shape: pl.BlockSpec(shape, lambda e: (0,) * len(shape))
    wide = pl.BlockSpec((1, rows, ff), lambda e: (k, 0, e))
    aliased = list(kept or ())
    return pl.pallas_call(
        expert_kernel,
        grid=(experts,),
        in_specs=[
            const(rows, depth),
            const(rows, depth),
            pl.BlockSpec((1, rows, LANES), lambda e: (k, 0, 0)),
            pl.BlockSpec((depth, LANES), lambda e: (0, router_col)),
            pl.BlockSpec((1, depth, ff), lambda e: (e, 0, 0)),
            pl.BlockSpec((1, depth, ff), lambda e: (e, 0, 0)),
            pl.BlockSpec((blocks, 1, ff, tile), lambda e: (0, e, 0, 0)),
        ]
        + [pl.BlockSpec(memory_space=pl.ANY)] * len(aliased),
        out_specs=[
            wide,
            wide,
            wide,
            const(rows, depth),
            const(rows, depth),
            pl.BlockSpec((1, rows, LANES), lambda e: (k, 0, 0)),
        ],
        out_shape=[struct((count, rows, experts * ff), BF)] * 3
        + [struct((rows, depth), BF)] * 2
        + [struct((count, rows, LANES), BF)],
        input_output_aliases=dict(zip(range(7, 11), (0, 1, 2, 5))) if aliased else {},
        scratch_shapes=[
            pltpu.VMEM((rows, LANES), F32),
            pltpu.VMEM((rows, LANES), F32),
            pltpu.VMEM((rows, LANES), F32),
            pltpu.VMEM((rows, depth), F32),
            pltpu.VMEM((rows, depth), F32),
            pltpu.VMEM((ff, depth), BF),
        ],
        compiler_params=params(1),
        cost_estimate=cost(
            6 * rows * depth * ff * experts,
            3 * experts * depth * ff * 2 + 4 * rows * depth * 2 + 3 * rows * experts * ff * 2,
            2 * rows * ff * experts,
        ),
        name="experts",
    )(n2, cot, keep, weights_all, gate_w, up_w, down_w, *aliased)


def per_device(
    tokens,
    lengths,
    routes,
    slot_order,
    attn_gain,
    query_gain,
    key_gain,
    query_weight,
    key_weight,
    value_weight,
    out_weight,
    moe_gain,
    router_weight,
    gate_weight,
    up_weight,
    down_weight,
    cotangent,
):
    per, seqs, depth = tokens.shape
    count = lax.axis_size("tp")
    me = lax.axis_index("tp")
    length = per * count
    rows = seqs * per
    head_width = query_gain.shape[0]
    local = query_weight.shape[1]
    scale = head_width ** (-0.5)

    first = jnp.concatenate(
        [
            query_weight,
            key_weight,
            value_weight,
            jnp.pad(router_weight, ((0, 0), (0, LANES - EXPERTS))),
        ],
        axis=1,
    )
    weights_all = lax.all_gather(first, "fsdp", axis=0, tiled=True)

    tok = jnp.transpose(tokens, (1, 0, 2)).reshape(rows, depth)
    tok_float = tok.astype(F32)
    n1_own = (tok_float * rms_scale(tok_float) * attn_gain).astype(BF)
    n1 = ring_gather(n1_own, count)

    out_rows = jnp.concatenate(ring_gather(out_weight, count, -1), axis=0)
    out_all = lax.all_gather(out_rows, "fsdp", axis=0, tiled=False)
    gate_all = lax.all_gather(gate_weight, "fsdp", axis=1, tiled=True)
    up_all = lax.all_gather(up_weight, "fsdp", axis=1, tiled=True)
    down_all = lax.all_gather(down_weight, "fsdp", axis=0, tiled=False)

    own_pos = me * per + jnp.arange(per, dtype=jnp.int32)
    valid_own = own_pos[None, :] < lengths[:, None]
    route_t = jnp.transpose(routes, (2, 1, 0)).reshape(TOP, rows)
    order_t = jnp.transpose(slot_order, (2, 1, 0)).reshape(TOP, rows)
    names = jnp.arange(EXPERTS, dtype=jnp.int32)[:, None]
    order_own = jnp.full((EXPERTS, rows), FAR, jnp.int32)
    for j in range(TOP):
        order_own = jnp.where(route_t[j][None, :] == names, order_t[j][None, :], order_own)
    order_own = jnp.where(valid_own.reshape(1, rows), order_own, FAR)
    order_all = jnp.stack(ring_gather(order_own, count))
    keep = keep_rows(order_all, length * seqs * TOP)

    owner = (me - jnp.arange(count, dtype=jnp.int32)) % count
    chunk_pos = owner[:, None] * per + jnp.arange(per, dtype=jnp.int32)[None, :]
    half = head_width // 2
    frequency = ROPE_BASE ** (-(jnp.arange(half, dtype=F32) * 2.0 / head_width))
    angles = chunk_pos.astype(F32)[:, :, None] * frequency
    cos_half, sin_half = jnp.cos(angles), jnp.sin(angles)
    cos = jnp.concatenate([cos_half, cos_half], axis=-1)
    sin = jnp.concatenate([-sin_half, sin_half], axis=-1)
    key_valid = (chunk_pos.reshape(1, length) < lengths[:, None]).astype(F32)
    key_valid = jnp.broadcast_to(key_valid[:, :, None], (seqs, length, LANES))

    gain_q, gain_k = query_gain[None, :], key_gain[None, :]
    kept = None
    for k in range(count):
        kept = project(k, count, seqs, n1[k], weights_all, cos, sin, gain_q, gain_k, kept)
    q_raw, k_raw, q, k_low, v = kept

    cot = jnp.transpose(cotangent, (1, 0, 2)).reshape(rows, depth)
    cot_own = jnp.where(valid_own.reshape(rows, 1), cot, jnp.zeros_like(cot))
    cot_own, _ = lax.optimization_barrier((cot_own, n1[-1]))
    cots = ring_gather(cot_own, count)

    ob, lse = attend(q, k_low, v, key_valid, scale)
    ob_rows = ob.reshape(count, rows, local)
    ob_parts = [ob_rows[0]] + [shift(ob_rows[s], count, -s) for s in range(1, count)]
    x1 = out_project(tok, ob_parts, out_all)
    n2_own = (x1 * rms_scale(x1) * moe_gain).astype(BF)
    n2 = ring_gather(n2_own, count)

    kept = None
    y_parts, dn_parts = [], []
    for k in range(count):
        hp, da, du, y_k, dn_k, dl = experts_pass(
            k, count, n2[k], cots[k], keep, weights_all, gate_all, up_all, down_all, kept
        )
        kept = (hp, da, du, dl)
        y_parts.append(y_k)
        dn_parts.append(dn_k)
    dn2 = ring_scatter(dn_parts)

    n2_all = jnp.concatenate(n2, axis=0)
    cot_all = jnp.concatenate(cots, axis=0)
    all_rows = count * rows
    ff = gate_weight.shape[2]

    def expert_grad(left, right):
        full = dot_tn(left, right.reshape(all_rows, EXPERTS * ff)).astype(BF)
        own = lax.psum_scatter(full, "fsdp", scatter_dimension=0, tiled=True)
        return own.reshape(own.shape[0], EXPERTS, ff)

    gate_grad = jnp.transpose(expert_grad(n2_all, da), (1, 0, 2)).astype(F32)
    up_grad = jnp.transpose(expert_grad(n2_all, du), (1, 0, 2)).astype(F32)
    down_grad = jnp.transpose(expert_grad(cot_all, hp), (1, 2, 0)).astype(F32)
    router_term = dot_tn(n2_all, dl.reshape(all_rows, LANES))[:, :EXPERTS]

    moe_back, moe_gain_term = norm_back(dn2, x1, moe_gain)
    dx1 = moe_back + cot_own.astype(F32)
    db = dx1.astype(BF)
    dob = out_back(db, out_all, count)
    dob_parts = [dob[0]] + [shift(dob[s], count, s) for s in range(1, count)]
    d_ob = jnp.stack(dob_parts).reshape(count, seqs, per, local)

    y_sum = ring_scatter(y_parts)
    layer_out = (x1 + y_sum).astype(BF)

    ob_cat = jnp.concatenate(ob_parts, axis=1)
    out_full = dot_tn(db, ob_cat).astype(BF)
    out_sum = lax.psum_scatter(out_full, "fsdp", scatter_dimension=0, tiled=True)
    out_pieces = [out_sum[:, s * local : (s + 1) * local] for s in range(count)]
    out_weight_grad = jnp.transpose(ring_scatter(out_pieces, -1))

    dq, dk, dv, gains = attend_back(
        q, k_low, v, ob, d_ob, lse, key_valid, q_raw, k_raw, cos, sin, gain_q, gain_k, scale
    )
    dn1_parts = [None] * count
    for k in list(range(1, count)) + [0]:
        dn1_parts[k] = input_back(k, dq, dk, dv, weights_all)
    dn1 = ring_scatter(dn1_parts)
    n1_all = jnp.concatenate(n1, axis=0)
    d_all = jnp.concatenate([d.reshape(all_rows, local) for d in (dq, dk, dv)], axis=1)
    qkv_full = dot_tn(n1_all, d_all).astype(BF)
    qkv_sum = lax.psum_scatter(qkv_full, "fsdp", scatter_dimension=0, tiled=True).astype(F32)

    attn_back, attn_gain_term = norm_back(dn1, tok_float, attn_gain)
    tokens_grad = attn_back + dx1

    small = lax.psum(
        (attn_gain_term, gains[0], gains[1], moe_gain_term, router_term), ("fsdp", "tp")
    )
    router_rows = depth // lax.axis_size("fsdp")
    router_grad = lax.dynamic_slice_in_dim(
        small[4], lax.axis_index("fsdp") * router_rows, router_rows, 0
    )

    def back_to_positions(value):
        return jnp.transpose(value.reshape(seqs, per, depth), (1, 0, 2))

    return (
        back_to_positions(layer_out),
        back_to_positions(tokens_grad),
        small[0],
        small[1],
        small[2],
        qkv_sum[:, :local],
        qkv_sum[:, local : 2 * local],
        qkv_sum[:, 2 * local :],
        out_weight_grad,
        small[3],
        router_grad,
        gate_grad,
        up_grad,
        down_grad,
    )


def solution(mesh):
    return jax.shard_map(
        per_device,
        mesh=mesh,
        in_specs=(
            P("tp", "fsdp", None),
            P("fsdp"),
            P("tp", "fsdp", None),
            P("tp", "fsdp", None),
            P(),
            P(),
            P(),
            P("fsdp", "tp"),
            P("fsdp", "tp"),
            P("fsdp", "tp"),
            P("tp", "fsdp"),
            P(),
            P("fsdp", None),
            P(None, "fsdp", "tp"),
            P(None, "fsdp", "tp"),
            P(None, "tp", "fsdp"),
            P("tp", "fsdp", None),
        ),
        out_specs=(
            P("tp", "fsdp", None),
            P("tp", "fsdp", None),
            P(),
            P(),
            P(),
            P("fsdp", "tp"),
            P("fsdp", "tp"),
            P("fsdp", "tp"),
            P("tp", "fsdp"),
            P(),
            P("fsdp", None),
            P(None, "fsdp", "tp"),
            P(None, "fsdp", "tp"),
            P(None, "tp", "fsdp"),
        ),
        check_vma=False,
    )
```

time: 4970 us -> 1520 us (0.31)
  local copies, waits for them, and re-layouts: 1640 us -> 44.5 us
  waiting for transfers between devices: 1590 us -> 665 us
  matrix products: 873 us -> 168 us
  other arithmetic: 734 us -> 59.7 us
  Pallas kernels: 0 us -> 465 us
  starting transfers between devices: 1.26 us -> 56.1 us
    reduce_scatter x11 -> x5, waiting for transfers between devices: 1250 us -> 0.03 us  [the longest x1 0.02 us: per_device(): lax.psum_scatter(out_full, 'fsdp', scatter_dimension=0, tiled=True)]
    gather x29 -> x0, local copies, waits for them, and re-layouts: 1230 us -> none  [the longest x16 693 us: expert_forward(): inputs = tokens_flat.at[row_ids].get(mode='fill', fill_value=0)]
    dot_general x78 -> x6, matrix products: 866 us -> 168 us  [dot_tn(): lax.dot_general(a, b, (((0,), (0,)), ((), ())), preferred_element_type=F32)]
    ppermute x0 -> x33, waiting for transfers between devices: none -> 663 us  [shift(): lax.ppermute(value, 'tp', [(i, (i + step) % count) for i in range(count)])]
    scatter-add x8 -> x0, other arithmetic: 608 us -> none  [the longest x4 304 us: expert_backward(): accumulated.at[row_ids.reshape(-1)]]
    pallas_call x0 -> x17, Pallas kernels: none -> 465 us  [the longest x4 314 us: experts_pass(): pl.pallas_call(expert_kernel, grid=(experts,), in_specs=[const(rows, dept...]
    all_gather x11 -> x5, waiting for transfers between devices: 343 us -> 0.06 us  [the longest x1 0.02 us: per_device(): gate_all = lax.all_gather(gate_weight, 'fsdp', axis=1, tiled=True)]
    scatter x3 -> x0, local copies, waits for them, and re-layouts: 181 us -> none  [the longest x1 60.6 us: per_device(): slot_probs = jnp.zeros((EXPERTS * CAP,), jnp.float32).at[target].set(pair...]
  transfers between devices with their start and end apart: 24 -> 44, of which waited for: 16 -> 22; matrix products, arithmetic and copies ran while one was open for 44% -> 17% of each run, Pallas kernels for 0% -> 31%
where the time goes in v1:
time: 1520 us; the launch traced here: 1510 us
  waiting for transfers between devices  665 us (44%)
  Pallas kernels  465 us (31%)
  matrix products  168 us (11%)
  other arithmetic  59.7 us (4%)
  starting transfers between devices  56.1 us (4%)
  local copies, waits for them, and re-layouts  44.5 us (3%)
  blocking collectives  38.5 us (3%)
    ppermute x33, waiting for transfers between devices, shift(): lax.ppermute(value, 'tp', [(i, (i + step) % count) for i in range(count)])  663 us
    pallas_call x4, Pallas kernels, experts_pass(): pl.pallas_call(expert_kernel, grid=(experts,), in_specs=[const(rows, dept...  314 us
    dot_general x6, matrix products, dot_tn(): lax.dot_general(a, b, (((0,), (0,)), ((), ())), preferred_element_type=F32)  168 us
    ppermute x33, starting transfers between devices, shift(): lax.ppermute(value, 'tp', [(i, (i + step) % count) for i in range(count)])  55.7 us
    pallas_call x1, Pallas kernels, attend_back(): pl.pallas_call(functools.partial(attend_back_kernel, scale), grid=(seqs,...  38.6 us
    psum x1, blocking collectives, per_device(): lax.psum((attn_gain_term, gains[0], gains[1], moe_gain_term, router_term)...  38.5 us
    pallas_call x4, Pallas kernels, project(): pl.pallas_call(functools.partial(qkv_kernel, seqs), grid=(groups,), in_sp...  37.7 us
    pallas_call x4, Pallas kernels, input_back(): pl.pallas_call(input_back_kernel, grid=(depth // tile,), in_specs=[grad]...  31.7 us
  transfers between devices with their start and end apart: 44, of which 22 were waited for; matrix products, arithmetic and copies ran while one was open for 17% of the time, Pallas kernels for 31%

profile of v1, /device:TPU:0, one launch (start us, length us, event | category | flops | bytes accessed | tf_op | source)
XLA Modules:
  0.0 1510.9 jit_solution(558267693417528901)
XLA Ops:
  49.2 47.0 %collective-permute-done.x_ref = bf16[512,2048]{1,0:T(8,128)(2,1)} collective-permute-done((bf16[512,2048]{1,0:T(8,128)(2,1)S(1)}, bf16[512,2048]{1,0:T(8,128)(2,1)}, u32[]{:S(2)}, u32[]{:S(2)}) %collective-permute-start) | collective-permute-done | bytes 2097184 | tf_op jit(solution)/shard_map/ppermute | solution.py:64
  96.2 45.8 %collective-permute-done.1.x_ref = bf16[512,2048]{1,0:T(8,128)(2,1)} collective-permute-done((bf16[512,2048]{1,0:T(8,128)(2,1)}, bf16[512,2048]{1,0:T(8,128)(2,1)}, u32[]{:S(2)}, u32[]{:S(2)}) %collective-permute-start.1) | collective-permute-done | bytes 2097184 | tf_op jit(solution)/shard_map/ppermute | solution.py:64
  197.0 18.3 %attend.1 = (bf16[4,2,256,512]{3,2,1,0:T(8,128)(2,1)}, f32[8,4,256]{2,1,0:T(4,128)}) custom-call(bf16[4,2,256,512]{3,2,1,0:T(8,128)(2,1)} %get-tuple-element.80.q_ref.refs_0_, bf16[4,2,256,512]{3,2,1,0:T(8,128)(2,1)} %get-tuple-element.81.k_ref.refs_1_, bf16[4,2,256,512]{3,2,1,0:T(8,128)(2,1)} %get-tuple-element.82.v_ref.refs_2_, ...), custom_call_target="tpu_custom_call" | custom-call | flops 4294967296 | bytes 8388608 | tf_op jit(solution)/shard_map/attend/pallas_call | solution.py:192
  222.3 93.1 %collective-permute-done.4.refs_2_ = bf16[512,512]{1,0:T(8,128)(2,1)S(1)} collective-permute-done((bf16[512,512]{1,0:T(8,128)(2,1)S(1)}, bf16[512,512]{1,0:T(8,128)(2,1)S(1)}, u32[]{:S(2)}, u32[]{:S(2)}) %collective-permute-start.4) | collective-permute-done | bytes 524320 | tf_op jit(solution)/shard_map/ppermute | solution.py:64
  343.7 44.8 %collective-permute-done.9.n2_ref = bf16[512,2048]{1,0:T(8,128)(2,1)S(1)} collective-permute-done((bf16[512,2048]{1,0:T(8,128)(2,1)S(1)}, bf16[512,2048]{1,0:T(8,128)(2,1)S(1)}, u32[]{:S(2)}, u32[]{:S(2)}) %collective-permute-start.9) | collective-permute-done | bytes 2097184 | tf_op jit(solution)/shard_map/ppermute | solution.py:64
  391.1 87.0 %collective-permute-done.11 = s32[16,512]{1,0:T(8,128)S(1)} collective-permute-done((s32[16,512]{1,0:T(8,128)S(1)}, s32[16,512]{1,0:T(8,128)S(1)}, u32[]{:S(2)}, u32[]{:S(2)}) %collective-permute-start.11) | collective-permute-done | bytes 32800 | tf_op jit(solution)/shard_map/ppermute | solution.py:64
  494.1 78.3 %experts.4 = (bf16[4,512,4096]{2,1,0:T(8,128)(2,1)}, bf16[4,512,4096]{2,1,0:T(8,128)(2,1)}, bf16[4,512,4096]{2,1,0:T(8,128)(2,1)}, bf16[512,2048]{1,0:T(8,128)(2...) custom-call(bf16[512,2048]{1,0:T(8,128)(2,1)} %copy-done.14, bf16[512,2048]{1,0:T(8,128)(2,1)} %copy-done.5, ...), custom_call_target="tpu_custom_call" | custom-call | flops 51539607552 | bytes 71303168 | tf_op jit(solution)/shard_map/experts/pallas_call | solution.py:460
  572.4 78.9 %experts.5 = (bf16[4,512,4096]{2,1,0:T(8,128)(2,1)}, bf16[4,512,4096]{2,1,0:T(8,128)(2,1)}, bf16[4,512,4096]{2,1,0:T(8,128)(2,1)}, bf16[512,2048]{1,0:T(8,128)(2...) custom-call(bf16[512,2048]{1,0:T(8,128)(2,1)} %copy-done.42, ...), custom_call_target="tpu_custom_call", output_to_operand_aliasing={{0}: (7, {}), {1}: (8, {}), {2}: (9, {}), {5}: (10, {})} | custom-call | flops 51539607552 | bytes 71303168 | tf_op jit(solution)/shard_map/experts/pallas_call | solution.py:460
  652.0 78.6 %experts.6 = (bf16[4,512,4096]{2,1,0:T(8,128)(2,1)}, bf16[4,512,4096]{2,1,0:T(8,128)(2,1)}, bf16[4,512,4096]{2,1,0:T(8,128)(2,1)}, bf16[512,2048]{1,0:T(8,128)(2...) custom-call(bf16[512,2048]{1,0:T(8,128)(2,1)} %collective-permute-do, ...), custom_call_target="tpu_custom_call", output_to_operand_aliasing={{0}: (7, {}), {1}: (8, {}), {2}: (9, {}), {5}: (10, {})} | custom-call | flops 51539607552 | bytes 71303168 | tf_op jit(solution)/shard_map/experts/pallas_call | solution.py:460
  737.2 78.7 %experts.7 = (bf16[4,512,4096]{2,1,0:T(8,128)(2,1)}, bf16[4,512,4096]{2,1,0:T(8,128)(2,1)}, bf16[4,512,4096]{2,1,0:T(8,128)(2,1)}, bf16[512,2048]{1,0:T(8,128)(2...) custom-call(bf16[512,2048]{1,0:T(8,128)(2,1)} %collective-permute-do, ...), custom_call_target="tpu_custom_call", output_to_operand_aliasing={{0}: (7, {}), {1}: (8, {}), {2}: (9, {}), {5}: (10, {})} | custom-call | flops 51539607552 | bytes 71303168 | tf_op jit(solution)/shard_map/experts/pallas_call | solution.py:460
  823.8 42.3 %collective-permute-done.23 = bf16[512,2048]{1,0:T(8,128)(2,1)} collective-permute-done((bf16[512,2048]{1,0:T(8,128)(2,1)}, bf16[512,2048]{1,0:T(8,128)(2,1)}, u32[]{:S(2)}, u32[]{:S(2)}) %collective-permute-start.23) | collective-permute-done | bytes 2097184 | tf_op jit(solution)/shard_map/ppermute | solution.py:64
  907.7 28.5 %collective-permute-done.25 = bf16[512,512]{1,0:T(8,128)(2,1)S(1)} collective-permute-done((bf16[512,512]{1,0:T(8,128)(2,1)S(1)}, bf16[512,512]{1,0:T(8,128)(2,1)S(1)}, u32[]{:S(2)}, u32[]{:S(2)}) %collective-permute-start.25) | collective-permute-done | bytes 524320 | tf_op jit(solution)/shard_map/ppermute | solution.py:64
  937.8 38.6 %attend_back.1 = (bf16[4,2,256,512]{3,2,1,0:T(8,128)(2,1)}, bf16[4,2,256,512]{3,2,1,0:T(8,128)(2,1)}, bf16[4,2,256,512]{3,2,1,0:T(8,128)(2,1)}, f32[8,128]{1,0:T(8,128)}) custom-call(bf16[4,2,256,512]{3,2,1,0:T(8,128)(2,1)} %get-tuple-element.80.q_ref.refs_0_, bf16[4,2,256,512]{3,2,1,0:T(8,128)(2,1)} %get-tuple-element.81.k_ref.refs_1_, ...), custom_call_target="tpu_custom_call" | custom-call | flops 10737418240 | bytes 25165824 | tf_op jit(solution)/shard_map/attend_back/pallas_call | solution.py:276
  976.4 19.4 %fusion.15 = bf16[2048,1536]{1,0:T(8,128)(2,1)} fusion(bf16[512,2048]{1,0:T(8,128)(2,1)} %collective-permute-done.2.x_ref, bf16[512,2048]{1,0:T(8,128)(2,1)} %collective-permute-done.1.x_ref, bf16[512,2048]{1,0:T(8,128)(2,1)} %collective-permute-done.x_ref, bf16[512,2048]{1,0:T(8,128)(2,1)S(1)} %copy-done.11, bf16[2048,512]{1,0:T(8,128)(2,1)} %bitcast.99, ...), kind=kOutput, calls=%fused_computation.19 | convolution fusion | flops 12940476416 | bytes 20971520 | tf_op jit(solution)/shard_map/dot_general | solution.py:33
  997.4 45.0 %convolution_convert_fusion.2 = bf16[2048,4096]{1,0:T(8,128)(2,1)} fusion(bf16[2048,4096]{1,0:T(8,128)(2,1)} %bitcast.179, bf16[512,2048]{1,0:T(8,128)(2,1)} %collective-permute-done.18.n2_ref, bf16[512,2048]{1,0:T(8,128)(2,1)} %collective-permute-done.15.n2_ref, bf16[512,2048]{1,0:T(8,128)(2,1)} %copy-done.42, bf16[512,2048]{1,0:T(8,128)(2,1)S(1)} %copy-done.16), kind=kOutput, calls=%fused_computation.2 | convolution fusion | flops 34401681408 | bytes 41943040 | tf_op jit(solution)/shard_map/dot_general | solution.py:33
  1042.5 46.8 %convolution_convert_fusion.1 = bf16[2048,4096]{1,0:T(8,128)(2,1)} fusion(bf16[2048,4096]{1,0:T(8,128)(2,1)} %bitcast.180, bf16[512,2048]{1,0:T(8,128)(2,1)} %collective-permute-done.18.n2_ref, bf16[512,2048]{1,0:T(8,128)(2,1)} %collective-permute-done.15.n2_ref, bf16[512,2048]{1,0:T(8,128)(2,1)} %copy-done.42, bf16[512,2048]{1,0:T(8,128)(2,1)S(1)} %copy-done.16), kind=kOutput, calls=%fused_computation.1 | convolution fusion | flops 34401681408 | bytes 41943040 | tf_op jit(solution)/shard_map/dot_general | solution.py:33
  1090.9 44.8 %convolution_convert_fusion = bf16[2048,4096]{1,0:T(8,128)(2,1)} fusion(bf16[2048,4096]{1,0:T(8,128)(2,1)} %bitcast.178, bf16[512,2048]{1,0:T(8,128)(2,1)} %collective-permute-done.19.c_ref, bf16[512,2048]{1,0:T(8,128)(2,1)} %collective-permute-done.16.c_ref, bf16[512,2048]{1,0:T(8,128)(2,1)} %collective-permute-done.10.c_ref, bf16[512,2048]{1,0:T(8,128)(2,1)S(1)} %copy-done.7), kind=kOutput, calls=%fused_computation | convolution fusion | flops 34401681408 | bytes 41943040 | tf_op jit(solution)/shard_map/dot_general | solution.py:33
  1154.5 39.7 %collective-permute-done.27 = bf16[512,2048]{1,0:T(8,128)(2,1)} collective-permute-done((bf16[512,2048]{1,0:T(8,128)(2,1)}, bf16[512,2048]{1,0:T(8,128)(2,1)}, u32[]{:S(2)}, u32[]{:S(2)}) %collective-permute-start.27) | collective-permute-done | bytes 2097184 | tf_op jit(solution)/shard_map/ppermute | solution.py:64
  1197.4 41.6 %collective-permute-done.14 = bf16[512,2048]{1,0:T(8,128)(2,1)S(1)} collective-permute-done((bf16[512,2048]{1,0:T(8,128)(2,1)}, bf16[512,2048]{1,0:T(8,128)(2,1)S(1)}, u32[]{:S(2)}, u32[]{:S(2)}) %collective-permute-start.14) | collective-permute-done | bytes 2097184 | tf_op jit(solution)/shard_map/ppermute | solution.py:64
  1249.6 34.5 %collective-permute-done.28 = bf16[512,2048]{1,0:T(8,128)(2,1)} collective-permute-done((bf16[512,2048]{1,0:T(8,128)(2,1)S(1)}, bf16[512,2048]{1,0:T(8,128)(2,1)}, u32[]{:S(2)}, u32[]{:S(2)}) %collective-permute-start.28) | collective-permute-done | bytes 2097184 | tf_op jit(solution)/shard_map/ppermute | solution.py:64
  1288.6 40.3 %collective-permute-done.17 = bf16[512,2048]{1,0:T(8,128)(2,1)S(1)} collective-permute-done((bf16[512,2048]{1,0:T(8,128)(2,1)}, bf16[512,2048]{1,0:T(8,128)(2,1)S(1)}, u32[]{:S(2)}, u32[]{:S(2)}) %collective-permute-start.17) | collective-permute-done | bytes 2097184 | tf_op jit(solution)/shard_map/ppermute | solution.py:64
  1346.2 27.9 %collective-permute-done.29 = bf16[512,2048]{1,0:T(8,128)(2,1)} collective-permute-done((bf16[512,2048]{1,0:T(8,128)(2,1)}, bf16[512,2048]{1,0:T(8,128)(2,1)}, u32[]{:S(2)}, u32[]{:S(2)}) %collective-permute-start.29) | collective-permute-done | bytes 2097184 | tf_op jit(solution)/shard_map/ppermute | solution.py:64
  1377.9 42.0 %collective-permute-done.30 = bf16[256,512]{1,0:T(8,128)(2,1)S(1)} collective-permute-done((bf16[256,512]{1,0:T(8,128)(2,1)S(1)}, bf16[256,512]{1,0:T(8,128)(2,1)S(1)}, u32[]{:S(2)}, u32[]{:S(2)}) %collective-permute-start.30) | collective-permute-done | bytes 262176 | tf_op jit(solution)/shard_map/ppermute | solution.py:64
  1441.9 38.5 %all-reduce.1 = (f32[2048]{0:T(1024)}, f32[128]{0:T(128)}, f32[128]{0:T(128)}, f32[2048]{0:T(1024)}) all-reduce(f32[2048]{0:T(1024)S(1)} %get-tuple-element.174, f32[128]{0:T(128)S(1)} %get-tuple-element.213, f32[128]{0:T(128)S(1)} %get-tuple-element.212, f32[2048]{0:T(1024)S(1)} %copy-done.36), channel_id=1, replica_groups=mesh['fsdp'=8,'tp'=4] {'fsdp','tp'}, use_global_device_ids=true, to_apply=%region_5.6 | all-reduce | flops 4352 | bytes 34816 | tf_op jit(solution)/shard_map/psum | solution.py:651
  (249 shorter events, 315.7 us)
Async XLA Ops:
  7.2 142.1 %all-gather.8.cloned.1.call-start = ((), (), s32[]{:S(2)}) async-start(), calls=%async_computation.5 | async-start | bytes 7667712 | tf_op jit(solution)/shard_map/all_gather | solution.py:540
  10.1 307.1 %all-gather.14.cloned.1.call-start = ((), (), s32[]{:S(2)}) async-start(), calls=%async_computation.14 | async-start | bytes 9437184 | tf_op jit(solution)/shard_map/all_gather | solution.py:548
  40.3 453.7 %all-gather.10.cloned.1.call-start = ((), (), s32[]{:S(2)}) async-start(), calls=%async_computation.6 | async-start | bytes 18874368 | tf_op jit(solution)/shard_map/all_gather | solution.py:549
  41.1 453.0 %all-gather.12.cloned.1.call-start = ((), (), s32[]{:S(2)}) async-start(), calls=%async_computation.7 | async-start | bytes 18874368 | tf_op jit(solution)/shard_map/all_gather | solution.py:550
  41.7 452.4 %all-gather.16.cloned.1.call-start = ((), (), s32[]{:S(2)}) async-start(), calls=%async_computation.15 | async-start | bytes 18874368 | tf_op jit(solution)/shard_map/all_gather | solution.py:551
  42.3 1288.8 %all-reduce.4.cloned.1.call-start = ((), (), s32[]{:S(2)}) async-start(), calls=%async_computation.10 | async-start | bytes 262144 | tf_op jit(solution)/shard_map/psum | solution.py:651
  218.0 97.4 %collective-permute-start.4 = (bf16[512,512]{1,0:T(8,128)(2,1)S(1)}, bf16[512,512]{1,0:T(8,128)(2,1)S(1)}, u32[]{:S(2)}, u32[]{:S(2)}) collective-permute-start(bf16[512,512]{1,0:T(8,128)(2,1)S(1)} %bitcast.119), channel_id=1, source_target_pairs={{0,2},{1,3},{2,0},{3,1},{4,6},{5,7},{6,4},{7,5},{8,10},{9,11},{10,... | collective-permute-start | bytes 1572872 | tf_op jit(solution)/shard_map/ppermute | solution.py:64
  218.0 97.4 %collective-permute-start.5 = (bf16[512,512]{1,0:T(8,128)(2,1)S(1)}, bf16[512,512]{1,0:T(8,128)(2,1)S(1)}, u32[]{:S(2)}, u32[]{:S(2)}) collective-permute-start(bf16[512,512]{1,0:T(8,128)(2,1)S(1)} %bitcast.117), channel_id=1, source_target_pairs={{0,1},{1,2},{2,3},{3,0},{4,5},{5,6},{6,7},{7,4},{8,9},{9,10},{10,1... | collective-permute-start | bytes 1572872 | tf_op jit(solution)/shard_map/ppermute | solution.py:64
  219.7 97.5 %collective-permute-start.3 = (bf16[512,512]{1,0:T(8,128)(2,1)S(1)}, bf16[512,512]{1,0:T(8,128)(2,1)}, u32[]{:S(2)}, u32[]{:S(2)}) collective-permute-start(bf16[512,512]{1,0:T(8,128)(2,1)S(1)} %bitcast.116), channel_id=1, source_target_pairs={{0,3},{1,0},{2,1},{3,2},{4,7},{5,4},{6,5},{7,6},{8,11},{9,8},{10,9... | collective-permute-start | bytes 1572872 | tf_op jit(solution)/shard_map/ppermute | solution.py:64
  222.2 120.3 %collective-permute-start.10 = (bf16[512,2048]{1,0:T(8,128)(2,1)S(1)}, bf16[512,2048]{1,0:T(8,128)(2,1)}, u32[]{:S(2)}, u32[]{:S(2)}) collective-permute-start(bf16[512,2048]{1,0:T(8,128)(2,1)S(1)} %bitcast_select_fusion.c_ref), channel_id=1, source_target_pairs={{0,1},{1,2},{2,3},{3,0},{4,5},{5,6},{6,7},{7,4},{8,9},{9,10},{10,1... | collective-permute-start | bytes 6291464 | tf_op jit(solution)/shard_map/ppermute | solution.py:64
  342.5 151.4 %collective-permute-start.16 = (bf16[512,2048]{1,0:T(8,128)(2,1)}, bf16[512,2048]{1,0:T(8,128)(2,1)}, u32[]{:S(2)}, u32[]{:S(2)}) collective-permute-start(bf16[512,2048]{1,0:T(8,128)(2,1)} %collective-permute-done.10.c_ref), channel_id=1, source_target_pairs={{0,1},{1,2},{2,3},{3,0},{4,5},{5,6},{6,7},{7,4},{8,9},{9,10},{10,1... | collective-permute-start | bytes 6291464 | tf_op jit(solution)/shard_map/ppermute | solution.py:64
  388.5 105.4 %collective-permute-start.15 = (bf16[512,2048]{1,0:T(8,128)(2,1)S(1)}, bf16[512,2048]{1,0:T(8,128)(2,1)}, u32[]{:S(2)}, u32[]{:S(2)}) collective-permute-start(bf16[512,2048]{1,0:T(8,128)(2,1)S(1)} %collective-permute-done.9.n2_ref), channel_id=1, source_target_pairs={{0,1},{1,2},{2,3},{3,0},{4,5},{5,6},{6,7},{7,4},{8,9},{9,10},{10,1... | collective-permute-start | bytes 6291464 | tf_op jit(solution)/shard_map/ppermute | solution.py:64
  391.1 87.1 %collective-permute-start.11 = (s32[16,512]{1,0:T(8,128)S(1)}, s32[16,512]{1,0:T(8,128)S(1)}, u32[]{:S(2)}, u32[]{:S(2)}) collective-permute-start(s32[16,512]{1,0:T(8,128)S(1)} %select_select_fusion), channel_id=1, source_target_pairs={{0,1},{1,2},{2,3},{3,0},{4,5},{5,6},{6,7},{7,4},{8,9},{9,10},{10,1... | collective-permute-start | bytes 98312 | tf_op jit(solution)/shard_map/ppermute | solution.py:64
  493.9 243.3 %collective-permute-start.19 = (bf16[512,2048]{1,0:T(8,128)(2,1)}, bf16[512,2048]{1,0:T(8,128)(2,1)}, u32[]{:S(2)}, u32[]{:S(2)}) collective-permute-start(bf16[512,2048]{1,0:T(8,128)(2,1)} %collective-permute-done.16.c_ref), channel_id=1, source_target_pairs={{0,1},{1,2},{2,3},{3,0},{4,5},{5,6},{6,7},{7,4},{8,9},{9,10},{10,1... | collective-permute-start | bytes 6291464 | tf_op jit(solution)/shard_map/ppermute | solution.py:64
  493.9 243.3 %collective-permute-start.18 = (bf16[512,2048]{1,0:T(8,128)(2,1)}, bf16[512,2048]{1,0:T(8,128)(2,1)}, u32[]{:S(2)}, u32[]{:S(2)}) collective-permute-start(bf16[512,2048]{1,0:T(8,128)(2,1)} %collective-permute-done.15.n2_ref), channel_id=1, source_target_pairs={{0,1},{1,2},{2,3},{3,0},{4,5},{5,6},{6,7},{7,4},{8,9},{9,10},{10,1... | collective-permute-start | bytes 6291464 | tf_op jit(solution)/shard_map/ppermute | solution.py:64
  823.8 517.2 %reduce-scatter.8.cloned.1.call-start = ((), (), s32[]{:S(2)}) async-start(), calls=%async_computation.9 | async-start | bytes 9437184 | tf_op jit(solution)/shard_map/reduce_scatter | solution.py:632
  884.5 598.4 %reduce-scatter.6.cloned.1.call-start = ((), (), s32[]{:S(2)}) async-start(), calls=%async_computation.8 | async-start | bytes 7077888 | tf_op jit(solution)/shard_map/reduce_scatter | solution.py:646
  995.9 494.6 %reduce-scatter.10.cloned.1.call-start = ((), (), s32[]{:S(2)}) async-start(), calls=%async_computation.11 | async-start | bytes 18874368 | tf_op jit(solution)/shard_map/reduce_scatter | solution.py:612
  1042.5 452.6 %reduce-scatter.12.cloned.1.call-start = ((), (), s32[]{:S(2)}) async-start(), calls=%async_computation.12 | async-start | bytes 18874368 | tf_op jit(solution)/shard_map/reduce_scatter | solution.py:612
  1089.3 410.3 %reduce-scatter.14.cloned.1.call-start = ((), (), s32[]{:S(2)}) async-start(), calls=%async_computation.13 | async-start | bytes 18874368 | tf_op jit(solution)/shard_map/reduce_scatter | solution.py:612
  1144.3 94.7 %collective-permute-start.14 = (bf16[512,2048]{1,0:T(8,128)(2,1)}, bf16[512,2048]{1,0:T(8,128)(2,1)S(1)}, u32[]{:S(2)}, u32[]{:S(2)}) collective-permute-start(bf16[512,2048]{1,0:T(8,128)(2,1)} %get-tuple-element.89), channel_id=1, source_target_pairs={{0,1},{1,2},{2,3},{3,0},{4,5},{5,6},{6,7},{7,4},{8,9},{9,10},{10,1... | collective-permute-start | bytes 6291464 | tf_op jit(solution)/shard_map/ppermute | solution.py:64
  1197.3 86.8 %collective-permute-start.28 = (bf16[512,2048]{1,0:T(8,128)(2,1)S(1)}, bf16[512,2048]{1,0:T(8,128)(2,1)}, u32[]{:S(2)}, u32[]{:S(2)}) collective-permute-start(bf16[512,2048]{1,0:T(8,128)(2,1)S(1)} %add_convert_fusion.1), channel_id=1, source_target_pairs={{0,1},{1,2},{2,3},{3,0},{4,5},{5,6},{6,7},{7,4},{8,9},{9,10},{10,1... | collective-permute-start | bytes 6291464 | tf_op jit(solution)/shard_map/ppermute | solution.py:64
  1241.1 87.8 %collective-permute-start.17 = (bf16[512,2048]{1,0:T(8,128)(2,1)}, bf16[512,2048]{1,0:T(8,128)(2,1)S(1)}, u32[]{:S(2)}, u32[]{:S(2)}) collective-permute-start(bf16[512,2048]{1,0:T(8,128)(2,1)} %add_convert_fusion.6), channel_id=1, source_target_pairs={{0,1},{1,2},{2,3},{3,0},{4,5},{5,6},{6,7},{7,4},{8,9},{9,10},{10,1... | collective-permute-start | bytes 6291464 | tf_op jit(solution)/shard_map/ppermute | solution.py:64
  1331.0 94.3 %collective-permute-start.20 = (bf16[512,2048]{1,0:T(8,128)(2,1)}, bf16[512,2048]{1,0:T(8,128)(2,1)}, u32[]{:S(2)}, u32[]{:S(2)}) collective-permute-start(bf16[512,2048]{1,0:T(8,128)(2,1)} %add_convert_fusion.5), channel_id=1, source_target_pairs={{0,1},{1,2},{2,3},{3,0},{4,5},{5,6},{6,7},{7,4},{8,9},{9,10},{10,1... | collective-permute-start | bytes 6291464 | tf_op jit(solution)/shard_map/ppermute | solution.py:64
  (65 other events, 2526.7 us)
Sparse Core Ops, SparseCore 0:
  10.5 50.4 all-gather.7
  62.8 54.3 all-gather.13
  119.2 89.8 all-gather.9
  210.8 89.8 all-gather.11
  302.5 89.8 all-gather.15
  823.9 134.5 all-reduce.3
  962.0 70.2 reduce-scatter.7
  1036.1 61.7 reduce-scatter.5
  1101.5 115.9 reduce-scatter.9
  1220.8 115.9 reduce-scatter.11
  1340.4 116.5 reduce-scatter.13

commit v2 on v1

--- a/solution.py
+++ b/solution.py
@@ -19,6 +19,7 @@
 BF = jnp.bfloat16
 F32 = jnp.float32
 VMEM_BYTES = 58 * 1024 * 1024
+GROUPS = 2
 
 
 def dot_nn(a, b):
@@ -40,7 +41,7 @@
 
 
 def cost(macs, nbytes, exps=0):
-    return pl.CostEstimate(flops=2 * macs, bytes_accessed=nbytes, transcendentals=exps)
+    return pl.CostEstimate(flops=32 * macs, bytes_accessed=nbytes, transcendentals=exps)
 
 
 def struct(shape, dtype):
@@ -64,11 +65,22 @@
     return lax.ppermute(value, "tp", [(i, (i + step) % count) for i in range(count)])
 
 
+def after(value, *done):
+    return lax.optimization_barrier((value,) + done)[0]
+
+
 def ring_gather(value, count, step=1):
     held = [value]
     for _ in range(count - 1):
         held.append(shift(held[-1], count, step))
     return held
+
+
+def plus(arrived, *parts):
+    total = arrived.astype(F32)
+    for part in parts:
+        total = total + part.astype(F32)
+    return total
 
 
 def ring_scatter(parts, step=1):
@@ -77,8 +89,8 @@
     for k in range(2, count + 1):
         arrived = shift(total, count, step)
         if k < count:
-            total = (arrived.astype(F32) + parts[k].astype(F32)).astype(BF)
-    return arrived.astype(F32) + parts[0].astype(F32)
+            total = plus(arrived, parts[k]).astype(BF)
+    return plus(arrived, parts[0])
 
 
 def keep_kernel(bits, order_ref, keep_ref):
@@ -327,7 +339,7 @@
         out_specs=pl.BlockSpec((rows, tile), lambda t: (0, t)),
         out_shape=struct((rows, depth), BF),
         compiler_params=params(1),
-        cost_estimate=cost(rows * depth * local * 3, rows * depth * 2 + depth * local * 6),
+        cost_estimate=cost(rows * depth * local * 3 // 16, rows * depth * 2 + depth * local * 6),
         name="input_back",
     )(dq, dk, dv, weights, weights, weights)
 
@@ -388,12 +400,13 @@
     )(db, weights)
 
 
-def expert_kernel(n2_ref, c_ref, keep_ref, router_ref, g_ref, u_ref, d_ref, *rest):
-    hp_ref, da_ref, du_ref, y_ref, dn_ref, dl_ref = rest[-12:-6]
-    probs, gates, grads, y_acc, dn_acc, d_full = rest[-6:]
+def expert_kernel(group, experts, n2_ref, c_ref, keep_ref, router_ref, tile_ref, w_ref, *rest):
+    last = group == GROUPS - 1
+    wt_ref, grad_in = rest[0], rest[1]
+    hp_ref, da_ref, du_ref, y_ref, dn_ref, grad_out = rest[-14:-8]
+    probs, gates, grads, hp_all, da_all, du_all, full, low = rest[-8:]
     e = pl.program_id(0)
-    experts = pl.num_programs(0)
-    blocks, _, _, tile = d_ref.shape
+    blocks, _, _, ff, tile = w_ref.shape
     rows = n2_ref.shape[0]
     lane = lax.broadcasted_iota(jnp.int32, (rows, LANES), 1)
 
@@ -404,100 +417,190 @@
         soft = raised / jnp.sum(raised, axis=-1, keepdims=True)
         probs[...] = soft
         gates[...] = soft * keep_ref[0]
-        grads[...] = jnp.zeros_like(grads)
-
-    for j in range(blocks):
-        d_full[:, j * tile : (j + 1) * tile] = d_ref[j, 0]
-    here = lane == e
-    gate = jnp.sum(jnp.where(here, gates[...], 0.0), axis=-1, keepdims=True)
-    x = n2_ref[...]
-    pre = dot_nn(x, g_ref[0])
-    up = dot_nn(x, u_ref[0])
-    back = dot_nt(c_ref[...], d_full[...])
-    sig = 1.0 / (1.0 + jnp.exp(-pre))
-    act = pre * sig
-    hid = act * up
-    hp = (hid * gate).astype(BF)
-    column = jnp.sum(back * hid, axis=-1, keepdims=True)
-    grads[...] += jnp.where(here, column * keep_ref[0], 0.0)
-    dh = back * gate
-    du = (dh * act).astype(BF)
-    da = (dh * up * (sig + act * (1.0 - sig))).astype(BF)
-    hp_ref[0] = hp
-    da_ref[0] = da
-    du_ref[0] = du
-    y_part = dot_nn(hp, d_full[...])
-    dn_part = dot_nt(da, g_ref[0]) + dot_nt(du, u_ref[0])
-
-    @pl.when(e == 0)
+        grads[...] = jnp.zeros_like(grads) if group == 0 else grad_in[...]
+
+    @pl.when(e < experts)
     def _():
-        y_acc[...] = y_part
-        dn_acc[...] = dn_part
-
-    @pl.when(e > 0)
-    def _():
-        y_acc[...] += y_part
-        dn_acc[...] += dn_part
+        for t in range(3):
+            for j in range(blocks):
+                full[t, :, j * tile : (j + 1) * tile] = w_ref[j, t, 0]
+        here = lane == e + group * experts
+        gate = jnp.sum(jnp.where(here, gates[...], 0.0), axis=-1, keepdims=True)
+        x = n2_ref[...]
+        pre = dot_nt(x, full[0])
+        up = dot_nt(x, full[1])
+        back = dot_nt(c_ref[...], full[2])
+        sig = 1.0 / (1.0 + jnp.exp(-pre))
+        act = pre * sig
+        hid = act * up
+        hp = (hid * gate).astype(BF)
+        column = jnp.sum(back * hid, axis=-1, keepdims=True)
+        grads[...] += jnp.where(here, column * keep_ref[0], 0.0)
+        dh = back * gate
+        du = (dh * act).astype(BF)
+        da = (dh * up * (sig + act * (1.0 - sig))).astype(BF)
+        hp_ref[0] = hp
+        da_ref[0] = da
+        du_ref[0] = du
+        place = pl.ds(pl.multiple_of(e * ff, ff), ff)
+        hp_all[:, place] = hp
+        da_all[:, place] = da
+        du_all[:, place] = du
 
     @pl.when(e == experts - 1)
     def _():
-        soft = probs[...]
-        gd = grads[...]
-        dl = (soft * (gd - jnp.sum(soft * gd, axis=-1, keepdims=True))).astype(BF)
-        dl_ref[0] = dl
-        y_ref[...] = y_acc[...].astype(BF)
-        dn_ref[...] = (dn_acc[...] + dot_nt(dl, router_ref[...])).astype(BF)
-
-
-def experts_pass(k, count, n2, cot, keep, weights_all, gate_w, up_w, down_w, kept):
+        if last:
+            soft = probs[...]
+            gd = grads[...]
+            dl = (soft * (gd - jnp.sum(soft * gd, axis=-1, keepdims=True))).astype(BF)
+            grad_out[...] = dl
+            low[...] = dl
+        else:
+            grad_out[...] = grads[...]
+
+    @pl.when(e >= experts)
+    def _():
+        wide = experts * ff
+        y_ref[...] = dot_nn(hp_all[...], wt_ref[0, 2].reshape(wide, tile)).astype(BF)
+        total = dot_nn(da_all[...], wt_ref[0, 0].reshape(wide, tile))
+        total = total + dot_nn(du_all[...], wt_ref[0, 1].reshape(wide, tile))
+        if last:
+            total = total + dot_nt(low[...], tile_ref[...])
+        dn_ref[...] = total.astype(BF)
+
+
+def experts_pass(k, count, group, n2, cot, keep, weights_all, weights, grad, kept):
     rows, depth = n2.shape
-    experts, _, ff = gate_w.shape
-    blocks, _, _, tile = down_w.shape
+    blocks, _, experts, ff, tile = weights.shape
     router_col = weights_all.shape[1] // LANES - 1
     const = lambda *shape: pl.BlockSpec(shape, lambda e: (0,) * len(shape))
-    wide = pl.BlockSpec((1, rows, ff), lambda e: (k, 0, e))
+    near = lambda e: jnp.minimum(e, experts - 1)
+    far = lambda e: jnp.maximum(e - experts, 0)
+    wide = pl.BlockSpec((1, rows, ff), lambda e: (k, 0, near(e)))
+    part = pl.BlockSpec((rows, tile), lambda e: (0, far(e)))
     aliased = list(kept or ())
+    grad = jnp.zeros((8, LANES), F32) if grad is None else grad
     return pl.pallas_call(
-        expert_kernel,
-        grid=(experts,),
+        functools.partial(expert_kernel, group, experts),
+        grid=(experts + blocks,),
         in_specs=[
             const(rows, depth),
             const(rows, depth),
             pl.BlockSpec((1, rows, LANES), lambda e: (k, 0, 0)),
             pl.BlockSpec((depth, LANES), lambda e: (0, router_col)),
-            pl.BlockSpec((1, depth, ff), lambda e: (e, 0, 0)),
-            pl.BlockSpec((1, depth, ff), lambda e: (e, 0, 0)),
-            pl.BlockSpec((blocks, 1, ff, tile), lambda e: (0, e, 0, 0)),
+            pl.BlockSpec((tile, LANES), lambda e: (far(e), router_col)),
+            pl.BlockSpec((blocks, 3, 1, ff, tile), lambda e: (0, 0, near(e), 0, 0)),
+            pl.BlockSpec((1, 3, experts, ff, tile), lambda e: (far(e), 0, 0, 0, 0)),
+            const(*grad.shape),
         ]
         + [pl.BlockSpec(memory_space=pl.ANY)] * len(aliased),
-        out_specs=[
-            wide,
-            wide,
-            wide,
-            const(rows, depth),
-            const(rows, depth),
-            pl.BlockSpec((1, rows, LANES), lambda e: (k, 0, 0)),
-        ],
+        out_specs=[wide, wide, wide, part, part, const(rows, LANES)],
         out_shape=[struct((count, rows, experts * ff), BF)] * 3
         + [struct((rows, depth), BF)] * 2
-        + [struct((count, rows, LANES), BF)],
-        input_output_aliases=dict(zip(range(7, 11), (0, 1, 2, 5))) if aliased else {},
-        scratch_shapes=[
-            pltpu.VMEM((rows, LANES), F32),
-            pltpu.VMEM((rows, LANES), F32),
-            pltpu.VMEM((rows, LANES), F32),
-            pltpu.VMEM((rows, depth), F32),
-            pltpu.VMEM((rows, depth), F32),
-            pltpu.VMEM((ff, depth), BF),
-        ],
+        + [struct((rows, LANES), BF if group == GROUPS - 1 else F32)],
+        input_output_aliases={8 + i: i for i in range(len(aliased))},
+        scratch_shapes=[pltpu.VMEM((rows, LANES), F32)] * 3
+        + [pltpu.VMEM((rows, experts * ff), BF)] * 3
+        + [pltpu.VMEM((3, ff, depth), BF), pltpu.VMEM((rows, LANES), BF)],
         compiler_params=params(1),
         cost_estimate=cost(
             6 * rows * depth * ff * experts,
-            3 * experts * depth * ff * 2 + 4 * rows * depth * 2 + 3 * rows * experts * ff * 2,
+            6 * experts * depth * ff * 2 + 4 * rows * depth * 2 + 3 * rows * experts * ff * 2,
             2 * rows * ff * experts,
         ),
-        name="experts",
-    )(n2, cot, keep, weights_all, gate_w, up_w, down_w, *aliased)
+        name=f"experts_{group}",
+    )(n2, cot, keep, weights_all, weights_all, weights, weights, grad, *aliased)
+
+
+def row_grad_kernel(count, plan, router, gain, *refs):
+    ins = list(refs)
+    lefts, rights = [], []
+    for parts, tiles in plan:
+        lefts.append([ins.pop(0) for _ in range(parts)])
+        rights.append([ins.pop(0) for _ in tiles])
+    dls = [ins.pop(0) for _ in range(count)] if router else []
+    weight_ref = ins.pop(0) if gain else None
+    out_ref, extra_ref, turned = ins.pop(0), ins.pop(0) if router or gain else None, ins.pop(0)
+    i = pl.program_id(0)
+    start = 0
+    for (parts, tiles), left, right in zip(plan, lefts, rights):
+        rows = left[0].shape[0]
+
+        @pl.when(i == start)
+        def _():
+            for k in range(parts):
+                turned[:, k * rows : (k + 1) * rows] = left[k][...].T
+            if router and start == 0:
+                total = None
+                for k in range(count):
+                    part = dot_nn(turned[:, k * rows : (k + 1) * rows], dls[k][...])
+                    total = part if total is None else total + part
+                extra_ref[...] = total
+            if gain:
+                extra_ref[...] = jnp.zeros_like(extra_ref)
+
+        for ref, steps in zip(right, tiles):
+
+            @pl.when(jnp.logical_and(i >= start, i < start + steps))
+            def _():
+                tile = out_ref.shape[1]
+                full = dot_nn(turned[:, : parts * rows], ref[...].reshape(parts * rows, tile))
+                out_ref[...] = full.astype(BF)
+                if gain:
+                    product = full * weight_ref[...].astype(F32)
+                    for j in range(tile // LANES):
+                        extra_ref[...] += product[:, j * LANES : (j + 1) * LANES]
+
+            start += steps
+
+
+def row_grads(pairs, tile, name, dls=(), weights=None):
+    plan, args, specs, start, macs = [], [], [], 0, 0
+    depth = pairs[0][0][0].shape[1]
+    most = max(sum(part.shape[0] for part in left) for left, _ in pairs)
+
+    def piece(array, first, steps):
+        lead = array.shape[:-1]
+        return pl.BlockSpec(
+            lead + (tile,),
+            lambda i: (0,) * len(lead) + (jnp.clip(i - first, 0, steps - 1),),
+        )
+
+    whole = pl.Buffered(1)
+    for left, right in pairs:
+        args += left
+        specs += [pl.BlockSpec(p.shape, lambda i: (0, 0), pipeline_mode=whole) for p in left]
+        tiles = []
+        for array in right:
+            steps = array.shape[-1] // tile
+            args.append(array)
+            specs.append(piece(array, start, steps))
+            tiles.append(steps)
+            start += steps
+            macs += len(left) * left[0].shape[0] * depth * steps * tile
+        plan.append((len(left), tuple(tiles)))
+    out_specs = [pl.BlockSpec((depth, tile), lambda i: (0, i))]
+    out_shape = [struct((depth, start * tile), BF)]
+    if dls:
+        args += dls
+        specs += [pl.BlockSpec(d.shape, lambda i: (0, 0)) for d in dls]
+    if weights is not None:
+        args.append(weights)
+        specs.append(pl.BlockSpec((depth, tile), lambda i: (0, i)))
+    if dls or weights is not None:
+        out_specs.append(pl.BlockSpec((depth, LANES), lambda i: (0, 0)))
+        out_shape.append(struct((depth, LANES), F32))
+    return pl.pallas_call(
+        functools.partial(row_grad_kernel, len(dls), tuple(plan), bool(dls), weights is not None),
+        grid=(start,),
+        in_specs=specs,
+        out_specs=out_specs,
+        out_shape=out_shape,
+        scratch_shapes=[pltpu.VMEM((depth, most), BF)],
+        compiler_params=params(1),
+        cost_estimate=cost(macs if 'experts' in name else macs // 16, 2 * depth * start * tile + 4 * most * depth),
+        name=name,
+    )(*args)
 
 
 def per_device(
@@ -542,13 +645,14 @@
     tok = jnp.transpose(tokens, (1, 0, 2)).reshape(rows, depth)
     tok_float = tok.astype(F32)
     n1_own = (tok_float * rms_scale(tok_float) * attn_gain).astype(BF)
-    n1 = ring_gather(n1_own, count)
-
-    out_rows = jnp.concatenate(ring_gather(out_weight, count, -1), axis=0)
-    out_all = lax.all_gather(out_rows, "fsdp", axis=0, tiled=False)
-    gate_all = lax.all_gather(gate_weight, "fsdp", axis=1, tiled=True)
-    up_all = lax.all_gather(up_weight, "fsdp", axis=1, tiled=True)
-    down_all = lax.all_gather(down_weight, "fsdp", axis=0, tiled=False)
+    n1 = [n1_own, shift(n1_own, count, 1)]
+    turned = jnp.stack(
+        [jnp.swapaxes(gate_weight, 1, 2), jnp.swapaxes(up_weight, 1, 2), down_weight]
+    )
+    turned = after(turned, weights_all, n1[1])
+    each = EXPERTS // GROUPS
+    gather = lambda value: lax.all_gather(value, "fsdp", axis=0, tiled=False)
+    moe_weights = [gather(turned[:, g * each : (g + 1) * each]) for g in range(GROUPS)]
 
     own_pos = me * per + jnp.arange(per, dtype=jnp.int32)
     valid_own = own_pos[None, :] < lengths[:, None]
@@ -559,9 +663,6 @@
     for j in range(TOP):
         order_own = jnp.where(route_t[j][None, :] == names, order_t[j][None, :], order_own)
     order_own = jnp.where(valid_own.reshape(1, rows), order_own, FAR)
-    order_all = jnp.stack(ring_gather(order_own, count))
-    keep = keep_rows(order_all, length * seqs * TOP)
-
     owner = (me - jnp.arange(count, dtype=jnp.int32)) % count
     chunk_pos = owner[:, None] * per + jnp.arange(per, dtype=jnp.int32)[None, :]
     half = head_width // 2
@@ -574,82 +675,170 @@
     key_valid = jnp.broadcast_to(key_valid[:, :, None], (seqs, length, LANES))
 
     gain_q, gain_k = query_gain[None, :], key_gain[None, :]
-    kept = None
+    kept, done = None, []
     for k in range(count):
-        kept = project(k, count, seqs, n1[k], weights_all, cos, sin, gain_q, gain_k, kept)
+        if k > 1:
+            n1.append(shift(after(n1[-1], *done[: k - 2]), count, 1))
+        kept = project(
+            k, count, seqs, after(n1[k], *done[-1:]), weights_all, cos, sin, gain_q, gain_k, kept
+        )
+        done.append(kept[4])
+    outs = ring_gather(after(out_weight, n1[-1]), count, -1)
+    orders = ring_gather(after(order_own, n1[-1]), count)
     q_raw, k_raw, q, k_low, v = kept
+    out_all = gather(after(jnp.concatenate(outs, axis=0), moe_weights[0], v))
 
     cot = jnp.transpose(cotangent, (1, 0, 2)).reshape(rows, depth)
     cot_own = jnp.where(valid_own.reshape(rows, 1), cot, jnp.zeros_like(cot))
-    cot_own, _ = lax.optimization_barrier((cot_own, n1[-1]))
-    cots = ring_gather(cot_own, count)
+    cots = [cot_own, shift(after(cot_own, n1[-1], outs[-1], orders[-1]), count, 1)]
+    keep = keep_rows(after(jnp.stack(orders), v), length * seqs * TOP)
 
     ob, lse = attend(q, k_low, v, key_valid, scale)
-    ob_rows = ob.reshape(count, rows, local)
+    ob_rows = after(ob.reshape(count, rows, local), cots[1], keep)
     ob_parts = [ob_rows[0]] + [shift(ob_rows[s], count, -s) for s in range(1, count)]
     x1 = out_project(tok, ob_parts, out_all)
     n2_own = (x1 * rms_scale(x1) * moe_gain).astype(BF)
-    n2 = ring_gather(n2_own, count)
-
-    kept = None
-    y_parts, dn_parts = [], []
-    for k in range(count):
-        hp, da, du, y_k, dn_k, dl = experts_pass(
-            k, count, n2[k], cots[k], keep, weights_all, gate_all, up_all, down_all, kept
+    n2 = [n2_own, shift(n2_own, count, 1)]
+    cots.append(shift(after(cots[1], *ob_parts[1:]), count, 1))
+    token = [n2_own]
+
+    bufs = [None] * GROUPS
+    ys = [[] for _ in range(count)]
+    dns = [[] for _ in range(count)]
+    grads = [None] * count
+
+    def run(group, k):
+        hp, da, du, y_k, dn_k, grads[k] = experts_pass(
+            k, count, group, after(n2[k], *token), cots[k], keep, weights_all, moe_weights[group],
+            grads[k], bufs[group],
         )
-        kept = (hp, da, du, dl)
-        y_parts.append(y_k)
-        dn_parts.append(dn_k)
-    dn2 = ring_scatter(dn_parts)
-
-    n2_all = jnp.concatenate(n2, axis=0)
-    cot_all = jnp.concatenate(cots, axis=0)
-    all_rows = count * rows
+        bufs[group] = (hp, da, du)
+        ys[k].append(y_k)
+        dns[k].append(dn_k)
+        token[0] = dn_k
+        return dn_k
+
+    def next_inputs(done):
+        if len(n2) < count:
+            n2.append(shift(after(n2[-1], done), count, 1))
+        if len(cots) < count:
+            cots.append(shift(after(cots[-1], done), count, 1))
+
+    def both(parts):
+        return plus(parts[0], *parts[1:]).astype(BF)
+
+    ready = run(0, 0)
+    next_inputs(ready)
+    run(0, 1)
+    ready = run(1, 0)
+    next_inputs(ready)
+    for k in range(2, count):
+        run(0, k)
+        if k < count - 1:
+            next_inputs(run(1, k - 1))
+    dn_run = shift(both(dns[1]), count, 1)
+    token.append(dn_run)
+    y_run = shift(after(both(ys[1]), dns[count - 1][0]), count, 1)
     ff = gate_weight.shape[2]
-
-    def expert_grad(left, right):
-        full = dot_tn(left, right.reshape(all_rows, EXPERTS * ff)).astype(BF)
-        own = lax.psum_scatter(full, "fsdp", scatter_dimension=0, tiled=True)
-        return own.reshape(own.shape[0], EXPERTS, ff)
-
-    gate_grad = jnp.transpose(expert_grad(n2_all, da), (1, 0, 2)).astype(F32)
-    up_grad = jnp.transpose(expert_grad(n2_all, du), (1, 0, 2)).astype(F32)
-    down_grad = jnp.transpose(expert_grad(cot_all, hp), (1, 2, 0)).astype(F32)
-    router_term = dot_tn(n2_all, dl.reshape(all_rows, LANES))[:, :EXPERTS]
+    hp, da, du = bufs[0]
+    first_full = row_grads(
+        [([after(n2[0], *token)] + n2[1:], [da, du]), (cots, [hp])], ff, "experts_first_grads"
+    )[0]
+    first_own = lax.psum_scatter(first_full, "fsdp", scatter_dimension=0, tiled=True)
+    token = [first_full, y_run]
+    run(1, count - 2)
+    for k in range(2, count):
+        dn_run = plus(dn_run, *dns[k]).astype(BF)
+        token.append(dn_run)
+        if k == count - 2:
+            run(1, count - 1)
+        dn_run = shift(dn_run, count, 1)
+    hp, da, du = bufs[1]
+    last_full, router_term = row_grads(
+        [([after(n2[0], *token)] + n2[1:], [da, du])], ff, "experts_last_grads", grads
+    )
+    dn2 = plus(after(dn_run, last_full), *dns[0])
 
     moe_back, moe_gain_term = norm_back(dn2, x1, moe_gain)
     dx1 = moe_back + cot_own.astype(F32)
     db = dx1.astype(BF)
     dob = out_back(db, out_all, count)
+    last_own = lax.psum_scatter(after(last_full, dob), "fsdp", scatter_dimension=0, tiled=True)
+    dob = after(dob, first_own)
     dob_parts = [dob[0]] + [shift(dob[s], count, s) for s in range(1, count)]
+    rest_full = row_grads(
+        [(cots, [hp]), ([after(db, dob)], ob_parts)], ff, "rest_grads"
+    )[0]
     d_ob = jnp.stack(dob_parts).reshape(count, seqs, per, local)
-
-    y_sum = ring_scatter(y_parts)
-    layer_out = (x1 + y_sum).astype(BF)
-
-    ob_cat = jnp.concatenate(ob_parts, axis=1)
-    out_full = dot_tn(db, ob_cat).astype(BF)
-    out_sum = lax.psum_scatter(out_full, "fsdp", scatter_dimension=0, tiled=True)
-    out_pieces = [out_sum[:, s * local : (s + 1) * local] for s in range(count)]
-    out_weight_grad = jnp.transpose(ring_scatter(out_pieces, -1))
+    d_ob = after(d_ob, rest_full)
+    y_run = shift(after(plus(y_run, *ys[2]).astype(BF), d_ob), count, 1)
 
     dq, dk, dv, gains = attend_back(
         q, k_low, v, ob, d_ob, lse, key_valid, q_raw, k_raw, cos, sin, gain_q, gain_k, scale
     )
-    dn1_parts = [None] * count
-    for k in list(range(1, count)) + [0]:
-        dn1_parts[k] = input_back(k, dq, dk, dv, weights_all)
-    dn1 = ring_scatter(dn1_parts)
-    n1_all = jnp.concatenate(n1, axis=0)
-    d_all = jnp.concatenate([d.reshape(all_rows, local) for d in (dq, dk, dv)], axis=1)
-    qkv_full = dot_tn(n1_all, d_all).astype(BF)
-    qkv_sum = lax.psum_scatter(qkv_full, "fsdp", scatter_dimension=0, tiled=True).astype(F32)
-
-    attn_back, attn_gain_term = norm_back(dn1, tok_float, attn_gain)
+    part = input_back(1, after(dq, y_run), dk, dv, weights_all)
+    rest_own = lax.psum_scatter(after(rest_full, part), "fsdp", scatter_dimension=0, tiled=True)
+    dn1_run = shift(part, count, 1)
+    qkv_full, attn_gain_wide = row_grads(
+        [([after(n1[0], part)] + n1[1:], [a.reshape(count * rows, local) for a in (dq, dk, dv)])],
+        min(256, local), "qkv_grads", weights=weights_all,
+    )
+    qkv_own = lax.psum_scatter(qkv_full, "fsdp", scatter_dimension=0, tiled=True)
+
+    attn_gain_term = jnp.sum(attn_gain_wide, axis=1) / attn_gain
+    packed = jnp.concatenate(
+        [router_term[:, :EXPERTS].reshape(-1, LANES)]
+        + [v.reshape(-1, LANES) for v in (attn_gain_term, moe_gain_term, gains[:2])],
+        axis=0,
+    )
+    bits = [1 << b for b in range(count.bit_length() - 1)]
+    across = lambda value, axis, bit: value + lax.ppermute(
+        value, axis, [(i, i ^ bit) for i in range(lax.axis_size(axis))]
+    )
+
+    part = input_back(2, after(dq, qkv_full), dk, dv, weights_all)
+    dn1_run = after(dn1_run, last_own)
+    for k in range(2, count):
+        dn1_run = plus(dn1_run, part).astype(BF)
+        if k - 2 < len(bits):
+            packed = across(after(packed, dn1_run), "tp", bits[k - 2])
+        dn1_run = shift(dn1_run, count, 1)
+        part = input_back((k + 1) % count, dq, dk, dv, weights_all)
+    dn1 = plus(dn1_run, part)
+    for k in range(3, count):
+        y_run = shift(after(plus(y_run, *ys[k]).astype(BF), dn1_run), count, 1)
+    for bit in bits[max(count - 2, 0) :]:
+        packed = across(packed, "tp", bit)
+    for b in range(lax.axis_size("fsdp").bit_length() - 1):
+        packed = across(packed, "fsdp", 1 << b)
+
+    layer_out = (x1 + plus(y_run, *ys[0])).astype(BF)
+
+    qkv_sum = qkv_own.astype(F32)
+    out_own = after(rest_own, dn1_run)[:, each * ff :]
+    out_pieces = [out_own[:, s * local : (s + 1) * local] for s in range(count)]
+    out_weight_grad = jnp.transpose(ring_scatter(out_pieces, -1))
+
+    def expert_out(owns, axes):
+        shaped = [own.reshape(own.shape[0], each, ff) for own in owns]
+        return jnp.concatenate([jnp.transpose(v, axes) for v in shaped], axis=0).astype(F32)
+
+    wide = each * ff
+    gate_grad = expert_out((first_own[:, :wide], last_own[:, :wide]), (1, 0, 2))
+    up_grad = expert_out((first_own[:, wide : 2 * wide], last_own[:, wide:]), (1, 0, 2))
+    down_grad = expert_out((first_own[:, 2 * wide :], rest_own[:, :wide]), (1, 2, 0))
+
+    attn_back = norm_back(dn1, tok_float, attn_gain)[0]
     tokens_grad = attn_back + dx1
 
-    small = lax.psum(
-        (attn_gain_term, gains[0], gains[1], moe_gain_term, router_term), ("fsdp", "tp")
+    split = depth * EXPERTS // LANES
+    across = depth // LANES
+    small = (
+        packed[split : split + across].reshape(depth),
+        packed[split + 2 * across],
+        packed[split + 2 * across + 1],
+        packed[split + across : split + 2 * across].reshape(depth),
+        packed[:split].reshape(depth, EXPERTS),
     )
     router_rows = depth // lax.axis_size("fsdp")
     router_grad = lax.dynamic_slice_in_dim(

time: 1520 us -> 1290 us (0.85)
  waiting for transfers between devices: 665 us -> 370 us
  Pallas kernels: 465 us -> 653 us
  matrix products: 168 us -> 0 us
  starting transfers between devices: 56.1 us -> 102 us
  blocking collectives: 38.5 us -> 0 us
  other arithmetic: 59.7 us -> 92.3 us
    ppermute x33, waiting for transfers between devices: 663 us -> 326 us  [shift(): lax.ppermute(value, 'tp', [(i, (i + step) % count) for i in range(count)])]
    pallas_call x4 -> x12, Pallas kernels: 314 us -> 502 us  [the longest x8 322 us: experts_pass(): pl.pallas_call(functools.partial(expert_kernel, group, experts), grid=(ex...]
    dot_general x6 -> x0, matrix products: 168 us -> none  [dot_tn(): lax.dot_general(a, b, (((0,), (0,)), ((), ())), preferred_element_type=F32)]
    ppermute x0 -> x5, waiting for transfers between devices: none -> 43.9 us  [per_device(): lax.ppermute(value, axis, [(i, i ^ bit) for i in range(lax.axis_size(axis...]
    psum x1 -> x0, blocking collectives: 38.5 us -> none  [per_device(): lax.psum((attn_gain_term, gains[0], gains[1], moe_gain_term, router_term)...]
    ppermute x33, starting transfers between devices: 55.7 us -> 90.3 us  [shift(): lax.ppermute(value, 'tp', [(i, (i + step) % count) for i in range(count)])]
    convert_element_type x10 -> x14, other arithmetic: 23.5 us -> 47.1 us  [the longest x2 9.9 us: per_device(): dn_run = plus(dn_run, *dns[k]).astype(BF)]
  transfers between devices with their start and end apart: 44 -> 46, of which waited for: 22 -> 21; matrix products, arithmetic and copies ran while one was open for 17% -> 10% of each run, Pallas kernels for 31% -> 51%
where the time goes in v2:
time: 1290 us; the launch traced here: 1280 us
  Pallas kernels  653 us (51%)
  waiting for transfers between devices  370 us (29%)
  starting transfers between devices  102 us (8%)
  other arithmetic  92.3 us (7%)
  local copies, waits for them, and re-layouts  48 us (4%)
  between operations  15.2 us (1%)
    ppermute x33, waiting for transfers between devices, shift(): lax.ppermute(value, 'tp', [(i, (i + step) % count) for i in range(count)])  326 us
    pallas_call x8, Pallas kernels, experts_pass(): pl.pallas_call(functools.partial(expert_kernel, group, experts), grid=(ex...  322 us
    pallas_call x4, Pallas kernels, row_grads(): pl.pallas_call(functools.partial(row_grad_kernel, len(dls), tuple(plan),...  181 us
    ppermute x33, starting transfers between devices, shift(): lax.ppermute(value, 'tp', [(i, (i + step) % count) for i in range(count)])  90.3 us
    ppermute x5, waiting for transfers between devices, per_device(): lax.ppermute(value, axis, [(i, i ^ bit) for i in range(lax.axis_size(axis...  43.9 us
    pallas_call x1, Pallas kernels, attend_back(): pl.pallas_call(functools.partial(attend_back_kernel, scale), grid=(seqs,...  38.7 us
    pallas_call x4, Pallas kernels, project(): pl.pallas_call(functools.partial(qkv_kernel, seqs), grid=(groups,), in_sp...  37.4 us
    pallas_call x4, Pallas kernels, input_back(): pl.pallas_call(input_back_kernel, grid=(depth // tile,), in_specs=[grad]...  31.8 us
  transfers between devices with their start and end apart: 46, of which 21 were waited for; matrix products, arithmetic and copies ran while one was open for 10% of the time, Pallas kernels for 51%

profile of v2, /device:TPU:0, one launch (start us, length us, event | category | flops | bytes accessed | tf_op | source)
XLA Modules:
  0.0 1280.7 jit_solution(4598503089079236475)
XLA Ops:
  31.2 35.4 %collective-permute-done.x_ref.refs_1_ = bf16[512,2048]{1,0:T(8,128)(2,1)} collective-permute-done((bf16[512,2048]{1,0:T(8,128)(2,1)}, bf16[512,2048]{1,0:T(8,128)(2,1)}, u32[]{:S(2)}, u32[]{:S(2)}) %collective-permute-start) | collective-permute-done | bytes 2097184 | tf_op jit(solution)/shard_map/ppermute | solution.py:65
  86.5 39.2 %collective-permute-done.1.x_ref.refs_2_ = bf16[512,2048]{1,0:T(8,128)(2,1)S(1)} collective-permute-done((bf16[512,2048]{1,0:T(8,128)(2,1)}, bf16[512,2048]{1,0:T(8,128)(2,1)S(1)}, u32[]{:S(2)}, u32[]{:S(2)}) %collective-permute-start.1) | collective-permute-done | bytes 2097184 | tf_op jit(solution)/shard_map/ppermute | solution.py:65
  125.7 49.6 %collective-permute-done.2.x_ref.refs_3_ = bf16[512,2048]{1,0:T(8,128)(2,1)S(1)} collective-permute-done((bf16[512,2048]{1,0:T(8,128)(2,1)S(1)}, bf16[512,2048]{1,0:T(8,128)(2,1)S(1)}, u32[]{:S(2)}, u32[]{:S(2)}) %collective-permute-start.2) | collective-permute-done | bytes 2097184 | tf_op jit(solution)/shard_map/ppermute | solution.py:65
  224.2 18.3 %attend.1 = (bf16[4,2,256,512]{3,2,1,0:T(8,128)(2,1)}, f32[8,4,256]{2,1,0:T(4,128)}) custom-call(bf16[4,2,256,512]{3,2,1,0:T(8,128)(2,1)} %get-tuple-element.150.q_ref.refs_0_, bf16[4,2,256,512]{3,2,1,0:T(8,128)(2,1)} %get-tuple-element.151.k_ref.refs_1_, bf16[4,2,256,512]{3,2,1,0:T(8,128)(2,1)} %get-tuple-element.152.v_ref.refs_2_, ...), custom_call_target="tpu_custom_call" | custom-call | flops 68719476736 | bytes 8388608 | tf_op jit(solution)/shard_map/attend/pallas_call | solution.py:204
  246.9 18.8 %collective-permute-done.9.c_ref.refs_7_.refs_1_ = bf16[512,2048]{1,0:T(8,128)(2,1)S(1)} collective-permute-done((bf16[512,2048]{1,0:T(8,128)(2,1)S(1)}, bf16[512,2048]{1,0:T(8,128)(2,1)S(1)}, u32[]{:S(2)}, u32[]{:S(2)}) %collective-permute-start.9) | collective-permute-done | bytes 2097184 | tf_op jit(solution)/shard_map/ppermute | solution.py:65
  298.1 57.0 %collective-permute-start.15 = (bf16[512,2048]{1,0:T(8,128)(2,1)}, bf16[512,2048]{1,0:T(8,128)(2,1)}, u32[]{:S(2)}, u32[]{:S(2)}) collective-permute-start(bf16[512,2048]{1,0:T(8,128)(2,1)} %copy-done.47), channel_id=1, source_target_pairs={{0,1},{1,2},{2,3},{3,0},{4,5},{5,6},{6,7},{7,4},{8,9},{9,10},{10,1... | collective-permute-start | bytes 6291464 | tf_op jit(solution)/shard_map/ppermute | solution.py:65
  372.6 39.3 %experts_0.4 = (bf16[4,512,2048]{2,1,0:T(8,128)(2,1)}, bf16[4,512,2048]{2,1,0:T(8,128)(2,1)}, bf16[4,512,2048]{2,1,0:T(8,128)(2,1)}, bf16[512,2048]{1,0:T(8,128)...) custom-call(bf16[512,2048]{1,0:T(8,128)(2,1)} %multiply_convert_fusion.n2_ref.refs_0_, ...), custom_call_target="tpu_custom_call" | custom-call | flops 412316860416 | bytes 65011712 | tf_op jit(solution)/shard_map/experts_0/pallas_call | solution.py:483
  412.0 34.3 %collective-permute-done.13.n2_ref.refs_1_ = bf16[512,2048]{1,0:T(8,128)(2,1)} collective-permute-done((bf16[512,2048]{1,0:T(8,128)(2,1)}, bf16[512,2048]{1,0:T(8,128)(2,1)}, u32[]{:S(2)}, u32[]{:S(2)}) %collective-permute-start.13) | collective-permute-done | bytes 2097184 | tf_op jit(solution)/shard_map/ppermute | solution.py:65
  448.9 39.1 %experts_0.5 = (bf16[4,512,2048]{2,1,0:T(8,128)(2,1)}, bf16[4,512,2048]{2,1,0:T(8,128)(2,1)}, bf16[4,512,2048]{2,1,0:T(8,128)(2,1)}, bf16[512,2048]{1,0:T(8,128)...) custom-call(bf16[512,2048]{1,0:T(8,128)(2,1)} %collective-permute-do, ...), custom_call_target="tpu_custom_call", output_to_operand_aliasing={{0}: (8, {}), {1}: (9, {}), {2}: (10, {})} | custom-call | flops 412316860416 | bytes 65011712 | tf_op jit(solution)/shard_map/experts_0/pallas_call | solution.py:483
  488.0 39.5 %experts_1.4 = (bf16[4,512,2048]{2,1,0:T(8,128)(2,1)}, bf16[4,512,2048]{2,1,0:T(8,128)(2,1)}, bf16[4,512,2048]{2,1,0:T(8,128)(2,1)}, bf16[512,2048]{1,0:T(8,128)...) custom-call(bf16[512,2048]{1,0:T(8,128)(2,1)} %multiply_convert_fusion.n2_ref.refs_0_, ...), custom_call_target="tpu_custom_call" | custom-call | flops 412316860416 | bytes 65011712 | tf_op jit(solution)/shard_map/experts_1/pallas_call | solution.py:483
  538.1 39.1 %experts_0.6 = (bf16[4,512,2048]{2,1,0:T(8,128)(2,1)}, bf16[4,512,2048]{2,1,0:T(8,128)(2,1)}, bf16[4,512,2048]{2,1,0:T(8,128)(2,1)}, bf16[512,2048]{1,0:T(8,128)...) custom-call(bf16[512,2048]{1,0:T(8,128)(2,1)} %collective-permute-do, ...), custom_call_target="tpu_custom_call", output_to_operand_aliasing={{0}: (8, {}), {1}: (9, {}), {2}: (10, {})} | custom-call | flops 412316860416 | bytes 65011712 | tf_op jit(solution)/shard_map/experts_0/pallas_call | solution.py:483
  577.2 39.7 %experts_1.5 = (bf16[4,512,2048]{2,1,0:T(8,128)(2,1)}, bf16[4,512,2048]{2,1,0:T(8,128)(2,1)}, bf16[4,512,2048]{2,1,0:T(8,128)(2,1)}, bf16[512,2048]{1,0:T(8,128)...) custom-call(bf16[512,2048]{1,0:T(8,128)(2,1)} %collective-permute-do, ...), custom_call_target="tpu_custom_call", output_to_operand_aliasing={{0}: (8, {}), {1}: (9, {}), {2}: (10, {})} | custom-call | flops 412316860416 | bytes 65011712 | tf_op jit(solution)/shard_map/experts_1/pallas_call | solution.py:483
  623.4 39.2 %experts_0.7 = (bf16[4,512,2048]{2,1,0:T(8,128)(2,1)}, bf16[4,512,2048]{2,1,0:T(8,128)(2,1)}, bf16[4,512,2048]{2,1,0:T(8,128)(2,1)}, bf16[512,2048]{1,0:T(8,128)...) custom-call(bf16[512,2048]{1,0:T(8,128)(2,1)} %collective-permute-do, ...), custom_call_target="tpu_custom_call", output_to_operand_aliasing={{0}: (8, {}), {1}: (9, {}), {2}: (10, {})} | custom-call | flops 412316860416 | bytes 65011712 | tf_op jit(solution)/shard_map/experts_0/pallas_call | solution.py:483
  671.7 71.5 %experts_first_grads.1 = bf16[2048,6144]{1,0:T(8,128)(2,1)} custom-call(bf16[512,2048]{1,0:T(8,128)(2,1)} %multiply_convert_fusion.n2_ref.refs_0_, bf16[512,2048]{1,0:T(8,128)(2,1)} %collective-permute-done.13.n2_ref.refs_1_, bf16[512,2048]{1,0:T(8,128)(2,1)} %collective-permute-done.14.n2_ref.refs_2_, ...), custom_call_target="tpu_custom_call" | custom-call | flops 824633720832 | bytes 41943040 | tf_op jit(solution)/shard_map/experts_first_grads/pallas_call | solution.py:593
  743.6 45.1 %experts_1.6 = (bf16[4,512,2048]{2,1,0:T(8,128)(2,1)}, bf16[4,512,2048]{2,1,0:T(8,128)(2,1)}, bf16[4,512,2048]{2,1,0:T(8,128)(2,1)}, bf16[512,2048]{1,0:T(8,128)...) custom-call(bf16[512,2048]{1,0:T(8,128)(2,1)} %collective-permute-do, ...), custom_call_target="tpu_custom_call", output_to_operand_aliasing={{0}: (8, {}), {1}: (9, {}), {2}: (10, {})} | custom-call | flops 412316860416 | bytes 65011712 | tf_op jit(solution)/shard_map/experts_1/pallas_call | solution.py:483
  793.7 40.6 %experts_1.7 = (bf16[4,512,2048]{2,1,0:T(8,128)(2,1)}, bf16[4,512,2048]{2,1,0:T(8,128)(2,1)}, bf16[4,512,2048]{2,1,0:T(8,128)(2,1)}, bf16[512,2048]{1,0:T(8,128)...) custom-call(bf16[512,2048]{1,0:T(8,128)(2,1)} %collective-permute-do, ...), custom_call_target="tpu_custom_call", output_to_operand_aliasing={{0}: (8, {}), {1}: (9, {}), {2}: (10, {})} | custom-call | flops 412316860416 | bytes 65011712 | tf_op jit(solution)/shard_map/experts_1/pallas_call | solution.py:483
  843.7 47.1 %experts_last_grads.1 = (bf16[2048,4096]{1,0:T(8,128)(2,1)}, f32[2048,128]{1,0:T(8,128)}) custom-call(bf16[512,2048]{1,0:T(8,128)(2,1)} %multiply_convert_fusion.n2_ref.refs_0_, bf16[512,2048]{1,0:T(8,128)(2,1)} %collective-permute-done.13.n2_ref.refs_1_, bf16[512,2048]{1,0:T(8,128)(2,1)} %collective-permute-done.14.n2_ref.refs_2_, ...), custom_call_target="tpu_custom_call" | custom-call | flops 549755813888 | bytes 33554432 | tf_op jit(solution)/shard_map/experts_last_grads/pallas_call | solution.py:593
  922.5 38.5 %rest_grads.1 = bf16[2048,4096]{1,0:T(8,128)(2,1)} custom-call(bf16[512,2048]{1,0:T(8,128)(2,1)} %copy-done.17, bf16[512,2048]{1,0:T(8,128)(2,1)} %copy-done.47, bf16[512,2048]{1,0:T(8,128)(2,1)} %collective-permute-done.15.c_ref.refs_8_.refs_2_, bf16[512,2048]{1,0:T(8,128)(2,1)} %collective-permute-done.17.c_ref.refs_9_.refs_3_, ...), custom_call_target="tpu_custom_call" | custom-call | flops 21474836480 | bytes 33554432 | tf_op jit(solution)/shard_map/rest_grads/pallas_call | solution.py:593
  965.6 38.7 %attend_back.1 = (bf16[4,2,256,512]{3,2,1,0:T(8,128)(2,1)}, bf16[4,2,256,512]{3,2,1,0:T(8,128)(2,1)}, bf16[4,2,256,512]{3,2,1,0:T(8,128)(2,1)}, f32[8,128]{1,0:T(8,128)}) custom-call(bf16[4,2,256,512]{3,2,1,0:T(8,128)(2,1)} %get-tuple-element.150.q_ref.refs_0_, bf16[4,2,256,512]{3,2,1,0:T(8,128)(2,1)} %get-tuple-element.151.k_ref.refs_1_, ...), custom_call_target="tpu_custom_call" | custom-call | flops 171798691840 | bytes 25165824 | tf_op jit(solution)/shard_map/attend_back/pallas_call | solution.py:288
  1020.5 23.6 %qkv_grads.1 = (bf16[2048,1536]{1,0:T(8,128)(2,1)}, f32[2048,128]{1,0:T(8,128)}) custom-call(bf16[512,2048]{1,0:T(8,128)(2,1)} %multiply_convert_fusion.1.x_ref.refs_0_, bf16[512,2048]{1,0:T(8,128)(2,1)} %collective-permute-done.x_ref.refs_1_, bf16[512,2048]{1,0:T(8,128)(2,1)} %copy-done.45, bf16[512,2048]{1,0:T(8,128)(2,1)} %copy-done.46, ...), custom_call_target="tpu_custom_call" | custom-call | flops 12884901888 | bytes 23068672 | tf_op jit(solution)/shard_map/qkv_grads/pallas_call | solution.py:593
  1052.7 13.0 %collective-permute-done.26 = bf16[512,2048]{1,0:T(8,128)(2,1)} collective-permute-done((bf16[512,2048]{1,0:T(8,128)(2,1)S(1)}, bf16[512,2048]{1,0:T(8,128)(2,1)}, u32[]{:S(2)}, u32[]{:S(2)}) %collective-permute-start.26) | collective-permute-done | bytes 2097184 | tf_op jit(solution)/shard_map/ppermute | solution.py:65
  1083.4 35.2 %collective-permute-done.27 = bf16[512,2048]{1,0:T(8,128)(2,1)} collective-permute-done((bf16[512,2048]{1,0:T(8,128)(2,1)}, bf16[512,2048]{1,0:T(8,128)(2,1)}, u32[]{:S(2)}, u32[]{:S(2)}) %collective-permute-start.27) | collective-permute-done | bytes 2097184 | tf_op jit(solution)/shard_map/ppermute | solution.py:65
  1132.3 41.2 %collective-permute-done.31 = f32[290,128]{1,0:T(8,128)S(1)} collective-permute-done((f32[290,128]{1,0:T(8,128)S(1)}, f32[290,128]{1,0:T(8,128)S(1)}, u32[]{:S(2)}, u32[]{:S(2)}) %collective-permute-start.31) | collective-permute-done | bytes 148512 | tf_op jit(solution)/shard_map/ppermute | solution.py:795
  1218.7 34.9 %collective-permute-done.35 = bf16[256,512]{1,0:T(8,128)(2,1)S(1)} collective-permute-done((bf16[256,512]{1,0:T(8,128)(2,1)S(1)}, bf16[256,512]{1,0:T(8,128)(2,1)S(1)}, u32[]{:S(2)}, u32[]{:S(2)}) %collective-permute-start.35) | collective-permute-done | bytes 262176 | tf_op jit(solution)/shard_map/ppermute | solution.py:65
  (292 shorter events, 347.3 us)
Async XLA Ops:
  7.2 59.4 %all-gather.8.cloned.1.call-start = ((), (), s32[]{:S(2)}) async-start(), calls=%async_computation.4 | async-start | bytes 7667712 | tf_op jit(solution)/shard_map/all_gather | solution.py:643
  10.3 194.3 %all-gather.10.cloned.1.call-start = ((), (), s32[]{:S(2)}) async-start(), calls=%async_computation.9 | async-start | bytes 28311552 | tf_op jit(solution)/shard_map/all_gather | solution.py:654
  15.6 51.0 %collective-permute-start = (bf16[512,2048]{1,0:T(8,128)(2,1)}, bf16[512,2048]{1,0:T(8,128)(2,1)}, u32[]{:S(2)}, u32[]{:S(2)}) collective-permute-start(bf16[512,2048]{1,0:T(8,128)(2,1)} %multiply_convert_fusion.1.x_ref.refs_0_), channel_id=1, source_target_pairs={{0,1},{1,2},{2,3},{3,0},{4,5},{5,6},{6,7},{7,4},{8,9},{9,10},{10,1... | collective-permute-start | bytes 6291464 | tf_op jit(solution)/shard_map/ppermute | solution.py:65
  72.9 282.2 %all-gather.12.cloned.1.call-start = ((), (), s32[]{:S(2)}) async-start(), calls=%async_computation.10 | async-start | bytes 9437184 | tf_op jit(solution)/shard_map/all_gather | solution.py:654
  76.8 48.8 %collective-permute-start.1 = (bf16[512,2048]{1,0:T(8,128)(2,1)}, bf16[512,2048]{1,0:T(8,128)(2,1)S(1)}, u32[]{:S(2)}, u32[]{:S(2)}) collective-permute-start(bf16[512,2048]{1,0:T(8,128)(2,1)} %collective-permute-done.x_ref.refs_1_), channel_id=1, source_target_pairs={{0,1},{1,2},{2,3},{3,0},{4,5},{5,6},{6,7},{7,4},{8,9},{9,10},{10,1... | collective-permute-start | bytes 6291464 | tf_op jit(solution)/shard_map/ppermute | solution.py:65
  125.7 49.6 %collective-permute-start.2 = (bf16[512,2048]{1,0:T(8,128)(2,1)S(1)}, bf16[512,2048]{1,0:T(8,128)(2,1)S(1)}, u32[]{:S(2)}, u32[]{:S(2)}) collective-permute-start(bf16[512,2048]{1,0:T(8,128)(2,1)S(1)} %collective-permute-done.1.x_ref.refs_2_), channel_id=1, source_target_pairs={{0,1},{1,2},{2,3},{3,0},{4,5},{5,6},{6,7},{7,4},{8,9},{9,10},{10,1... | collective-permute-start | bytes 6291464 | tf_op jit(solution)/shard_map/ppermute | solution.py:65
  204.6 283.4 %all-gather.14.cloned.1.call-start = ((), (), s32[]{:S(2)}) async-start(), calls=%async_computation.11 | async-start | bytes 28311552 | tf_op jit(solution)/shard_map/all_gather | solution.py:654
  272.8 644.2 %reduce-scatter.5.cloned.1.call-start = ((), (), s32[]{:S(2)}) async-start(), calls=%async_computation.5 | async-start | bytes 28311552 | tf_op jit(solution)/shard_map/reduce_scatter | solution.py:747
  298.1 113.9 %collective-permute-start.15 = (bf16[512,2048]{1,0:T(8,128)(2,1)}, bf16[512,2048]{1,0:T(8,128)(2,1)}, u32[]{:S(2)}, u32[]{:S(2)}) collective-permute-start(bf16[512,2048]{1,0:T(8,128)(2,1)} %copy-done.47), channel_id=1, source_target_pairs={{0,1},{1,2},{2,3},{3,0},{4,5},{5,6},{6,7},{7,4},{8,9},{9,10},{10,1... | collective-permute-start | bytes 6291464 | tf_op jit(solution)/shard_map/ppermute | solution.py:65
  371.7 74.6 %collective-permute-start.13 = (bf16[512,2048]{1,0:T(8,128)(2,1)}, bf16[512,2048]{1,0:T(8,128)(2,1)}, u32[]{:S(2)}, u32[]{:S(2)}) collective-permute-start(bf16[512,2048]{1,0:T(8,128)(2,1)} %multiply_convert_fusion.n2_ref.refs_0_), channel_id=1, source_target_pairs={{0,1},{1,2},{2,3},{3,0},{4,5},{5,6},{6,7},{7,4},{8,9},{9,10},{10,1... | collective-permute-start | bytes 6291464 | tf_op jit(solution)/shard_map/ppermute | solution.py:65
  412.0 211.5 %collective-permute-start.17 = (bf16[512,2048]{1,0:T(8,128)(2,1)}, bf16[512,2048]{1,0:T(8,128)(2,1)}, u32[]{:S(2)}, u32[]{:S(2)}) collective-permute-start(bf16[512,2048]{1,0:T(8,128)(2,1)} %collective-permute-done.15.c_ref.refs_8_.refs_2_), channel_id=1, source_target_pairs={{0,1},{1,2},{2,3},{3,0},{4,5},{5,6},{6,7},{7,4},{8,9},{9,10},{10,1... | collective-permute-start | bytes 6291464 | tf_op jit(solution)/shard_map/ppermute | solution.py:65
  446.4 89.1 %collective-permute-start.14 = (bf16[512,2048]{1,0:T(8,128)(2,1)}, bf16[512,2048]{1,0:T(8,128)(2,1)}, u32[]{:S(2)}, u32[]{:S(2)}) collective-permute-start(bf16[512,2048]{1,0:T(8,128)(2,1)} %collective-permute-done.13.n2_ref.refs_1_), channel_id=1, source_target_pairs={{0,1},{1,2},{2,3},{3,0},{4,5},{5,6},{6,7},{7,4},{8,9},{9,10},{10,1... | collective-permute-start | bytes 6291464 | tf_op jit(solution)/shard_map/ppermute | solution.py:65
  535.4 88.0 %collective-permute-start.16 = (bf16[512,2048]{1,0:T(8,128)(2,1)}, bf16[512,2048]{1,0:T(8,128)(2,1)}, u32[]{:S(2)}, u32[]{:S(2)}) collective-permute-start(bf16[512,2048]{1,0:T(8,128)(2,1)} %collective-permute-done.14.n2_ref.refs_2_), channel_id=1, source_target_pairs={{0,1},{1,2},{2,3},{3,0},{4,5},{5,6},{6,7},{7,4},{8,9},{9,10},{10,1... | collective-permute-start | bytes 6291464 | tf_op jit(solution)/shard_map/ppermute | solution.py:65
  621.0 50.7 %collective-permute-start.19 = (bf16[512,2048]{1,0:T(8,128)(2,1)}, bf16[512,2048]{1,0:T(8,128)(2,1)}, u32[]{:S(2)}, u32[]{:S(2)}) collective-permute-start(bf16[512,2048]{1,0:T(8,128)(2,1)} %add_convert_fusion.7), channel_id=1, source_target_pairs={{0,1},{1,2},{2,3},{3,0},{4,5},{5,6},{6,7},{7,4},{8,9},{9,10},{10,1... | collective-permute-start | bytes 6291464 | tf_op jit(solution)/shard_map/ppermute | solution.py:65
  662.6 81.0 %collective-permute-start.18 = (bf16[512,2048]{1,0:T(8,128)(2,1)}, bf16[512,2048]{1,0:T(8,128)(2,1)}, u32[]{:S(2)}, u32[]{:S(2)}) collective-permute-start(bf16[512,2048]{1,0:T(8,128)(2,1)} %add_convert_fusion.8), channel_id=1, source_target_pairs={{0,1},{1,2},{2,3},{3,0},{4,5},{5,6},{6,7},{7,4},{8,9},{9,10},{10,1... | collective-permute-start | bytes 6291464 | tf_op jit(solution)/shard_map/ppermute | solution.py:65
  743.2 309.5 %reduce-scatter.7.cloned.1.call-start = ((), (), s32[]{:S(2)}) async-start(), calls=%async_computation.6 | async-start | bytes 18874368 | tf_op jit(solution)/shard_map/reduce_scatter | solution.py:766
  911.0 292.2 %reduce-scatter.11.cloned.1.call-start = ((), (), s32[]{:S(2)}) async-start(), calls=%async_computation.8 | async-start | bytes 18874368 | tf_op jit(solution)/shard_map/reduce_scatter | solution.py:780
  1016.0 248.1 %reduce-scatter.9.cloned.1.call-start = ((), (), s32[]{:S(2)}) async-start(), calls=%async_computation.7 | async-start | bytes 7077888 | tf_op jit(solution)/shard_map/reduce_scatter | solution.py:786
  1017.5 48.1 %collective-permute-start.26 = (bf16[512,2048]{1,0:T(8,128)(2,1)S(1)}, bf16[512,2048]{1,0:T(8,128)(2,1)}, u32[]{:S(2)}, u32[]{:S(2)}) collective-permute-start(bf16[512,2048]{1,0:T(8,128)(2,1)S(1)} %copy-done.14), channel_id=1, source_target_pairs={{0,1},{1,2},{2,3},{3,0},{4,5},{5,6},{6,7},{7,4},{8,9},{9,10},{10,1... | collective-permute-start | bytes 6291464 | tf_op jit(solution)/shard_map/ppermute | solution.py:65
  1070.2 48.4 %collective-permute-start.27 = (bf16[512,2048]{1,0:T(8,128)(2,1)}, bf16[512,2048]{1,0:T(8,128)(2,1)}, u32[]{:S(2)}, u32[]{:S(2)}) collective-permute-start(bf16[512,2048]{1,0:T(8,128)(2,1)} %add_convert_fusion.2), channel_id=1, source_target_pairs={{0,1},{1,2},{2,3},{3,0},{4,5},{5,6},{6,7},{7,4},{8,9},{9,10},{10,1... | collective-permute-start | bytes 6291464 | tf_op jit(solution)/shard_map/ppermute | solution.py:65
  1080.8 47.5 %collective-permute-start.30 = (f32[290,128]{1,0:T(8,128)S(1)}, f32[290,128]{1,0:T(8,128)S(1)}, u32[]{:S(2)}, u32[]{:S(2)}) collective-permute-start(f32[290,128]{1,0:T(8,128)S(1)} %pad_maximum_fusion.5), channel_id=1, source_target_pairs={{0,1},{1,0},{2,3},{3,2},{4,5},{5,4},{6,7},{7,6},{8,9},{9,8},{10,11... | collective-permute-start | bytes 445448 | tf_op jit(solution)/shard_map/ppermute | solution.py:795
  1123.1 75.4 %collective-permute-start.28 = (bf16[512,2048]{1,0:T(8,128)(2,1)}, bf16[512,2048]{1,0:T(8,128)(2,1)}, u32[]{:S(2)}, u32[]{:S(2)}) collective-permute-start(bf16[512,2048]{1,0:T(8,128)(2,1)} %add_convert_fusion.1), channel_id=1, source_target_pairs={{0,1},{1,2},{2,3},{3,0},{4,5},{5,6},{6,7},{7,4},{8,9},{9,10},{10,1... | collective-permute-start | bytes 6291464 | tf_op jit(solution)/shard_map/ppermute | solution.py:65
  1198.5 55.5 %collective-permute-start.29 = (bf16[512,2048]{1,0:T(8,128)(2,1)}, bf16[512,2048]{1,0:T(8,128)(2,1)}, u32[]{:S(2)}, u32[]{:S(2)}) collective-permute-start(bf16[512,2048]{1,0:T(8,128)(2,1)} %add_convert_fusion.3), channel_id=1, source_target_pairs={{0,1},{1,2},{2,3},{3,0},{4,5},{5,6},{6,7},{7,4},{8,9},{9,10},{10,1... | collective-permute-start | bytes 6291464 | tf_op jit(solution)/shard_map/ppermute | solution.py:65
  1204.2 49.3 %collective-permute-start.35 = (bf16[256,512]{1,0:T(8,128)(2,1)S(1)}, bf16[256,512]{1,0:T(8,128)(2,1)S(1)}, u32[]{:S(2)}, u32[]{:S(2)}) collective-permute-start(bf16[256,512]{1,0:T(8,128)(2,1)S(1)} %slice.193), channel_id=1, source_target_pairs={{0,3},{1,0},{2,1},{3,2},{4,7},{5,4},{6,5},{7,6},{8,11},{9,8},{10,9... | collective-permute-start | bytes 786440 | tf_op jit(solution)/shard_map/ppermute | solution.py:65
  (74 other events, 1563.4 us)
Sparse Core Ops, SparseCore 0:
  10.5 50.4 all-gather.7
  73.0 124.7 all-gather.9
  204.7 55.8 all-gather.11
  272.9 124.5 all-gather.13
  743.3 154.2 reduce-scatter.4
  911.1 117.4 reduce-scatter.6
  1032.2 115.9 reduce-scatter.10
  1151.6 64.9 reduce-scatter.8

commit v3 on v2

--- a/solution.py
+++ b/solution.py
@@ -69,11 +69,8 @@
     return lax.optimization_barrier((value,) + done)[0]
 
 
-def ring_gather(value, count, step=1):
-    held = [value]
-    for _ in range(count - 1):
-        held.append(shift(held[-1], count, step))
-    return held
+def exchange(parts, step):
+    return [parts[0]] + [shift(parts[s], len(parts), s * step) for s in range(1, len(parts))]
 
 
 def plus(arrived, *parts):
@@ -81,16 +78,6 @@
     for part in parts:
         total = total + part.astype(F32)
     return total
-
-
-def ring_scatter(parts, step=1):
-    count = len(parts)
-    total = parts[1]
-    for k in range(2, count + 1):
-        arrived = shift(total, count, step)
-        if k < count:
-            total = plus(arrived, parts[k]).astype(BF)
-    return plus(arrived, parts[0])
 
 
 def keep_kernel(bits, order_ref, keep_ref):
@@ -177,7 +164,7 @@
         out_shape=shapes,
         input_output_aliases={8 + i: i for i in range(len(aliased))},
         compiler_params=params(1),
-        cost_estimate=cost(rows * depth * local * 3, rows * depth * 2 + depth * local * 6),
+        cost_estimate=cost(rows * depth * local * 3 // 16, rows * depth * 2 + depth * local * 6),
         name="project",
     )(x, weights, weights, weights, cos, sin, gain_q, gain_k, *aliased)
 
@@ -402,7 +389,7 @@
 
 def expert_kernel(group, experts, n2_ref, c_ref, keep_ref, router_ref, tile_ref, w_ref, *rest):
     last = group == GROUPS - 1
-    wt_ref, grad_in = rest[0], rest[1]
+    wt_ref, grad_in, y_in, dn_in = rest[:4]
     hp_ref, da_ref, du_ref, y_ref, dn_ref, grad_out = rest[-14:-8]
     probs, gates, grads, hp_all, da_all, du_all, full, low = rest[-8:]
     e = pl.program_id(0)
@@ -461,15 +448,19 @@
     @pl.when(e >= experts)
     def _():
         wide = experts * ff
-        y_ref[...] = dot_nn(hp_all[...], wt_ref[0, 2].reshape(wide, tile)).astype(BF)
+        y = dot_nn(hp_all[...], wt_ref[0, 2].reshape(wide, tile))
         total = dot_nn(da_all[...], wt_ref[0, 0].reshape(wide, tile))
         total = total + dot_nn(du_all[...], wt_ref[0, 1].reshape(wide, tile))
         if last:
             total = total + dot_nt(low[...], tile_ref[...])
+        if group > 0:
+            y = y + y_in[...].astype(F32)
+            total = total + dn_in[...].astype(F32)
+        y_ref[...] = y.astype(BF)
         dn_ref[...] = total.astype(BF)
 
 
-def experts_pass(k, count, group, n2, cot, keep, weights_all, weights, grad, kept):
+def experts_pass(k, count, group, n2, cot, keep, weights_all, weights, before, kept):
     rows, depth = n2.shape
     blocks, _, experts, ff, tile = weights.shape
     router_col = weights_all.shape[1] // LANES - 1
@@ -479,7 +470,7 @@
     wide = pl.BlockSpec((1, rows, ff), lambda e: (k, 0, near(e)))
     part = pl.BlockSpec((rows, tile), lambda e: (0, far(e)))
     aliased = list(kept or ())
-    grad = jnp.zeros((8, LANES), F32) if grad is None else grad
+    grad, *sums = before or (jnp.zeros((8, LANES), F32),)
     return pl.pallas_call(
         functools.partial(expert_kernel, group, experts),
         grid=(experts + blocks,),
@@ -493,12 +484,13 @@
             pl.BlockSpec((1, 3, experts, ff, tile), lambda e: (far(e), 0, 0, 0, 0)),
             const(*grad.shape),
         ]
+        + [part] * len(sums)
         + [pl.BlockSpec(memory_space=pl.ANY)] * len(aliased),
         out_specs=[wide, wide, wide, part, part, const(rows, LANES)],
         out_shape=[struct((count, rows, experts * ff), BF)] * 3
         + [struct((rows, depth), BF)] * 2
         + [struct((rows, LANES), BF if group == GROUPS - 1 else F32)],
-        input_output_aliases={8 + i: i for i in range(len(aliased))},
+        input_output_aliases={8 + len(sums) + i: i for i in range(len(aliased))},
         scratch_shapes=[pltpu.VMEM((rows, LANES), F32)] * 3
         + [pltpu.VMEM((rows, experts * ff), BF)] * 3
         + [pltpu.VMEM((3, ff, depth), BF), pltpu.VMEM((rows, LANES), BF)],
@@ -509,7 +501,7 @@
             2 * rows * ff * experts,
         ),
         name=f"experts_{group}",
-    )(n2, cot, keep, weights_all, weights_all, weights, weights, grad, *aliased)
+    )(n2, cot, keep, weights_all, weights_all, weights, weights, grad, *sums, *aliased)
 
 
 def row_grad_kernel(count, plan, router, gain, *refs):
@@ -645,15 +637,8 @@
     tok = jnp.transpose(tokens, (1, 0, 2)).reshape(rows, depth)
     tok_float = tok.astype(F32)
     n1_own = (tok_float * rms_scale(tok_float) * attn_gain).astype(BF)
-    n1 = [n1_own, shift(n1_own, count, 1)]
-    turned = jnp.stack(
-        [jnp.swapaxes(gate_weight, 1, 2), jnp.swapaxes(up_weight, 1, 2), down_weight]
-    )
-    turned = after(turned, weights_all, n1[1])
-    each = EXPERTS // GROUPS
-    gather = lambda value: lax.all_gather(value, "fsdp", axis=0, tiled=False)
-    moe_weights = [gather(turned[:, g * each : (g + 1) * each]) for g in range(GROUPS)]
-
+    outs = exchange([after(out_weight, n1_own)] * count, -1)
+    n1 = [n1_own, shift(after(n1_own, *outs[1:]), count, 1)]
     own_pos = me * per + jnp.arange(per, dtype=jnp.int32)
     valid_own = own_pos[None, :] < lengths[:, None]
     route_t = jnp.transpose(routes, (2, 1, 0)).reshape(TOP, rows)
@@ -663,6 +648,25 @@
     for j in range(TOP):
         order_own = jnp.where(route_t[j][None, :] == names, order_t[j][None, :], order_own)
     order_own = jnp.where(valid_own.reshape(1, rows), order_own, FAR)
+    orders = exchange([after(order_own, n1[1])] * count, 1)
+
+    each = EXPERTS // GROUPS
+    gather = lambda value: lax.all_gather(value, "fsdp", axis=0, tiled=False)
+
+    def group_weights(g):
+        part = slice(g * each, (g + 1) * each)
+        stacked = jnp.concatenate(
+            [
+                jnp.swapaxes(gate_weight[part], 1, 2),
+                jnp.swapaxes(up_weight[part], 1, 2),
+                down_weight[part],
+            ]
+        )
+        stacked = after(stacked, weights_all, n1[1])
+        return gather(stacked.reshape((3, each) + stacked.shape[1:]))
+
+    out_all = gather(jnp.concatenate(outs, axis=0))
+    moe_weights = [group_weights(g) for g in range(GROUPS)]
     owner = (me - jnp.arange(count, dtype=jnp.int32)) % count
     chunk_pos = owner[:, None] * per + jnp.arange(per, dtype=jnp.int32)[None, :]
     half = head_width // 2
@@ -678,54 +682,44 @@
     kept, done = None, []
     for k in range(count):
         if k > 1:
-            n1.append(shift(after(n1[-1], *done[: k - 2]), count, 1))
+            n1.append(shift(after(n1[-1], *(done[: k - 1] if k > 2 else ())), count, 1))
         kept = project(
             k, count, seqs, after(n1[k], *done[-1:]), weights_all, cos, sin, gain_q, gain_k, kept
         )
         done.append(kept[4])
-    outs = ring_gather(after(out_weight, n1[-1]), count, -1)
-    orders = ring_gather(after(order_own, n1[-1]), count)
     q_raw, k_raw, q, k_low, v = kept
-    out_all = gather(after(jnp.concatenate(outs, axis=0), moe_weights[0], v))
+    keep = keep_rows(after(jnp.stack(orders), done[1]), length * seqs * TOP)
 
     cot = jnp.transpose(cotangent, (1, 0, 2)).reshape(rows, depth)
     cot_own = jnp.where(valid_own.reshape(rows, 1), cot, jnp.zeros_like(cot))
-    cots = [cot_own, shift(after(cot_own, n1[-1], outs[-1], orders[-1]), count, 1)]
-    keep = keep_rows(after(jnp.stack(orders), v), length * seqs * TOP)
+    cots = [cot_own, shift(after(cot_own, n1[-1], done[count - 2]), count, 1)]
 
     ob, lse = attend(q, k_low, v, key_valid, scale)
-    ob_rows = after(ob.reshape(count, rows, local), cots[1], keep)
-    ob_parts = [ob_rows[0]] + [shift(ob_rows[s], count, -s) for s in range(1, count)]
+    ob_rows = after(ob.reshape(count, rows, local), cots[1])
+    ob_parts = exchange(ob_rows, -1)
     x1 = out_project(tok, ob_parts, out_all)
     n2_own = (x1 * rms_scale(x1) * moe_gain).astype(BF)
     n2 = [n2_own, shift(n2_own, count, 1)]
-    cots.append(shift(after(cots[1], *ob_parts[1:]), count, 1))
     token = [n2_own]
 
     bufs = [None] * GROUPS
-    ys = [[] for _ in range(count)]
-    dns = [[] for _ in range(count)]
-    grads = [None] * count
+    ys, dns, grads = [None] * count, [None] * count, [None] * count
 
     def run(group, k):
-        hp, da, du, y_k, dn_k, grads[k] = experts_pass(
+        before = (grads[k], ys[k], dns[k]) if group else None
+        hp, da, du, ys[k], dns[k], grads[k] = experts_pass(
             k, count, group, after(n2[k], *token), cots[k], keep, weights_all, moe_weights[group],
-            grads[k], bufs[group],
+            before, bufs[group],
         )
         bufs[group] = (hp, da, du)
-        ys[k].append(y_k)
-        dns[k].append(dn_k)
-        token[0] = dn_k
-        return dn_k
+        token[0] = dns[k]
+        return dns[k]
 
     def next_inputs(done):
         if len(n2) < count:
             n2.append(shift(after(n2[-1], done), count, 1))
         if len(cots) < count:
             cots.append(shift(after(cots[-1], done), count, 1))
-
-    def both(parts):
-        return plus(parts[0], *parts[1:]).astype(BF)
 
     ready = run(0, 0)
     next_inputs(ready)
@@ -736,9 +730,9 @@
         run(0, k)
         if k < count - 1:
             next_inputs(run(1, k - 1))
-    dn_run = shift(both(dns[1]), count, 1)
+    dn_run = shift(dns[1], count, 1)
     token.append(dn_run)
-    y_run = shift(after(both(ys[1]), dns[count - 1][0]), count, 1)
+    y_run = shift(after(ys[1], dns[count - 1]), count, 1)
     ff = gate_weight.shape[2]
     hp, da, du = bufs[0]
     first_full = row_grads(
@@ -748,7 +742,7 @@
     token = [first_full, y_run]
     run(1, count - 2)
     for k in range(2, count):
-        dn_run = plus(dn_run, *dns[k]).astype(BF)
+        dn_run = plus(dn_run, dns[k]).astype(BF)
         token.append(dn_run)
         if k == count - 2:
             run(1, count - 1)
@@ -757,7 +751,8 @@
     last_full, router_term = row_grads(
         [([after(n2[0], *token)] + n2[1:], [da, du])], ff, "experts_last_grads", grads
     )
-    dn2 = plus(after(dn_run, last_full), *dns[0])
+    dn2 = plus(after(dn_run, last_full), dns[0])
+
 
     moe_back, moe_gain_term = norm_back(dn2, x1, moe_gain)
     dx1 = moe_back + cot_own.astype(F32)
@@ -765,19 +760,22 @@
     dob = out_back(db, out_all, count)
     last_own = lax.psum_scatter(after(last_full, dob), "fsdp", scatter_dimension=0, tiled=True)
     dob = after(dob, first_own)
-    dob_parts = [dob[0]] + [shift(dob[s], count, s) for s in range(1, count)]
+    dob_parts = exchange(dob, 1)
     rest_full = row_grads(
         [(cots, [hp]), ([after(db, dob)], ob_parts)], ff, "rest_grads"
     )[0]
     d_ob = jnp.stack(dob_parts).reshape(count, seqs, per, local)
-    d_ob = after(d_ob, rest_full)
-    y_run = shift(after(plus(y_run, *ys[2]).astype(BF), d_ob), count, 1)
+    y_sum = plus(after(y_run, dob), ys[2]).astype(BF)
+    d_ob = after(d_ob, rest_full, y_sum)
+    y_run = shift(after(y_sum, d_ob), count, 1)
+    for k in range(3, count - 1):
+        y_run = shift(plus(y_run, ys[k]).astype(BF), count, 1)
 
     dq, dk, dv, gains = attend_back(
         q, k_low, v, ob, d_ob, lse, key_valid, q_raw, k_raw, cos, sin, gain_q, gain_k, scale
     )
     part = input_back(1, after(dq, y_run), dk, dv, weights_all)
-    rest_own = lax.psum_scatter(after(rest_full, part), "fsdp", scatter_dimension=0, tiled=True)
+    rest_own = lax.psum_scatter(after(rest_full, d_ob), "fsdp", scatter_dimension=0, tiled=True)
     dn1_run = shift(part, count, 1)
     qkv_full, attn_gain_wide = row_grads(
         [([after(n1[0], part)] + n1[1:], [a.reshape(count * rows, local) for a in (dq, dk, dv)])],
@@ -805,19 +803,19 @@
         dn1_run = shift(dn1_run, count, 1)
         part = input_back((k + 1) % count, dq, dk, dv, weights_all)
     dn1 = plus(dn1_run, part)
-    for k in range(3, count):
-        y_run = shift(after(plus(y_run, *ys[k]).astype(BF), dn1_run), count, 1)
     for bit in bits[max(count - 2, 0) :]:
         packed = across(packed, "tp", bit)
+    qkv_sum = qkv_own.astype(F32)
+    out_own = rest_own[:, each * ff :]
+    out_own = after(out_own, dn1_run)
+    out_pieces = [out_own[:, s * local : (s + 1) * local] for s in range(count)]
+    out_pieces = exchange(out_pieces, 1)
+    out_weight_grad = jnp.transpose(plus(*out_pieces))
+    y_run = plus(after(y_run, *out_pieces[1:]), ys[count - 1]).astype(BF)
+    y_run = shift(y_run, count, 1)
+
     for b in range(lax.axis_size("fsdp").bit_length() - 1):
-        packed = across(packed, "fsdp", 1 << b)
-
-    layer_out = (x1 + plus(y_run, *ys[0])).astype(BF)
-
-    qkv_sum = qkv_own.astype(F32)
-    out_own = after(rest_own, dn1_run)[:, each * ff :]
-    out_pieces = [out_own[:, s * local : (s + 1) * local] for s in range(count)]
-    out_weight_grad = jnp.transpose(ring_scatter(out_pieces, -1))
+        packed = across(after(packed, part, *out_pieces[1:]) if b == 0 else packed, "fsdp", 1 << b)
 
     def expert_out(owns, axes):
         shaped = [own.reshape(own.shape[0], each, ff) for own in owns]
@@ -830,6 +828,8 @@
 
     attn_back = norm_back(dn1, tok_float, attn_gain)[0]
     tokens_grad = attn_back + dx1
+    y_run = after(y_run, tokens_grad, out_weight_grad)
+    layer_out = (x1 + plus(y_run, ys[0])).astype(BF)
 
     split = depth * EXPERTS // LANES
     across = depth // LANES

time: 1290 us -> 1190 us (0.922)
  waiting for transfers between devices: 370 us -> 309 us
  starting transfers between devices: 102 us -> 63.7 us
  other arithmetic: 92.3 us -> 78.9 us
    ppermute x33, waiting for transfers between devices: 326 us -> 266 us  [shift(): lax.ppermute(value, 'tp', [(i, (i + step) % count) for i in range(count)])]
    ppermute x33, starting transfers between devices: 90.3 us -> 57.5 us  [shift(): lax.ppermute(value, 'tp', [(i, (i + step) % count) for i in range(count)])]
    convert_element_type x9 -> x5, other arithmetic: 29.4 us -> 20.8 us  [the longest x2 9.09 us: per_device(): dn_run = plus(dn_run, dns[k]).astype(BF)]
  transfers between devices with their start and end apart: 46 -> 46, of which waited for: 21 -> 24; matrix products, arithmetic and copies ran while one was open for 10% -> 10% of each run, Pallas kernels for 51% -> 55%
where the time goes in v3:
time: 1190 us; the launch traced here: 1180 us
  Pallas kernels  654 us (55%)
  waiting for transfers between devices  309 us (26%)
  other arithmetic  78.9 us (7%)
  starting transfers between devices  63.7 us (5%)
  local copies, waits for them, and re-layouts  60.4 us (5%)
  between operations  15.2 us (1%)
    pallas_call x8, Pallas kernels, experts_pass(): pl.pallas_call(functools.partial(expert_kernel, group, experts), grid=(ex...  324 us
    ppermute x33, waiting for transfers between devices, shift(): lax.ppermute(value, 'tp', [(i, (i + step) % count) for i in range(count)])  266 us
    pallas_call x4, Pallas kernels, row_grads(): pl.pallas_call(functools.partial(row_grad_kernel, len(dls), tuple(plan),...  181 us
    ppermute x33, starting transfers between devices, shift(): lax.ppermute(value, 'tp', [(i, (i + step) % count) for i in range(count)])  57.5 us
    pallas_call x1, Pallas kernels, attend_back(): pl.pallas_call(functools.partial(attend_back_kernel, scale), grid=(seqs,...  38.6 us
    pallas_call x4, Pallas kernels, project(): pl.pallas_call(functools.partial(qkv_kernel, seqs), grid=(groups,), in_sp...  36.6 us
    ppermute x5, waiting for transfers between devices, per_device(): lax.ppermute(value, axis, [(i, i ^ bit) for i in range(lax.axis_size(axis...  36.1 us
    pallas_call x4, Pallas kernels, input_back(): pl.pallas_call(input_back_kernel, grid=(depth // tile,), in_specs=[grad]...  31.9 us
  transfers between devices with their start and end apart: 46, of which 24 were waited for; matrix products, arithmetic and copies ran while one was open for 10% of the time, Pallas kernels for 55%

profile of v3, /device:TPU:0, one launch (start us, length us, event | category | flops | bytes accessed | tf_op | source)
XLA Modules:
  0.0 1182.0 jit_solution(11924821933574908590)
XLA Ops:
  65.8 25.8 %collective-permute-done.3.x_ref.refs_1_ = bf16[512,2048]{1,0:T(8,128)(2,1)} collective-permute-done((bf16[512,2048]{1,0:T(8,128)(2,1)S(1)}, bf16[512,2048]{1,0:T(8,128)(2,1)}, u32[]{:S(2)}, u32[]{:S(2)}) %collective-permute-start.3) | collective-permute-done | bytes 2097184 | tf_op jit(solution)/shard_map/ppermute | solution.py:65
  118.7 21.7 %collective-permute-done.4.x_ref.refs_2_ = bf16[512,2048]{1,0:T(8,128)(2,1)S(1)} collective-permute-done((bf16[512,2048]{1,0:T(8,128)(2,1)}, bf16[512,2048]{1,0:T(8,128)(2,1)S(1)}, u32[]{:S(2)}, u32[]{:S(2)}) %collective-permute-start.4) | collective-permute-done | bytes 2097184 | tf_op jit(solution)/shard_map/ppermute | solution.py:65
  148.8 37.3 %collective-permute-done.13 = s32[16,512]{1,0:T(8,128)S(1)} collective-permute-done((s32[16,512]{1,0:T(8,128)S(1)}, s32[16,512]{1,0:T(8,128)S(1)}, u32[]{:S(2)}, u32[]{:S(2)}) %collective-permute-start.13) | collective-permute-done | bytes 32800 | tf_op jit(solution)/shard_map/ppermute | solution.py:65
  210.7 18.3 %attend.1 = (bf16[4,2,256,512]{3,2,1,0:T(8,128)(2,1)}, f32[8,4,256]{2,1,0:T(4,128)}) custom-call(bf16[4,2,256,512]{3,2,1,0:T(8,128)(2,1)} %get-tuple-element.156.q_ref.refs_0_, bf16[4,2,256,512]{3,2,1,0:T(8,128)(2,1)} %get-tuple-element.157.k_ref.refs_1_, bf16[4,2,256,512]{3,2,1,0:T(8,128)(2,1)} %get-tuple-element.158.v_ref.refs_2_, ...), custom_call_target="tpu_custom_call" | custom-call | flops 68719476736 | bytes 8388608 | tf_op jit(solution)/shard_map/attend/pallas_call | solution.py:191
  229.1 20.7 %collective-permute-done.6.c_ref.refs_7_.refs_1_ = bf16[512,2048]{1,0:T(8,128)(2,1)} collective-permute-done((bf16[512,2048]{1,0:T(8,128)(2,1)S(1)}, bf16[512,2048]{1,0:T(8,128)(2,1)}, u32[]{:S(2)}, u32[]{:S(2)}) %collective-permute-start.6) | collective-permute-done | bytes 2097184 | tf_op jit(solution)/shard_map/ppermute | solution.py:65
  269.0 20.7 %collective-permute-done.8.refs_2_.refs_8_ = bf16[512,512]{1,0:T(8,128)(2,1)S(1)} collective-permute-done((bf16[512,512]{1,0:T(8,128)(2,1)S(1)}, bf16[512,512]{1,0:T(8,128)(2,1)S(1)}, u32[]{:S(2)}, u32[]{:S(2)}) %collective-permute-start.8) | collective-permute-done | bytes 524320 | tf_op jit(solution)/shard_map/ppermute | solution.py:65
  320.2 39.8 %experts_0.4 = (bf16[4,512,2048]{2,1,0:T(8,128)(2,1)}, bf16[4,512,2048]{2,1,0:T(8,128)(2,1)}, bf16[4,512,2048]{2,1,0:T(8,128)(2,1)}, bf16[512,2048]{1,0:T(8,128)...) custom-call(bf16[512,2048]{1,0:T(8,128)(2,1)} %multiply_convert_fusion.n2_ref.refs_0_, ...), custom_call_target="tpu_custom_call" | custom-call | flops 412316860416 | bytes 65011712 | tf_op jit(solution)/shard_map/experts_0/pallas_call | solution.py:474
  367.7 39.3 %experts_0.5 = (bf16[4,512,2048]{2,1,0:T(8,128)(2,1)}, bf16[4,512,2048]{2,1,0:T(8,128)(2,1)}, bf16[4,512,2048]{2,1,0:T(8,128)(2,1)}, bf16[512,2048]{1,0:T(8,128)...) custom-call(bf16[512,2048]{1,0:T(8,128)(2,1)} %collective-permute-do, ...), custom_call_target="tpu_custom_call", output_to_operand_aliasing={{0}: (8, {}), {1}: (9, {}), {2}: (10, {})} | custom-call | flops 412316860416 | bytes 65011712 | tf_op jit(solution)/shard_map/experts_0/pallas_call | solution.py:474
  407.0 40.0 %experts_1.4 = (bf16[4,512,2048]{2,1,0:T(8,128)(2,1)}, bf16[4,512,2048]{2,1,0:T(8,128)(2,1)}, bf16[4,512,2048]{2,1,0:T(8,128)(2,1)}, bf16[512,2048]{1,0:T(8,128)...) custom-call(bf16[512,2048]{1,0:T(8,128)(2,1)} %multiply_convert_fusion.n2_ref.refs_0_, ...), custom_call_target="tpu_custom_call" | custom-call | flops 412316860416 | bytes 65011712 | tf_op jit(solution)/shard_map/experts_1/pallas_call | solution.py:474
  459.7 39.1 %experts_0.6 = (bf16[4,512,2048]{2,1,0:T(8,128)(2,1)}, bf16[4,512,2048]{2,1,0:T(8,128)(2,1)}, bf16[4,512,2048]{2,1,0:T(8,128)(2,1)}, bf16[512,2048]{1,0:T(8,128)...) custom-call(bf16[512,2048]{1,0:T(8,128)(2,1)} %collective-permute-do, ...), custom_call_target="tpu_custom_call", output_to_operand_aliasing={{0}: (8, {}), {1}: (9, {}), {2}: (10, {})} | custom-call | flops 412316860416 | bytes 65011712 | tf_op jit(solution)/shard_map/experts_0/pallas_call | solution.py:474
  498.8 40.1 %experts_1.5 = (bf16[4,512,2048]{2,1,0:T(8,128)(2,1)}, bf16[4,512,2048]{2,1,0:T(8,128)(2,1)}, bf16[4,512,2048]{2,1,0:T(8,128)(2,1)}, bf16[512,2048]{1,0:T(8,128)...) custom-call(bf16[512,2048]{1,0:T(8,128)(2,1)} %collective-permute-do, ...), custom_call_target="tpu_custom_call", output_to_operand_aliasing={{0}: (10, {}), {1}: (11, {}), {2}: (12, {})} | custom-call | flops 412316860416 | bytes 65011712 | tf_op jit(solution)/shard_map/experts_1/pallas_call | solution.py:474
  539.2 14.6 %collective-permute-done.17.c_ref.refs_9_.refs_3_ = bf16[512,2048]{1,0:T(8,128)(2,1)} collective-permute-done((bf16[512,2048]{1,0:T(8,128)(2,1)}, bf16[512,2048]{1,0:T(8,128)(2,1)}, u32[]{:S(2)}, u32[]{:S(2)}) %collective-permute-start.17) | collective-permute-done | bytes 2097184 | tf_op jit(solution)/shard_map/ppermute | solution.py:65
  553.8 39.2 %experts_0.7 = (bf16[4,512,2048]{2,1,0:T(8,128)(2,1)}, bf16[4,512,2048]{2,1,0:T(8,128)(2,1)}, bf16[4,512,2048]{2,1,0:T(8,128)(2,1)}, bf16[512,2048]{1,0:T(8,128)...) custom-call(bf16[512,2048]{1,0:T(8,128)(2,1)} %collective-permute-do, ...), custom_call_target="tpu_custom_call", output_to_operand_aliasing={{0}: (8, {}), {1}: (9, {}), {2}: (10, {})} | custom-call | flops 412316860416 | bytes 65011712 | tf_op jit(solution)/shard_map/experts_0/pallas_call | solution.py:474
  598.8 71.5 %experts_first_grads.1 = bf16[2048,6144]{1,0:T(8,128)(2,1)} custom-call(bf16[512,2048]{1,0:T(8,128)(2,1)} %multiply_convert_fusion.n2_ref.refs_0_, bf16[512,2048]{1,0:T(8,128)(2,1)} %collective-permute-done.10.n2_ref.refs_1_, bf16[512,2048]{1,0:T(8,128)(2,1)} %collective-permute-done.14.n2_ref.refs_2_, ...), custom_call_target="tpu_custom_call" | custom-call | flops 824633720832 | bytes 41943040 | tf_op jit(solution)/shard_map/experts_first_grads/pallas_call | solution.py:585
  670.6 45.9 %experts_1.6 = (bf16[4,512,2048]{2,1,0:T(8,128)(2,1)}, bf16[4,512,2048]{2,1,0:T(8,128)(2,1)}, bf16[4,512,2048]{2,1,0:T(8,128)(2,1)}, bf16[512,2048]{1,0:T(8,128)...) custom-call(bf16[512,2048]{1,0:T(8,128)(2,1)} %collective-permute-do, ...), custom_call_target="tpu_custom_call", output_to_operand_aliasing={{0}: (10, {}), {1}: (11, {}), {2}: (12, {})} | custom-call | flops 412316860416 | bytes 65011712 | tf_op jit(solution)/shard_map/experts_1/pallas_call | solution.py:474
  720.9 41.1 %experts_1.7 = (bf16[4,512,2048]{2,1,0:T(8,128)(2,1)}, bf16[4,512,2048]{2,1,0:T(8,128)(2,1)}, bf16[4,512,2048]{2,1,0:T(8,128)(2,1)}, bf16[512,2048]{1,0:T(8,128)...) custom-call(bf16[512,2048]{1,0:T(8,128)(2,1)} %collective-permute-do, ...), custom_call_target="tpu_custom_call", output_to_operand_aliasing={{0}: (10, {}), {1}: (11, {}), {2}: (12, {})} | custom-call | flops 412316860416 | bytes 65011712 | tf_op jit(solution)/shard_map/experts_1/pallas_call | solution.py:474
  768.6 47.1 %experts_last_grads.1 = (bf16[2048,4096]{1,0:T(8,128)(2,1)}, f32[2048,128]{1,0:T(8,128)}) custom-call(bf16[512,2048]{1,0:T(8,128)(2,1)} %multiply_convert_fusion.n2_ref.refs_0_, bf16[512,2048]{1,0:T(8,128)(2,1)} %collective-permute-done.10.n2_ref.refs_1_, bf16[512,2048]{1,0:T(8,128)(2,1)} %collective-permute-done.14.n2_ref.refs_2_, ...), custom_call_target="tpu_custom_call" | custom-call | flops 549755813888 | bytes 33554432 | tf_op jit(solution)/shard_map/experts_last_grads/pallas_call | solution.py:585
  841.5 38.4 %rest_grads.1 = bf16[2048,4096]{1,0:T(8,128)(2,1)} custom-call(bf16[512,2048]{1,0:T(8,128)(2,1)} %copy-done.25, bf16[512,2048]{1,0:T(8,128)(2,1)} %collective-permute-done.6.c_ref.refs_7_.refs_1_, bf16[512,2048]{1,0:T(8,128)(2,1)} %collective-permute-done.15.c_ref.refs_8_.refs_2_, bf16[512,2048]{1,0:T(8,128)(2,1)} %collective-permute-done.17.c_ref.refs_9_.refs_3_, ...), custom_call_target="tpu_custom_call" | custom-call | flops 21474836480 | bytes 33554432 | tf_op jit(solution)/shard_map/rest_grads/pallas_call | solution.py:585
  890.0 38.6 %attend_back.1 = (bf16[4,2,256,512]{3,2,1,0:T(8,128)(2,1)}, bf16[4,2,256,512]{3,2,1,0:T(8,128)(2,1)}, bf16[4,2,256,512]{3,2,1,0:T(8,128)(2,1)}, f32[8,128]{1,0:T(8,128)}) custom-call(bf16[4,2,256,512]{3,2,1,0:T(8,128)(2,1)} %get-tuple-element.156.q_ref.refs_0_, bf16[4,2,256,512]{3,2,1,0:T(8,128)(2,1)} %get-tuple-element.157.k_ref.refs_1_, ...), custom_call_target="tpu_custom_call" | custom-call | flops 171798691840 | bytes 25165824 | tf_op jit(solution)/shard_map/attend_back/pallas_call | solution.py:275
  938.4 23.9 %qkv_grads.1 = (bf16[2048,1536]{1,0:T(8,128)(2,1)}, f32[2048,128]{1,0:T(8,128)}) custom-call(bf16[512,2048]{1,0:T(8,128)(2,1)} %multiply_convert_fusion.1.x_ref.refs_0_, bf16[512,2048]{1,0:T(8,128)(2,1)} %collective-permute-done.3.x_ref.refs_1_, bf16[512,2048]{1,0:T(8,128)(2,1)} %copy-done.21, bf16[512,2048]{1,0:T(8,128)(2,1)} %collective-permute-done.5.x_ref.refs_3_, ...), custom_call_target="tpu_custom_call" | custom-call | flops 12884901888 | bytes 23068672 | tf_op jit(solution)/shard_map/qkv_grads/pallas_call | solution.py:585
  996.3 31.1 %collective-permute-done.27 = bf16[512,2048]{1,0:T(8,128)(2,1)} collective-permute-done((bf16[512,2048]{1,0:T(8,128)(2,1)}, bf16[512,2048]{1,0:T(8,128)(2,1)}, u32[]{:S(2)}, u32[]{:S(2)}) %collective-permute-start.27) | collective-permute-done | bytes 2097184 | tf_op jit(solution)/shard_map/ppermute | solution.py:65
  1045.3 32.1 %collective-permute-done.33 = f32[290,128]{1,0:T(8,128)S(1)} collective-permute-done((f32[290,128]{1,0:T(8,128)S(1)}, f32[290,128]{1,0:T(8,128)S(1)}, u32[]{:S(2)}, u32[]{:S(2)}) %collective-permute-start.33) | collective-permute-done | bytes 148512 | tf_op jit(solution)/shard_map/ppermute | solution.py:793
  1098.7 15.9 %collective-permute-done.30 = bf16[256,512]{1,0:T(8,128)(2,1)S(1)} collective-permute-done((bf16[256,512]{1,0:T(8,128)(2,1)S(1)}, bf16[256,512]{1,0:T(8,128)(2,1)S(1)}, u32[]{:S(2)}, u32[]{:S(2)}) %collective-permute-start.30) | collective-permute-done | bytes 262176 | tf_op jit(solution)/shard_map/ppermute | solution.py:65
  1152.3 15.3 %collective-permute-done.32 = bf16[512,2048]{1,0:T(8,128)(2,1)} collective-permute-done((bf16[512,2048]{1,0:T(8,128)(2,1)}, bf16[512,2048]{1,0:T(8,128)(2,1)}, u32[]{:S(2)}, u32[]{:S(2)}) %collective-permute-start.32) | collective-permute-done | bytes 2097184 | tf_op jit(solution)/shard_map/ppermute | solution.py:65
  (304 shorter events, 369.5 us)
Async XLA Ops:
  7.2 84.4 %all-gather.6.cloned.1.call-start = ((), (), s32[]{:S(2)}) async-start(), calls=%async_computation.4 | async-start | bytes 7667712 | tf_op jit(solution)/shard_map/all_gather | solution.py:635
  10.3 249.6 %all-gather.12.cloned.1.call-start = ((), (), s32[]{:S(2)}) async-start(), calls=%async_computation.11 | async-start | bytes 9437184 | tf_op jit(solution)/shard_map/all_gather | solution.py:654
  39.5 280.1 %all-gather.8.cloned.1.call-start = ((), (), s32[]{:S(2)}) async-start(), calls=%async_computation.5 | async-start | bytes 28311552 | tf_op jit(solution)/shard_map/all_gather | solution.py:654
  39.6 52.0 %collective-permute-start.3 = (bf16[512,2048]{1,0:T(8,128)(2,1)S(1)}, bf16[512,2048]{1,0:T(8,128)(2,1)}, u32[]{:S(2)}, u32[]{:S(2)}) collective-permute-start(bf16[512,2048]{1,0:T(8,128)(2,1)S(1)} %copy-done.11), channel_id=1, source_target_pairs={{0,1},{1,2},{2,3},{3,0},{4,5},{5,6},{6,7},{7,4},{8,9},{9,10},{10,1... | collective-permute-start | bytes 6291464 | tf_op jit(solution)/shard_map/ppermute | solution.py:65
  91.6 315.4 %all-gather.10.cloned.1.call-start = ((), (), s32[]{:S(2)}) async-start(), calls=%async_computation.6 | async-start | bytes 28311552 | tf_op jit(solution)/shard_map/all_gather | solution.py:654
  91.7 48.7 %collective-permute-start.4 = (bf16[512,2048]{1,0:T(8,128)(2,1)}, bf16[512,2048]{1,0:T(8,128)(2,1)S(1)}, u32[]{:S(2)}, u32[]{:S(2)}) collective-permute-start(bf16[512,2048]{1,0:T(8,128)(2,1)} %collective-permute-done.3.x_ref.refs_1_), channel_id=1, source_target_pairs={{0,1},{1,2},{2,3},{3,0},{4,5},{5,6},{6,7},{7,4},{8,9},{9,10},{10,1... | collective-permute-start | bytes 6291464 | tf_op jit(solution)/shard_map/ppermute | solution.py:65
  140.4 59.8 %collective-permute-start.5 = (bf16[512,2048]{1,0:T(8,128)(2,1)S(1)}, bf16[512,2048]{1,0:T(8,128)(2,1)}, u32[]{:S(2)}, u32[]{:S(2)}) collective-permute-start(bf16[512,2048]{1,0:T(8,128)(2,1)S(1)} %collective-permute-done.4.x_ref.refs_2_), channel_id=1, source_target_pairs={{0,1},{1,2},{2,3},{3,0},{4,5},{5,6},{6,7},{7,4},{8,9},{9,10},{10,1... | collective-permute-start | bytes 6291464 | tf_op jit(solution)/shard_map/ppermute | solution.py:65
  200.1 49.7 %collective-permute-start.6 = (bf16[512,2048]{1,0:T(8,128)(2,1)S(1)}, bf16[512,2048]{1,0:T(8,128)(2,1)}, u32[]{:S(2)}, u32[]{:S(2)}) collective-permute-start(bf16[512,2048]{1,0:T(8,128)(2,1)S(1)} %bitcast_select_fusion.c_ref.refs_6_.refs_0_), channel_id=1, source_target_pairs={{0,1},{1,2},{2,3},{3,0},{4,5},{5,6},{6,7},{7,4},{8,9},{9,10},{10,1... | collective-permute-start | bytes 6291464 | tf_op jit(solution)/shard_map/ppermute | solution.py:65
  256.1 578.3 %reduce-scatter.5.cloned.1.call-start = ((), (), s32[]{:S(2)}) async-start(), calls=%async_computation.7 | async-start | bytes 28311552 | tf_op jit(solution)/shard_map/reduce_scatter | solution.py:741
  307.1 57.6 %collective-permute-start.10 = (bf16[512,2048]{1,0:T(8,128)(2,1)}, bf16[512,2048]{1,0:T(8,128)(2,1)}, u32[]{:S(2)}, u32[]{:S(2)}) collective-permute-start(bf16[512,2048]{1,0:T(8,128)(2,1)} %multiply_convert_fusion.n2_ref.refs_0_), channel_id=1, source_target_pairs={{0,1},{1,2},{2,3},{3,0},{4,5},{5,6},{6,7},{7,4},{8,9},{9,10},{10,1... | collective-permute-start | bytes 6291464 | tf_op jit(solution)/shard_map/ppermute | solution.py:65
  364.7 93.5 %collective-permute-start.14 = (bf16[512,2048]{1,0:T(8,128)(2,1)}, bf16[512,2048]{1,0:T(8,128)(2,1)}, u32[]{:S(2)}, u32[]{:S(2)}) collective-permute-start(bf16[512,2048]{1,0:T(8,128)(2,1)} %collective-permute-done.10.n2_ref.refs_1_), channel_id=1, source_target_pairs={{0,1},{1,2},{2,3},{3,0},{4,5},{5,6},{6,7},{7,4},{8,9},{9,10},{10,1... | collective-permute-start | bytes 6291464 | tf_op jit(solution)/shard_map/ppermute | solution.py:65
  367.2 91.0 %collective-permute-start.15 = (bf16[512,2048]{1,0:T(8,128)(2,1)}, bf16[512,2048]{1,0:T(8,128)(2,1)}, u32[]{:S(2)}, u32[]{:S(2)}) collective-permute-start(bf16[512,2048]{1,0:T(8,128)(2,1)} %collective-permute-done.6.c_ref.refs_7_.refs_1_), channel_id=1, source_target_pairs={{0,1},{1,2},{2,3},{3,0},{4,5},{5,6},{6,7},{7,4},{8,9},{9,10},{10,1... | collective-permute-start | bytes 6291464 | tf_op jit(solution)/shard_map/ppermute | solution.py:65
  458.2 81.0 %collective-permute-start.16 = (bf16[512,2048]{1,0:T(8,128)(2,1)}, bf16[512,2048]{1,0:T(8,128)(2,1)}, u32[]{:S(2)}, u32[]{:S(2)}) collective-permute-start(bf16[512,2048]{1,0:T(8,128)(2,1)} %collective-permute-done.14.n2_ref.refs_2_), channel_id=1, source_target_pairs={{0,1},{1,2},{2,3},{3,0},{4,5},{5,6},{6,7},{7,4},{8,9},{9,10},{10,1... | collective-permute-start | bytes 6291464 | tf_op jit(solution)/shard_map/ppermute | solution.py:65
  458.9 94.9 %collective-permute-start.17 = (bf16[512,2048]{1,0:T(8,128)(2,1)}, bf16[512,2048]{1,0:T(8,128)(2,1)}, u32[]{:S(2)}, u32[]{:S(2)}) collective-permute-start(bf16[512,2048]{1,0:T(8,128)(2,1)} %collective-permute-done.15.c_ref.refs_8_.refs_2_), channel_id=1, source_target_pairs={{0,1},{1,2},{2,3},{3,0},{4,5},{5,6},{6,7},{7,4},{8,9},{9,10},{10,1... | collective-permute-start | bytes 6291464 | tf_op jit(solution)/shard_map/ppermute | solution.py:65
  538.9 59.9 %collective-permute-start.19 = (bf16[512,2048]{1,0:T(8,128)(2,1)}, bf16[512,2048]{1,0:T(8,128)(2,1)}, u32[]{:S(2)}, u32[]{:S(2)}) collective-permute-start(bf16[512,2048]{1,0:T(8,128)(2,1)} %get-tuple-element.190), channel_id=1, source_target_pairs={{0,1},{1,2},{2,3},{3,0},{4,5},{5,6},{6,7},{7,4},{8,9},{9,10},{10,1... | collective-permute-start | bytes 6291464 | tf_op jit(solution)/shard_map/ppermute | solution.py:65
  593.0 77.5 %collective-permute-start.18 = (bf16[512,2048]{1,0:T(8,128)(2,1)}, bf16[512,2048]{1,0:T(8,128)(2,1)}, u32[]{:S(2)}, u32[]{:S(2)}) collective-permute-start(bf16[512,2048]{1,0:T(8,128)(2,1)} %get-tuple-element.197), channel_id=1, source_target_pairs={{0,1},{1,2},{2,3},{3,0},{4,5},{5,6},{6,7},{7,4},{8,9},{9,10},{10,1... | collective-permute-start | bytes 6291464 | tf_op jit(solution)/shard_map/ppermute | solution.py:65
  670.3 300.7 %reduce-scatter.9.cloned.1.call-start = ((), (), s32[]{:S(2)}) async-start(), calls=%async_computation.9 | async-start | bytes 18874368 | tf_op jit(solution)/shard_map/reduce_scatter | solution.py:761
  768.1 47.5 %collective-permute-start.21 = (bf16[512,2048]{1,0:T(8,128)(2,1)}, bf16[512,2048]{1,0:T(8,128)(2,1)}, u32[]{:S(2)}, u32[]{:S(2)}) collective-permute-start(bf16[512,2048]{1,0:T(8,128)(2,1)} %add_convert_fusion.5), channel_id=1, source_target_pairs={{0,1},{1,2},{2,3},{3,0},{4,5},{5,6},{6,7},{7,4},{8,9},{9,10},{10,1... | collective-permute-start | bytes 6291464 | tf_op jit(solution)/shard_map/ppermute | solution.py:65
  834.4 252.1 %reduce-scatter.7.cloned.1.call-start = ((), (), s32[]{:S(2)}) async-start(), calls=%async_computation.8 | async-start | bytes 18874368 | tf_op jit(solution)/shard_map/reduce_scatter | solution.py:778
  837.1 46.7 %collective-permute-start.24 = (bf16[512,512]{1,0:T(8,128)(2,1)}, bf16[512,512]{1,0:T(8,128)(2,1)}, u32[]{:S(2)}, u32[]{:S(2)}) collective-permute-start(bf16[512,512]{1,0:T(8,128)(2,1)} %get-tuple-element.336), channel_id=1, source_target_pairs={{0,3},{1,0},{2,1},{3,2},{4,7},{5,4},{6,5},{7,6},{8,11},{9,8},{10,9... | collective-permute-start | bytes 1572872 | tf_op jit(solution)/shard_map/ppermute | solution.py:65
  886.8 249.5 %reduce-scatter.11.cloned.1.call-start = ((), (), s32[]{:S(2)}) async-start(), calls=%async_computation.10 | async-start | bytes 7077888 | tf_op jit(solution)/shard_map/reduce_scatter | solution.py:784
  936.1 43.6 %collective-permute-start.26 = (bf16[512,2048]{1,0:T(8,128)(2,1)}, bf16[512,2048]{1,0:T(8,128)(2,1)S(1)}, u32[]{:S(2)}, u32[]{:S(2)}) collective-permute-start(bf16[512,2048]{1,0:T(8,128)(2,1)} %input_back.4), channel_id=1, source_target_pairs={{0,1},{1,2},{2,3},{3,0},{4,5},{5,6},{6,7},{7,4},{8,9},{9,10},{10,1... | collective-permute-start | bytes 6291464 | tf_op jit(solution)/shard_map/ppermute | solution.py:65
  1032.2 57.5 %collective-permute-start.28 = (bf16[512,2048]{1,0:T(8,128)(2,1)}, bf16[512,2048]{1,0:T(8,128)(2,1)}, u32[]{:S(2)}, u32[]{:S(2)}) collective-permute-start(bf16[512,2048]{1,0:T(8,128)(2,1)} %add_convert_fusion.2), channel_id=1, source_target_pairs={{0,1},{1,2},{2,3},{3,0},{4,5},{5,6},{6,7},{7,4},{8,9},{9,10},{10,1... | collective-permute-start | bytes 6291464 | tf_op jit(solution)/shard_map/ppermute | solution.py:65
  1118.6 49.1 %collective-permute-start.32 = (bf16[512,2048]{1,0:T(8,128)(2,1)}, bf16[512,2048]{1,0:T(8,128)(2,1)}, u32[]{:S(2)}, u32[]{:S(2)}) collective-permute-start(bf16[512,2048]{1,0:T(8,128)(2,1)} %add_convert_fusion.1), channel_id=1, source_target_pairs={{0,1},{1,2},{2,3},{3,0},{4,5},{5,6},{6,7},{7,4},{8,9},{9,10},{10,1... | collective-permute-start | bytes 6291464 | tf_op jit(solution)/shard_map/ppermute | solution.py:65
  (79 other events, 1299.4 us)
Sparse Core Ops, SparseCore 0:
  10.4 50.4 all-gather.5
  62.8 54.3 all-gather.11
  119.7 125.3 all-gather.7
  256.2 124.8 all-gather.9
  670.4 154.6 reduce-scatter.4
  834.5 116.9 reduce-scatter.8
  955.0 115.9 reduce-scatter.6
  1074.4 61.7 reduce-scatter.10

commit v4 on v3

--- a/solution.py
+++ b/solution.py
@@ -205,10 +205,10 @@
 
 
 def attend_back_kernel(scale, *refs):
-    q_ref, k_ref, v_ref, o_ref, do_ref, lse_ref, valid_ref = refs[:7]
-    qr_ref, kr_ref, cos_ref, sin_ref, gq_ref, gk_ref = refs[7:13]
-    dq_ref, dk_ref, dv_ref, gains_ref = refs[13:17]
-    dk_acc, dv_acc = refs[17:]
+    q_ref, k_ref, v_ref, o_ref, lse_ref, valid_ref = refs[:6]
+    qr_ref, kr_ref, cos_ref, sin_ref, gq_ref, gk_ref = refs[6:12]
+    do_refs = refs[12:-6]
+    dq_ref, dk_ref, dv_ref, gains_ref, dk_acc, dv_acc = refs[-6:]
     count, _, rows, width = q_ref.shape
     length = count * rows
     first = jnp.logical_and(pl.program_id(0) == 0, pl.program_id(1) == 0)
@@ -237,7 +237,7 @@
     gain_k = jnp.zeros((1, width), F32)
     for i in range(count):
         query = q_ref[i, 0]
-        grad = do_ref[i, 0]
+        grad = do_refs[i][0]
         scores = dot_nt(keys, query) * scale
         weights = jnp.exp(jnp.where(valid, scores, NEG_FILL) - lse_ref[0, i : i + 1, :])
         delta = jnp.sum(
@@ -280,7 +280,6 @@
             head,
             head,
             head,
-            head,
             pl.BlockSpec((1, count, rows), lambda s, h: (s * heads + h, 0, 0)),
             pl.BlockSpec((1, count * rows, LANES), lambda s, h: (s, 0, 0)),
             head,
@@ -289,7 +288,8 @@
             const(count, rows, LANES),
             const(1, LANES),
             const(1, LANES),
-        ],
+        ]
+        + [pl.BlockSpec((1, rows, LANES), lambda s, h: (s, 0, h))] * count,
         out_specs=[head, head, head, const(8, LANES)],
         out_shape=[struct(q.shape, BF)] * 3 + [struct((8, LANES), F32)],
         scratch_shapes=[pltpu.VMEM((count * rows, LANES), F32)] * 2,
@@ -300,7 +300,7 @@
             seqs * heads * (count * rows) ** 2,
         ),
         name="attend_back",
-    )(q, k, v, o, do, lse, valid, q_raw, k_raw, cos, sin, gain_q, gain_k)
+    )(q, k, v, o, lse, valid, q_raw, k_raw, cos, sin, gain_q, gain_k, *do)
 
 
 def input_back_kernel(dq_ref, dk_ref, dv_ref, wq_ref, wk_ref, wv_ref, out_ref):
@@ -504,7 +504,7 @@
     )(n2, cot, keep, weights_all, weights_all, weights, weights, grad, *sums, *aliased)
 
 
-def row_grad_kernel(count, plan, router, gain, *refs):
+def row_grad_kernel(count, plan, router, gain, shared, *refs):
     ins = list(refs)
     lefts, rights = [], []
     for parts, tiles in plan:
@@ -512,6 +512,8 @@
         rights.append([ins.pop(0) for _ in tiles])
     dls = [ins.pop(0) for _ in range(count)] if router else []
     weight_ref = ins.pop(0) if gain else None
+    if shared:
+        ins.pop(0)
     out_ref, extra_ref, turned = ins.pop(0), ins.pop(0) if router or gain else None, ins.pop(0)
     i = pl.program_id(0)
     start = 0
@@ -546,7 +548,7 @@
             start += steps
 
 
-def row_grads(pairs, tile, name, dls=(), weights=None):
+def row_grads(pairs, tile, name, dls=(), weights=None, total=None, base=None):
     plan, args, specs, start, macs = [], [], [], 0, 0
     depth = pairs[0][0][0].shape[1]
     most = max(sum(part.shape[0] for part in left) for left, _ in pairs)
@@ -571,24 +573,37 @@
             start += steps
             macs += len(left) * left[0].shape[0] * depth * steps * tile
         plan.append((len(left), tuple(tiles)))
-    out_specs = [pl.BlockSpec((depth, tile), lambda i: (0, i))]
-    out_shape = [struct((depth, start * tile), BF)]
+    wide = base.shape[1] if base is not None else total or start * tile
+    skip = wide // tile - start if base is not None else 0
+    out_specs = [pl.BlockSpec((depth, tile), lambda i: (0, i + skip))]
+    out_shape = [struct((depth, wide), BF)]
     if dls:
         args += dls
         specs += [pl.BlockSpec(d.shape, lambda i: (0, 0)) for d in dls]
     if weights is not None:
         args.append(weights)
         specs.append(pl.BlockSpec((depth, tile), lambda i: (0, i)))
+    if base is not None:
+        args.append(base)
+        specs.append(pl.BlockSpec(memory_space=pl.ANY))
     if dls or weights is not None:
         out_specs.append(pl.BlockSpec((depth, LANES), lambda i: (0, 0)))
         out_shape.append(struct((depth, LANES), F32))
     return pl.pallas_call(
-        functools.partial(row_grad_kernel, len(dls), tuple(plan), bool(dls), weights is not None),
+        functools.partial(
+            row_grad_kernel,
+            len(dls),
+            tuple(plan),
+            bool(dls),
+            weights is not None,
+            base is not None,
+        ),
         grid=(start,),
         in_specs=specs,
         out_specs=out_specs,
         out_shape=out_shape,
         scratch_shapes=[pltpu.VMEM((depth, most), BF)],
+        input_output_aliases={} if base is None else {len(args) - 1: 0},
         compiler_params=params(1),
         cost_estimate=cost(macs if 'experts' in name else macs // 16, 2 * depth * start * tile + 4 * most * depth),
         name=name,
@@ -761,13 +776,14 @@
     last_own = lax.psum_scatter(after(last_full, dob), "fsdp", scatter_dimension=0, tiled=True)
     dob = after(dob, first_own)
     dob_parts = exchange(dob, 1)
+    y_sum = plus(after(y_run, dob), ys[2]).astype(BF)
     rest_full = row_grads(
-        [(cots, [hp]), ([after(db, dob)], ob_parts)], ff, "rest_grads"
+        [(cots, [hp]), ([after(db, dob)], ob_parts)],
+        ff, "rest_grads",
     )[0]
-    d_ob = jnp.stack(dob_parts).reshape(count, seqs, per, local)
-    y_sum = plus(after(y_run, dob), ys[2]).astype(BF)
-    d_ob = after(d_ob, rest_full, y_sum)
-    y_run = shift(after(y_sum, d_ob), count, 1)
+    d_ob = [after(part.reshape(seqs, per, local), rest_full, y_sum) for part in dob_parts]
+    rest_own = lax.psum_scatter(after(rest_full, *d_ob), "fsdp", scatter_dimension=0, tiled=True)
+    y_run = shift(after(y_sum, *d_ob), count, 1)
     for k in range(3, count - 1):
         y_run = shift(plus(y_run, ys[k]).astype(BF), count, 1)
 
@@ -775,13 +791,13 @@
         q, k_low, v, ob, d_ob, lse, key_valid, q_raw, k_raw, cos, sin, gain_q, gain_k, scale
     )
     part = input_back(1, after(dq, y_run), dk, dv, weights_all)
-    rest_own = lax.psum_scatter(after(rest_full, d_ob), "fsdp", scatter_dimension=0, tiled=True)
     dn1_run = shift(part, count, 1)
-    qkv_full, attn_gain_wide = row_grads(
+    attn_full, attn_gain_wide = row_grads(
         [([after(n1[0], part)] + n1[1:], [a.reshape(count * rows, local) for a in (dq, dk, dv)])],
         min(256, local), "qkv_grads", weights=weights_all,
     )
-    qkv_own = lax.psum_scatter(qkv_full, "fsdp", scatter_dimension=0, tiled=True)
+
+    attn_own = lax.psum_scatter(attn_full, "fsdp", scatter_dimension=0, tiled=True)
 
     attn_gain_term = jnp.sum(attn_gain_wide, axis=1) / attn_gain
     packed = jnp.concatenate(
@@ -794,28 +810,28 @@
         value, axis, [(i, i ^ bit) for i in range(lax.axis_size(axis))]
     )
 
-    part = input_back(2, after(dq, qkv_full), dk, dv, weights_all)
+    part = input_back(2, after(dq, attn_full), dk, dv, weights_all)
     dn1_run = after(dn1_run, last_own)
     for k in range(2, count):
         dn1_run = plus(dn1_run, part).astype(BF)
-        if k - 2 < len(bits):
-            packed = across(after(packed, dn1_run), "tp", bits[k - 2])
+        if k == 2:
+            packed = after(packed, dn1_run)
+            for b in range(lax.axis_size("fsdp").bit_length() - 1):
+                packed = across(packed, "fsdp", 1 << b)
+        elif bits:
+            packed = across(after(packed, dn1_run), "tp", bits.pop())
         dn1_run = shift(dn1_run, count, 1)
         part = input_back((k + 1) % count, dq, dk, dv, weights_all)
+    packed = after(packed, dn1_run)
+    while bits:
+        packed = across(packed, "tp", bits.pop())
     dn1 = plus(dn1_run, part)
-    for bit in bits[max(count - 2, 0) :]:
-        packed = across(packed, "tp", bit)
-    qkv_sum = qkv_own.astype(F32)
+    y_run = shift(plus(after(y_run, dn1_run, rest_own), ys[count - 1]).astype(BF), count, 1)
+    qkv_sum = attn_own.astype(F32)
     out_own = rest_own[:, each * ff :]
-    out_own = after(out_own, dn1_run)
     out_pieces = [out_own[:, s * local : (s + 1) * local] for s in range(count)]
     out_pieces = exchange(out_pieces, 1)
     out_weight_grad = jnp.transpose(plus(*out_pieces))
-    y_run = plus(after(y_run, *out_pieces[1:]), ys[count - 1]).astype(BF)
-    y_run = shift(y_run, count, 1)
-
-    for b in range(lax.axis_size("fsdp").bit_length() - 1):
-        packed = across(after(packed, part, *out_pieces[1:]) if b == 0 else packed, "fsdp", 1 << b)
 
     def expert_out(owns, axes):
         shaped = [own.reshape(own.shape[0], each, ff) for own in owns]

time: 1190 us -> 1180 us (level)
    reduce_scatter x2, waiting for transfers between devices: 7.12 us -> 36.3 us  [the longest x1 36.2 us: per_device(): lax.psum_scatter(attn_full, 'fsdp', scatter_dimension=0, tiled=True)]
    ppermute x33, waiting for transfers between devices: 266 us -> 244 us  [shift(): lax.ppermute(value, 'tp', [(i, (i + step) % count) for i in range(count)])]
    ppermute x5, waiting for transfers between devices: 36.1 us -> 18.7 us  [per_device(): lax.ppermute(value, axis, [(i, i ^ bit) for i in range(lax.axis_size(axis...]
  transfers between devices with their start and end apart: 46 -> 46, of which waited for: 24 -> 21; matrix products, arithmetic and copies ran while one was open for 10% -> 10% of each run, Pallas kernels for 55% -> 56%
where the time goes in v4:
time: 1180 us; the launch traced here: 1170 us
  Pallas kernels  654 us (55%)
  waiting for transfers between devices  300 us (25%)
  other arithmetic  78.9 us (7%)
  starting transfers between devices  66.2 us (6%)
  local copies, waits for them, and re-layouts  56.8 us (5%)
  between operations  15.1 us (1%)
    pallas_call x8, Pallas kernels, experts_pass(): pl.pallas_call(functools.partial(expert_kernel, group, experts), grid=(ex...  325 us
    ppermute x33, waiting for transfers between devices, shift(): lax.ppermute(value, 'tp', [(i, (i + step) % count) for i in range(count)])  244 us
    pallas_call x4, Pallas kernels, row_grads(): pl.pallas_call(functools.partial(row_grad_kernel, len(dls), tuple(plan),...  181 us
    ppermute x33, starting transfers between devices, shift(): lax.ppermute(value, 'tp', [(i, (i + step) % count) for i in range(count)])  60.3 us
    pallas_call x1, Pallas kernels, attend_back(): pl.pallas_call(functools.partial(attend_back_kernel, scale), grid=(seqs,...  38.6 us
    reduce_scatter x1, waiting for transfers between devices, per_device(): lax.psum_scatter(attn_full, 'fsdp', scatter_dimension=0, tiled=True)  36.2 us
    pallas_call x4, Pallas kernels, project(): pl.pallas_call(functools.partial(qkv_kernel, seqs), grid=(groups,), in_sp...  35.8 us
    pallas_call x4, Pallas kernels, input_back(): pl.pallas_call(input_back_kernel, grid=(depth // tile,), in_specs=[grad]...  31.7 us
  transfers between devices with their start and end apart: 46, of which 21 were waited for; matrix products, arithmetic and copies ran while one was open for 10% of the time, Pallas kernels for 56%

profile of v4, /device:TPU:0, one launch (start us, length us, event | category | flops | bytes accessed | tf_op | source)
XLA Modules:
  0.0 1170.4 jit_solution(17898166182567226809)
XLA Ops:
  61.9 31.5 %collective-permute-done.3.x_ref.refs_1_ = bf16[512,2048]{1,0:T(8,128)(2,1)} collective-permute-done((bf16[512,2048]{1,0:T(8,128)(2,1)}, bf16[512,2048]{1,0:T(8,128)(2,1)}, u32[]{:S(2)}, u32[]{:S(2)}) %collective-permute-start.3) | collective-permute-done | bytes 2097184 | tf_op jit(solution)/shard_map/ppermute | solution.py:65
  120.3 22.0 %collective-permute-done.4.x_ref.refs_2_ = bf16[512,2048]{1,0:T(8,128)(2,1)S(1)} collective-permute-done((bf16[512,2048]{1,0:T(8,128)(2,1)}, bf16[512,2048]{1,0:T(8,128)(2,1)S(1)}, u32[]{:S(2)}, u32[]{:S(2)}) %collective-permute-start.4) | collective-permute-done | bytes 2097184 | tf_op jit(solution)/shard_map/ppermute | solution.py:65
  151.2 36.7 %collective-permute-done.13 = s32[16,512]{1,0:T(8,128)S(1)} collective-permute-done((s32[16,512]{1,0:T(8,128)S(1)}, s32[16,512]{1,0:T(8,128)S(1)}, u32[]{:S(2)}, u32[]{:S(2)}) %collective-permute-start.13) | collective-permute-done | bytes 32800 | tf_op jit(solution)/shard_map/ppermute | solution.py:65
  212.6 18.3 %attend.1 = (bf16[4,2,256,512]{3,2,1,0:T(8,128)(2,1)}, f32[8,4,256]{2,1,0:T(4,128)}) custom-call(bf16[4,2,256,512]{3,2,1,0:T(8,128)(2,1)} %get-tuple-element.158.q_ref.refs_0_, bf16[4,2,256,512]{3,2,1,0:T(8,128)(2,1)} %get-tuple-element.159.k_ref.refs_1_, bf16[4,2,256,512]{3,2,1,0:T(8,128)(2,1)} %get-tuple-element.160.v_ref.refs_2_, ...), custom_call_target="tpu_custom_call" | custom-call | flops 68719476736 | bytes 8388608 | tf_op jit(solution)/shard_map/attend/pallas_call | solution.py:191
  230.9 20.6 %collective-permute-done.6.c_ref.refs_7_.refs_1_ = bf16[512,2048]{1,0:T(8,128)(2,1)} collective-permute-done((bf16[512,2048]{1,0:T(8,128)(2,1)S(1)}, bf16[512,2048]{1,0:T(8,128)(2,1)}, u32[]{:S(2)}, u32[]{:S(2)}) %collective-permute-start.6) | collective-permute-done | bytes 2097184 | tf_op jit(solution)/shard_map/ppermute | solution.py:65
  270.6 20.7 %collective-permute-done.8.refs_2_.refs_8_ = bf16[512,512]{1,0:T(8,128)(2,1)S(1)} collective-permute-done((bf16[512,512]{1,0:T(8,128)(2,1)S(1)}, bf16[512,512]{1,0:T(8,128)(2,1)S(1)}, u32[]{:S(2)}, u32[]{:S(2)}) %collective-permute-start.8) | collective-permute-done | bytes 524320 | tf_op jit(solution)/shard_map/ppermute | solution.py:65
  308.7 12.5 %collective-permute-start.10 = (bf16[512,2048]{1,0:T(8,128)(2,1)}, bf16[512,2048]{1,0:T(8,128)(2,1)}, u32[]{:S(2)}, u32[]{:S(2)}) collective-permute-start(bf16[512,2048]{1,0:T(8,128)(2,1)} %multiply_convert_fusion.n2_ref.refs_0_), channel_id=1, source_target_pairs={{0,1},{1,2},{2,3},{3,0},{4,5},{5,6},{6,7},{7,4},{8,9},{9,10},{10,1... | collective-permute-start | bytes 6291464 | tf_op jit(solution)/shard_map/ppermute | solution.py:65
  321.8 39.9 %experts_0.4 = (bf16[4,512,2048]{2,1,0:T(8,128)(2,1)}, bf16[4,512,2048]{2,1,0:T(8,128)(2,1)}, bf16[4,512,2048]{2,1,0:T(8,128)(2,1)}, bf16[512,2048]{1,0:T(8,128)...) custom-call(bf16[512,2048]{1,0:T(8,128)(2,1)} %multiply_convert_fusion.n2_ref.refs_0_, ...), custom_call_target="tpu_custom_call" | custom-call | flops 412316860416 | bytes 65011712 | tf_op jit(solution)/shard_map/experts_0/pallas_call | solution.py:474
  369.3 39.3 %experts_0.5 = (bf16[4,512,2048]{2,1,0:T(8,128)(2,1)}, bf16[4,512,2048]{2,1,0:T(8,128)(2,1)}, bf16[4,512,2048]{2,1,0:T(8,128)(2,1)}, bf16[512,2048]{1,0:T(8,128)...) custom-call(bf16[512,2048]{1,0:T(8,128)(2,1)} %collective-permute-do, ...), custom_call_target="tpu_custom_call", output_to_operand_aliasing={{0}: (8, {}), {1}: (9, {}), {2}: (10, {})} | custom-call | flops 412316860416 | bytes 65011712 | tf_op jit(solution)/shard_map/experts_0/pallas_call | solution.py:474
  408.6 40.0 %experts_1.4 = (bf16[4,512,2048]{2,1,0:T(8,128)(2,1)}, bf16[4,512,2048]{2,1,0:T(8,128)(2,1)}, bf16[4,512,2048]{2,1,0:T(8,128)(2,1)}, bf16[512,2048]{1,0:T(8,128)...) custom-call(bf16[512,2048]{1,0:T(8,128)(2,1)} %multiply_convert_fusion.n2_ref.refs_0_, ...), custom_call_target="tpu_custom_call" | custom-call | flops 412316860416 | bytes 65011712 | tf_op jit(solution)/shard_map/experts_1/pallas_call | solution.py:474
  461.3 39.1 %experts_0.6 = (bf16[4,512,2048]{2,1,0:T(8,128)(2,1)}, bf16[4,512,2048]{2,1,0:T(8,128)(2,1)}, bf16[4,512,2048]{2,1,0:T(8,128)(2,1)}, bf16[512,2048]{1,0:T(8,128)...) custom-call(bf16[512,2048]{1,0:T(8,128)(2,1)} %collective-permute-do, ...), custom_call_target="tpu_custom_call", output_to_operand_aliasing={{0}: (8, {}), {1}: (9, {}), {2}: (10, {})} | custom-call | flops 412316860416 | bytes 65011712 | tf_op jit(solution)/shard_map/experts_0/pallas_call | solution.py:474
  500.4 40.1 %experts_1.5 = (bf16[4,512,2048]{2,1,0:T(8,128)(2,1)}, bf16[4,512,2048]{2,1,0:T(8,128)(2,1)}, bf16[4,512,2048]{2,1,0:T(8,128)(2,1)}, bf16[512,2048]{1,0:T(8,128)...) custom-call(bf16[512,2048]{1,0:T(8,128)(2,1)} %collective-permute-do, ...), custom_call_target="tpu_custom_call", output_to_operand_aliasing={{0}: (10, {}), {1}: (11, {}), {2}: (12, {})} | custom-call | flops 412316860416 | bytes 65011712 | tf_op jit(solution)/shard_map/experts_1/pallas_call | solution.py:474
  540.8 14.5 %collective-permute-done.17.c_ref.refs_9_.refs_3_ = bf16[512,2048]{1,0:T(8,128)(2,1)} collective-permute-done((bf16[512,2048]{1,0:T(8,128)(2,1)}, bf16[512,2048]{1,0:T(8,128)(2,1)}, u32[]{:S(2)}, u32[]{:S(2)}) %collective-permute-start.17) | collective-permute-done | bytes 2097184 | tf_op jit(solution)/shard_map/ppermute | solution.py:65
  555.4 39.2 %experts_0.7 = (bf16[4,512,2048]{2,1,0:T(8,128)(2,1)}, bf16[4,512,2048]{2,1,0:T(8,128)(2,1)}, bf16[4,512,2048]{2,1,0:T(8,128)(2,1)}, bf16[512,2048]{1,0:T(8,128)...) custom-call(bf16[512,2048]{1,0:T(8,128)(2,1)} %collective-permute-do, ...), custom_call_target="tpu_custom_call", output_to_operand_aliasing={{0}: (8, {}), {1}: (9, {}), {2}: (10, {})} | custom-call | flops 412316860416 | bytes 65011712 | tf_op jit(solution)/shard_map/experts_0/pallas_call | solution.py:474
  600.3 71.6 %experts_first_grads.1 = bf16[2048,6144]{1,0:T(8,128)(2,1)} custom-call(bf16[512,2048]{1,0:T(8,128)(2,1)} %multiply_convert_fusion.n2_ref.refs_0_, bf16[512,2048]{1,0:T(8,128)(2,1)} %collective-permute-done.10.n2_ref.refs_1_, bf16[512,2048]{1,0:T(8,128)(2,1)} %collective-permute-done.14.n2_ref.refs_2_, ...), custom_call_target="tpu_custom_call" | custom-call | flops 824633720832 | bytes 41943040 | tf_op jit(solution)/shard_map/experts_first_grads/pallas_call | solution.py:592
  672.2 45.9 %experts_1.6 = (bf16[4,512,2048]{2,1,0:T(8,128)(2,1)}, bf16[4,512,2048]{2,1,0:T(8,128)(2,1)}, bf16[4,512,2048]{2,1,0:T(8,128)(2,1)}, bf16[512,2048]{1,0:T(8,128)...) custom-call(bf16[512,2048]{1,0:T(8,128)(2,1)} %collective-permute-do, ...), custom_call_target="tpu_custom_call", output_to_operand_aliasing={{0}: (10, {}), {1}: (11, {}), {2}: (12, {})} | custom-call | flops 412316860416 | bytes 65011712 | tf_op jit(solution)/shard_map/experts_1/pallas_call | solution.py:474
  722.6 41.4 %experts_1.7 = (bf16[4,512,2048]{2,1,0:T(8,128)(2,1)}, bf16[4,512,2048]{2,1,0:T(8,128)(2,1)}, bf16[4,512,2048]{2,1,0:T(8,128)(2,1)}, bf16[512,2048]{1,0:T(8,128)...) custom-call(bf16[512,2048]{1,0:T(8,128)(2,1)} %collective-permute-do, ...), custom_call_target="tpu_custom_call", output_to_operand_aliasing={{0}: (10, {}), {1}: (11, {}), {2}: (12, {})} | custom-call | flops 412316860416 | bytes 65011712 | tf_op jit(solution)/shard_map/experts_1/pallas_call | solution.py:474
  769.8 47.0 %experts_last_grads.1 = (bf16[2048,4096]{1,0:T(8,128)(2,1)}, f32[2048,128]{1,0:T(8,128)}) custom-call(bf16[512,2048]{1,0:T(8,128)(2,1)} %multiply_convert_fusion.n2_ref.refs_0_, bf16[512,2048]{1,0:T(8,128)(2,1)} %collective-permute-done.10.n2_ref.refs_1_, bf16[512,2048]{1,0:T(8,128)(2,1)} %collective-permute-done.14.n2_ref.refs_2_, ...), custom_call_target="tpu_custom_call" | custom-call | flops 549755813888 | bytes 33554432 | tf_op jit(solution)/shard_map/experts_last_grads/pallas_call | solution.py:592
  843.4 38.4 %rest_grads.1 = bf16[2048,4096]{1,0:T(8,128)(2,1)} custom-call(bf16[512,2048]{1,0:T(8,128)(2,1)} %copy-done.14, bf16[512,2048]{1,0:T(8,128)(2,1)} %collective-permute-done.6.c_ref.refs_7_.refs_1_, bf16[512,2048]{1,0:T(8,128)(2,1)} %collective-permute-done.15.c_ref.refs_8_.refs_2_, bf16[512,2048]{1,0:T(8,128)(2,1)} %collective-permute-done.17.c_ref.refs_9_.refs_3_, ...), custom_call_target="tpu_custom_call" | custom-call | flops 21474836480 | bytes 33554432 | tf_op jit(solution)/shard_map/rest_grads/pallas_call | solution.py:592
  888.3 38.6 %attend_back.1 = (bf16[4,2,256,512]{3,2,1,0:T(8,128)(2,1)}, bf16[4,2,256,512]{3,2,1,0:T(8,128)(2,1)}, bf16[4,2,256,512]{3,2,1,0:T(8,128)(2,1)}, f32[8,128]{1,0:T(8,128)}) custom-call(bf16[4,2,256,512]{3,2,1,0:T(8,128)(2,1)} %get-tuple-element.158.q_ref.refs_0_, bf16[4,2,256,512]{3,2,1,0:T(8,128)(2,1)} %get-tuple-element.159.k_ref.refs_1_, ...), custom_call_target="tpu_custom_call" | custom-call | flops 171798691840 | bytes 25165824 | tf_op jit(solution)/shard_map/attend_back/pallas_call | solution.py:275
  936.5 23.9 %qkv_grads.1 = (bf16[2048,1536]{1,0:T(8,128)(2,1)}, f32[2048,128]{1,0:T(8,128)}) custom-call(bf16[512,2048]{1,0:T(8,128)(2,1)} %multiply_convert_fusion.1.x_ref.refs_0_, bf16[512,2048]{1,0:T(8,128)(2,1)} %collective-permute-done.3.x_ref.refs_1_, bf16[512,2048]{1,0:T(8,128)(2,1)} %copy-done.12, bf16[512,2048]{1,0:T(8,128)(2,1)} %collective-permute-done.5.x_ref.refs_3_, ...), custom_call_target="tpu_custom_call" | custom-call | flops 12884901888 | bytes 23068672 | tf_op jit(solution)/shard_map/qkv_grads/pallas_call | solution.py:592
  990.3 31.1 %collective-permute-done.27 = bf16[512,2048]{1,0:T(8,128)(2,1)} collective-permute-done((bf16[512,2048]{1,0:T(8,128)(2,1)S(1)}, bf16[512,2048]{1,0:T(8,128)(2,1)}, u32[]{:S(2)}, u32[]{:S(2)}) %collective-permute-start.27) | collective-permute-done | bytes 2097184 | tf_op jit(solution)/shard_map/ppermute | solution.py:65
  1059.5 13.2 %collective-permute-done.36 = f32[290,128]{1,0:T(8,128)S(1)} collective-permute-done((f32[290,128]{1,0:T(8,128)S(1)}, f32[290,128]{1,0:T(8,128)S(1)}, u32[]{:S(2)}, u32[]{:S(2)}) %collective-permute-start.36) | collective-permute-done | bytes 148512 | tf_op jit(solution)/shard_map/ppermute | solution.py:809
  1102.1 36.2 %reduce-scatter.11.cloned.1.call-done = bf16[256,1536]{1,0:T(8,128)(2,1)} async-done(((bf16[2048,1536]{1,0:T(8,128)(2,1)}), bf16[256,1536]{1,0:T(8,128)(2,1)}) %reduce-scatter.11.cloned.1.call-update) | async-done | bytes 786448 | tf_op jit(solution)/shard_map/reduce_scatter | solution.py:800
  (274 shorter events, 353.7 us)
Async XLA Ops:
  7.2 86.2 %all-gather.6.cloned.1.call-start = ((), (), s32[]{:S(2)}) async-start(), calls=%async_computation.4 | async-start | bytes 7667712 | tf_op jit(solution)/shard_map/all_gather | solution.py:650
  10.3 251.2 %all-gather.12.cloned.1.call-start = ((), (), s32[]{:S(2)}) async-start(), calls=%async_computation.11 | async-start | bytes 9437184 | tf_op jit(solution)/shard_map/all_gather | solution.py:669
  41.1 280.1 %all-gather.8.cloned.1.call-start = ((), (), s32[]{:S(2)}) async-start(), calls=%async_computation.5 | async-start | bytes 28311552 | tf_op jit(solution)/shard_map/all_gather | solution.py:669
  41.1 52.2 %collective-permute-start.3 = (bf16[512,2048]{1,0:T(8,128)(2,1)}, bf16[512,2048]{1,0:T(8,128)(2,1)}, u32[]{:S(2)}, u32[]{:S(2)}) collective-permute-start(bf16[512,2048]{1,0:T(8,128)(2,1)} %multiply_convert_fusion.1.x_ref.refs_0_), channel_id=1, source_target_pairs={{0,1},{1,2},{2,3},{3,0},{4,5},{5,6},{6,7},{7,4},{8,9},{9,10},{10,1... | collective-permute-start | bytes 6291464 | tf_op jit(solution)/shard_map/ppermute | solution.py:65
  93.4 315.1 %all-gather.10.cloned.1.call-start = ((), (), s32[]{:S(2)}) async-start(), calls=%async_computation.6 | async-start | bytes 28311552 | tf_op jit(solution)/shard_map/all_gather | solution.py:669
  93.5 48.8 %collective-permute-start.4 = (bf16[512,2048]{1,0:T(8,128)(2,1)}, bf16[512,2048]{1,0:T(8,128)(2,1)S(1)}, u32[]{:S(2)}, u32[]{:S(2)}) collective-permute-start(bf16[512,2048]{1,0:T(8,128)(2,1)} %collective-permute-done.3.x_ref.refs_1_), channel_id=1, source_target_pairs={{0,1},{1,2},{2,3},{3,0},{4,5},{5,6},{6,7},{7,4},{8,9},{9,10},{10,1... | collective-permute-start | bytes 6291464 | tf_op jit(solution)/shard_map/ppermute | solution.py:65
  142.3 59.5 %collective-permute-start.5 = (bf16[512,2048]{1,0:T(8,128)(2,1)S(1)}, bf16[512,2048]{1,0:T(8,128)(2,1)}, u32[]{:S(2)}, u32[]{:S(2)}) collective-permute-start(bf16[512,2048]{1,0:T(8,128)(2,1)S(1)} %collective-permute-done.4.x_ref.refs_2_), channel_id=1, source_target_pairs={{0,1},{1,2},{2,3},{3,0},{4,5},{5,6},{6,7},{7,4},{8,9},{9,10},{10,1... | collective-permute-start | bytes 6291464 | tf_op jit(solution)/shard_map/ppermute | solution.py:65
  201.7 49.7 %collective-permute-start.6 = (bf16[512,2048]{1,0:T(8,128)(2,1)S(1)}, bf16[512,2048]{1,0:T(8,128)(2,1)}, u32[]{:S(2)}, u32[]{:S(2)}) collective-permute-start(bf16[512,2048]{1,0:T(8,128)(2,1)S(1)} %bitcast_select_fusion.c_ref.refs_6_.refs_0_), channel_id=1, source_target_pairs={{0,1},{1,2},{2,3},{3,0},{4,5},{5,6},{6,7},{7,4},{8,9},{9,10},{10,1... | collective-permute-start | bytes 6291464 | tf_op jit(solution)/shard_map/ppermute | solution.py:65
  257.7 578.0 %reduce-scatter.5.cloned.1.call-start = ((), (), s32[]{:S(2)}) async-start(), calls=%async_computation.7 | async-start | bytes 28311552 | tf_op jit(solution)/shard_map/reduce_scatter | solution.py:756
  308.7 57.6 %collective-permute-start.10 = (bf16[512,2048]{1,0:T(8,128)(2,1)}, bf16[512,2048]{1,0:T(8,128)(2,1)}, u32[]{:S(2)}, u32[]{:S(2)}) collective-permute-start(bf16[512,2048]{1,0:T(8,128)(2,1)} %multiply_convert_fusion.n2_ref.refs_0_), channel_id=1, source_target_pairs={{0,1},{1,2},{2,3},{3,0},{4,5},{5,6},{6,7},{7,4},{8,9},{9,10},{10,1... | collective-permute-start | bytes 6291464 | tf_op jit(solution)/shard_map/ppermute | solution.py:65
  366.3 93.5 %collective-permute-start.14 = (bf16[512,2048]{1,0:T(8,128)(2,1)}, bf16[512,2048]{1,0:T(8,128)(2,1)}, u32[]{:S(2)}, u32[]{:S(2)}) collective-permute-start(bf16[512,2048]{1,0:T(8,128)(2,1)} %collective-permute-done.10.n2_ref.refs_1_), channel_id=1, source_target_pairs={{0,1},{1,2},{2,3},{3,0},{4,5},{5,6},{6,7},{7,4},{8,9},{9,10},{10,1... | collective-permute-start | bytes 6291464 | tf_op jit(solution)/shard_map/ppermute | solution.py:65
  368.8 91.0 %collective-permute-start.15 = (bf16[512,2048]{1,0:T(8,128)(2,1)}, bf16[512,2048]{1,0:T(8,128)(2,1)}, u32[]{:S(2)}, u32[]{:S(2)}) collective-permute-start(bf16[512,2048]{1,0:T(8,128)(2,1)} %collective-permute-done.6.c_ref.refs_7_.refs_1_), channel_id=1, source_target_pairs={{0,1},{1,2},{2,3},{3,0},{4,5},{5,6},{6,7},{7,4},{8,9},{9,10},{10,1... | collective-permute-start | bytes 6291464 | tf_op jit(solution)/shard_map/ppermute | solution.py:65
  459.8 81.1 %collective-permute-start.16 = (bf16[512,2048]{1,0:T(8,128)(2,1)}, bf16[512,2048]{1,0:T(8,128)(2,1)}, u32[]{:S(2)}, u32[]{:S(2)}) collective-permute-start(bf16[512,2048]{1,0:T(8,128)(2,1)} %collective-permute-done.14.n2_ref.refs_2_), channel_id=1, source_target_pairs={{0,1},{1,2},{2,3},{3,0},{4,5},{5,6},{6,7},{7,4},{8,9},{9,10},{10,1... | collective-permute-start | bytes 6291464 | tf_op jit(solution)/shard_map/ppermute | solution.py:65
  460.4 94.9 %collective-permute-start.17 = (bf16[512,2048]{1,0:T(8,128)(2,1)}, bf16[512,2048]{1,0:T(8,128)(2,1)}, u32[]{:S(2)}, u32[]{:S(2)}) collective-permute-start(bf16[512,2048]{1,0:T(8,128)(2,1)} %collective-permute-done.15.c_ref.refs_8_.refs_2_), channel_id=1, source_target_pairs={{0,1},{1,2},{2,3},{3,0},{4,5},{5,6},{6,7},{7,4},{8,9},{9,10},{10,1... | collective-permute-start | bytes 6291464 | tf_op jit(solution)/shard_map/ppermute | solution.py:65
  540.5 59.8 %collective-permute-start.19 = (bf16[512,2048]{1,0:T(8,128)(2,1)}, bf16[512,2048]{1,0:T(8,128)(2,1)}, u32[]{:S(2)}, u32[]{:S(2)}) collective-permute-start(bf16[512,2048]{1,0:T(8,128)(2,1)} %get-tuple-element.192), channel_id=1, source_target_pairs={{0,1},{1,2},{2,3},{3,0},{4,5},{5,6},{6,7},{7,4},{8,9},{9,10},{10,1... | collective-permute-start | bytes 6291464 | tf_op jit(solution)/shard_map/ppermute | solution.py:65
  594.6 77.6 %collective-permute-start.18 = (bf16[512,2048]{1,0:T(8,128)(2,1)}, bf16[512,2048]{1,0:T(8,128)(2,1)}, u32[]{:S(2)}, u32[]{:S(2)}) collective-permute-start(bf16[512,2048]{1,0:T(8,128)(2,1)} %get-tuple-element.199), channel_id=1, source_target_pairs={{0,1},{1,2},{2,3},{3,0},{4,5},{5,6},{6,7},{7,4},{8,9},{9,10},{10,1... | collective-permute-start | bytes 6291464 | tf_op jit(solution)/shard_map/ppermute | solution.py:65
  671.9 296.6 %reduce-scatter.7.cloned.1.call-start = ((), (), s32[]{:S(2)}) async-start(), calls=%async_computation.8 | async-start | bytes 18874368 | tf_op jit(solution)/shard_map/reduce_scatter | solution.py:776
  769.4 47.5 %collective-permute-start.21 = (bf16[512,2048]{1,0:T(8,128)(2,1)}, bf16[512,2048]{1,0:T(8,128)(2,1)}, u32[]{:S(2)}, u32[]{:S(2)}) collective-permute-start(bf16[512,2048]{1,0:T(8,128)(2,1)} %add_convert_fusion.5), channel_id=1, source_target_pairs={{0,1},{1,2},{2,3},{3,0},{4,5},{5,6},{6,7},{7,4},{8,9},{9,10},{10,1... | collective-permute-start | bytes 6291464 | tf_op jit(solution)/shard_map/ppermute | solution.py:65
  835.7 241.4 %reduce-scatter.9.cloned.1.call-start = ((), (), s32[]{:S(2)}) async-start(), calls=%async_computation.9 | async-start | bytes 18874368 | tf_op jit(solution)/shard_map/reduce_scatter | solution.py:785
  838.4 47.2 %collective-permute-start.24 = (bf16[512,512]{1,0:T(8,128)(2,1)}, bf16[512,512]{1,0:T(8,128)(2,1)}, u32[]{:S(2)}, u32[]{:S(2)}) collective-permute-start(bf16[512,512]{1,0:T(8,128)(2,1)} %get-tuple-element.340), channel_id=1, source_target_pairs={{0,3},{1,0},{2,1},{3,2},{4,7},{5,4},{6,5},{7,6},{8,11},{9,8},{10,9... | collective-permute-start | bytes 1572872 | tf_op jit(solution)/shard_map/ppermute | solution.py:65
  885.6 252.7 %reduce-scatter.11.cloned.1.call-start = ((), (), s32[]{:S(2)}) async-start(), calls=%async_computation.10 | async-start | bytes 7077888 | tf_op jit(solution)/shard_map/reduce_scatter | solution.py:800
  1081.7 73.7 %collective-permute-start.29 = (bf16[512,2048]{1,0:T(8,128)(2,1)}, bf16[512,2048]{1,0:T(8,128)(2,1)}, u32[]{:S(2)}, u32[]{:S(2)}) collective-permute-start(bf16[512,2048]{1,0:T(8,128)(2,1)} %add_convert_fusion.1), channel_id=1, source_target_pairs={{0,1},{1,2},{2,3},{3,0},{4,5},{5,6},{6,7},{7,4},{8,9},{9,10},{10,1... | collective-permute-start | bytes 6291464 | tf_op jit(solution)/shard_map/ppermute | solution.py:65
  1097.9 47.9 %collective-permute-start.30 = (bf16[256,512]{1,0:T(8,128)(2,1)}, bf16[256,512]{1,0:T(8,128)(2,1)S(1)}, u32[]{:S(2)}, u32[]{:S(2)}) collective-permute-start(bf16[256,512]{1,0:T(8,128)(2,1)} %get-tuple-element.337), channel_id=1, source_target_pairs={{0,1},{1,2},{2,3},{3,0},{4,5},{5,6},{6,7},{7,4},{8,9},{9,10},{10,1... | collective-permute-start | bytes 786440 | tf_op jit(solution)/shard_map/ppermute | solution.py:65
  1101.7 51.6 %collective-permute-start.31 = (bf16[256,512]{1,0:T(8,128)(2,1)}, bf16[256,512]{1,0:T(8,128)(2,1)}, u32[]{:S(2)}, u32[]{:S(2)}) collective-permute-start(bf16[256,512]{1,0:T(8,128)(2,1)} %get-tuple-element.339), channel_id=1, source_target_pairs={{0,2},{1,3},{2,0},{3,1},{4,6},{5,7},{6,4},{7,5},{8,10},{9,11},{10,... | collective-permute-start | bytes 786440 | tf_op jit(solution)/shard_map/ppermute | solution.py:65
  (65 other events, 1307.3 us)
Sparse Core Ops, SparseCore 0:
  10.4 50.4 all-gather.5
  62.8 54.3 all-gather.11
  119.7 125.3 all-gather.7
  257.8 125.0 all-gather.9
  672.0 155.0 reduce-scatter.4
  835.8 117.6 reduce-scatter.6
  957.0 116.0 reduce-scatter.8
  1076.6 61.7 reduce-scatter.10

commit v5 on v4

--- a/solution.py
+++ b/solution.py
@@ -827,7 +827,6 @@
         packed = across(packed, "tp", bits.pop())
     dn1 = plus(dn1_run, part)
     y_run = shift(plus(after(y_run, dn1_run, rest_own), ys[count - 1]).astype(BF), count, 1)
-    qkv_sum = attn_own.astype(F32)
     out_own = rest_own[:, each * ff :]
     out_pieces = [out_own[:, s * local : (s + 1) * local] for s in range(count)]
     out_pieces = exchange(out_pieces, 1)
@@ -846,6 +845,8 @@
     tokens_grad = attn_back + dx1
     y_run = after(y_run, tokens_grad, out_weight_grad)
     layer_out = (x1 + plus(y_run, ys[0])).astype(BF)
+    layer_out = jnp.transpose(layer_out.reshape(seqs, per, depth), (1, 0, 2))
+    qkv_sum = after(attn_own, layer_out, out_weight_grad, packed).astype(F32)
 
     split = depth * EXPERTS // LANES
     across = depth // LANES
@@ -865,7 +866,7 @@
         return jnp.transpose(value.reshape(seqs, per, depth), (1, 0, 2))
 
     return (
-        back_to_positions(layer_out),
+        layer_out,
         back_to_positions(tokens_grad),
         small[0],
         small[1],

time: 1180 us -> 1180 us (level)
    reduce_scatter x1, waiting for transfers between devices: 36.2 us -> 0.01 us  [per_device(): lax.psum_scatter(attn_full, 'fsdp', scatter_dimension=0, tiled=True)]
    ppermute x33, waiting for transfers between devices: 244 us -> 280 us  [shift(): lax.ppermute(value, 'tp', [(i, (i + step) % count) for i in range(count)])]
  transfers between devices with their start and end apart: 46 -> 46, of which waited for: 21 -> 22; matrix products, arithmetic and copies ran while one was open for 10% -> 11% of each run, Pallas kernels for 56% -> 56%
where the time goes in v5:
time: 1180 us; the launch traced here: 1170 us
  Pallas kernels  654 us (55%)
  waiting for transfers between devices  299 us (25%)
  other arithmetic  79.9 us (7%)
  starting transfers between devices  66.2 us (6%)
  local copies, waits for them, and re-layouts  58.6 us (5%)
  between operations  15.1 us (1%)
    pallas_call x8, Pallas kernels, experts_pass(): pl.pallas_call(functools.partial(expert_kernel, group, experts), grid=(ex...  325 us
    ppermute x33, waiting for transfers between devices, shift(): lax.ppermute(value, 'tp', [(i, (i + step) % count) for i in range(count)])  280 us
    pallas_call x4, Pallas kernels, row_grads(): pl.pallas_call(functools.partial(row_grad_kernel, len(dls), tuple(plan),...  181 us
    ppermute x33, starting transfers between devices, shift(): lax.ppermute(value, 'tp', [(i, (i + step) % count) for i in range(count)])  60.3 us
    pallas_call x1, Pallas kernels, attend_back(): pl.pallas_call(functools.partial(attend_back_kernel, scale), grid=(seqs,...  38.6 us
    pallas_call x4, Pallas kernels, project(): pl.pallas_call(functools.partial(qkv_kernel, seqs), grid=(groups,), in_sp...  35.8 us
    pallas_call x4, Pallas kernels, input_back(): pl.pallas_call(input_back_kernel, grid=(depth // tile,), in_specs=[grad]...  31.7 us
  transfers between devices with their start and end apart: 46, of which 22 were waited for; matrix products, arithmetic and copies ran while one was open for 11% of the time, Pallas kernels for 56%

profile of v5, /device:TPU:0, one launch (start us, length us, event | category | flops | bytes accessed | tf_op | source)
XLA Modules:
  0.0 1172.7 jit_solution(9437046523928353756)
XLA Ops:
  61.9 31.5 %collective-permute-done.3.x_ref.refs_1_ = bf16[512,2048]{1,0:T(8,128)(2,1)} collective-permute-done((bf16[512,2048]{1,0:T(8,128)(2,1)}, bf16[512,2048]{1,0:T(8,128)(2,1)}, u32[]{:S(2)}, u32[]{:S(2)}) %collective-permute-start.3) | collective-permute-done | bytes 2097184 | tf_op jit(solution)/shard_map/ppermute | solution.py:65
  120.3 22.0 %collective-permute-done.4.x_ref.refs_2_ = bf16[512,2048]{1,0:T(8,128)(2,1)S(1)} collective-permute-done((bf16[512,2048]{1,0:T(8,128)(2,1)}, bf16[512,2048]{1,0:T(8,128)(2,1)S(1)}, u32[]{:S(2)}, u32[]{:S(2)}) %collective-permute-start.4) | collective-permute-done | bytes 2097184 | tf_op jit(solution)/shard_map/ppermute | solution.py:65
  151.2 36.7 %collective-permute-done.13 = s32[16,512]{1,0:T(8,128)S(1)} collective-permute-done((s32[16,512]{1,0:T(8,128)S(1)}, s32[16,512]{1,0:T(8,128)S(1)}, u32[]{:S(2)}, u32[]{:S(2)}) %collective-permute-start.13) | collective-permute-done | bytes 32800 | tf_op jit(solution)/shard_map/ppermute | solution.py:65
  212.6 18.3 %attend.1 = (bf16[4,2,256,512]{3,2,1,0:T(8,128)(2,1)}, f32[8,4,256]{2,1,0:T(4,128)}) custom-call(bf16[4,2,256,512]{3,2,1,0:T(8,128)(2,1)} %get-tuple-element.159.q_ref.refs_0_, bf16[4,2,256,512]{3,2,1,0:T(8,128)(2,1)} %get-tuple-element.160.k_ref.refs_1_, bf16[4,2,256,512]{3,2,1,0:T(8,128)(2,1)} %get-tuple-element.161.v_ref.refs_2_, ...), custom_call_target="tpu_custom_call" | custom-call | flops 68719476736 | bytes 8388608 | tf_op jit(solution)/shard_map/attend/pallas_call | solution.py:191
  230.9 20.6 %collective-permute-done.6.c_ref.refs_7_.refs_1_ = bf16[512,2048]{1,0:T(8,128)(2,1)} collective-permute-done((bf16[512,2048]{1,0:T(8,128)(2,1)S(1)}, bf16[512,2048]{1,0:T(8,128)(2,1)}, u32[]{:S(2)}, u32[]{:S(2)}) %collective-permute-start.6) | collective-permute-done | bytes 2097184 | tf_op jit(solution)/shard_map/ppermute | solution.py:65
  270.6 20.7 %collective-permute-done.8.refs_2_.refs_8_ = bf16[512,512]{1,0:T(8,128)(2,1)S(1)} collective-permute-done((bf16[512,512]{1,0:T(8,128)(2,1)S(1)}, bf16[512,512]{1,0:T(8,128)(2,1)S(1)}, u32[]{:S(2)}, u32[]{:S(2)}) %collective-permute-start.8) | collective-permute-done | bytes 524320 | tf_op jit(solution)/shard_map/ppermute | solution.py:65
  308.7 12.5 %collective-permute-start.10 = (bf16[512,2048]{1,0:T(8,128)(2,1)}, bf16[512,2048]{1,0:T(8,128)(2,1)}, u32[]{:S(2)}, u32[]{:S(2)}) collective-permute-start(bf16[512,2048]{1,0:T(8,128)(2,1)} %multiply_convert_fusion.n2_ref.refs_0_), channel_id=1, source_target_pairs={{0,1},{1,2},{2,3},{3,0},{4,5},{5,6},{6,7},{7,4},{8,9},{9,10},{10,1... | collective-permute-start | bytes 6291464 | tf_op jit(solution)/shard_map/ppermute | solution.py:65
  321.8 39.9 %experts_0.4 = (bf16[4,512,2048]{2,1,0:T(8,128)(2,1)}, bf16[4,512,2048]{2,1,0:T(8,128)(2,1)}, bf16[4,512,2048]{2,1,0:T(8,128)(2,1)}, bf16[512,2048]{1,0:T(8,128)...) custom-call(bf16[512,2048]{1,0:T(8,128)(2,1)} %multiply_convert_fusion.n2_ref.refs_0_, ...), custom_call_target="tpu_custom_call" | custom-call | flops 412316860416 | bytes 65011712 | tf_op jit(solution)/shard_map/experts_0/pallas_call | solution.py:474
  369.3 39.3 %experts_0.5 = (bf16[4,512,2048]{2,1,0:T(8,128)(2,1)}, bf16[4,512,2048]{2,1,0:T(8,128)(2,1)}, bf16[4,512,2048]{2,1,0:T(8,128)(2,1)}, bf16[512,2048]{1,0:T(8,128)...) custom-call(bf16[512,2048]{1,0:T(8,128)(2,1)} %collective-permute-do, ...), custom_call_target="tpu_custom_call", output_to_operand_aliasing={{0}: (8, {}), {1}: (9, {}), {2}: (10, {})} | custom-call | flops 412316860416 | bytes 65011712 | tf_op jit(solution)/shard_map/experts_0/pallas_call | solution.py:474
  408.6 40.0 %experts_1.4 = (bf16[4,512,2048]{2,1,0:T(8,128)(2,1)}, bf16[4,512,2048]{2,1,0:T(8,128)(2,1)}, bf16[4,512,2048]{2,1,0:T(8,128)(2,1)}, bf16[512,2048]{1,0:T(8,128)...) custom-call(bf16[512,2048]{1,0:T(8,128)(2,1)} %multiply_convert_fusion.n2_ref.refs_0_, ...), custom_call_target="tpu_custom_call" | custom-call | flops 412316860416 | bytes 65011712 | tf_op jit(solution)/shard_map/experts_1/pallas_call | solution.py:474
  461.3 39.1 %experts_0.6 = (bf16[4,512,2048]{2,1,0:T(8,128)(2,1)}, bf16[4,512,2048]{2,1,0:T(8,128)(2,1)}, bf16[4,512,2048]{2,1,0:T(8,128)(2,1)}, bf16[512,2048]{1,0:T(8,128)...) custom-call(bf16[512,2048]{1,0:T(8,128)(2,1)} %collective-permute-do, ...), custom_call_target="tpu_custom_call", output_to_operand_aliasing={{0}: (8, {}), {1}: (9, {}), {2}: (10, {})} | custom-call | flops 412316860416 | bytes 65011712 | tf_op jit(solution)/shard_map/experts_0/pallas_call | solution.py:474
  500.4 40.1 %experts_1.5 = (bf16[4,512,2048]{2,1,0:T(8,128)(2,1)}, bf16[4,512,2048]{2,1,0:T(8,128)(2,1)}, bf16[4,512,2048]{2,1,0:T(8,128)(2,1)}, bf16[512,2048]{1,0:T(8,128)...) custom-call(bf16[512,2048]{1,0:T(8,128)(2,1)} %collective-permute-do, ...), custom_call_target="tpu_custom_call", output_to_operand_aliasing={{0}: (10, {}), {1}: (11, {}), {2}: (12, {})} | custom-call | flops 412316860416 | bytes 65011712 | tf_op jit(solution)/shard_map/experts_1/pallas_call | solution.py:474
  540.8 14.5 %collective-permute-done.17.c_ref.refs_9_.refs_3_ = bf16[512,2048]{1,0:T(8,128)(2,1)} collective-permute-done((bf16[512,2048]{1,0:T(8,128)(2,1)}, bf16[512,2048]{1,0:T(8,128)(2,1)}, u32[]{:S(2)}, u32[]{:S(2)}) %collective-permute-start.17) | collective-permute-done | bytes 2097184 | tf_op jit(solution)/shard_map/ppermute | solution.py:65
  555.4 39.2 %experts_0.7 = (bf16[4,512,2048]{2,1,0:T(8,128)(2,1)}, bf16[4,512,2048]{2,1,0:T(8,128)(2,1)}, bf16[4,512,2048]{2,1,0:T(8,128)(2,1)}, bf16[512,2048]{1,0:T(8,128)...) custom-call(bf16[512,2048]{1,0:T(8,128)(2,1)} %collective-permute-do, ...), custom_call_target="tpu_custom_call", output_to_operand_aliasing={{0}: (8, {}), {1}: (9, {}), {2}: (10, {})} | custom-call | flops 412316860416 | bytes 65011712 | tf_op jit(solution)/shard_map/experts_0/pallas_call | solution.py:474
  600.3 71.6 %experts_first_grads.1 = bf16[2048,6144]{1,0:T(8,128)(2,1)} custom-call(bf16[512,2048]{1,0:T(8,128)(2,1)} %multiply_convert_fusion.n2_ref.refs_0_, bf16[512,2048]{1,0:T(8,128)(2,1)} %collective-permute-done.10.n2_ref.refs_1_, bf16[512,2048]{1,0:T(8,128)(2,1)} %collective-permute-done.14.n2_ref.refs_2_, ...), custom_call_target="tpu_custom_call" | custom-call | flops 824633720832 | bytes 41943040 | tf_op jit(solution)/shard_map/experts_first_grads/pallas_call | solution.py:592
  672.2 45.9 %experts_1.6 = (bf16[4,512,2048]{2,1,0:T(8,128)(2,1)}, bf16[4,512,2048]{2,1,0:T(8,128)(2,1)}, bf16[4,512,2048]{2,1,0:T(8,128)(2,1)}, bf16[512,2048]{1,0:T(8,128)...) custom-call(bf16[512,2048]{1,0:T(8,128)(2,1)} %collective-permute-do, ...), custom_call_target="tpu_custom_call", output_to_operand_aliasing={{0}: (10, {}), {1}: (11, {}), {2}: (12, {})} | custom-call | flops 412316860416 | bytes 65011712 | tf_op jit(solution)/shard_map/experts_1/pallas_call | solution.py:474
  722.6 41.4 %experts_1.7 = (bf16[4,512,2048]{2,1,0:T(8,128)(2,1)}, bf16[4,512,2048]{2,1,0:T(8,128)(2,1)}, bf16[4,512,2048]{2,1,0:T(8,128)(2,1)}, bf16[512,2048]{1,0:T(8,128)...) custom-call(bf16[512,2048]{1,0:T(8,128)(2,1)} %collective-permute-do, ...), custom_call_target="tpu_custom_call", output_to_operand_aliasing={{0}: (10, {}), {1}: (11, {}), {2}: (12, {})} | custom-call | flops 412316860416 | bytes 65011712 | tf_op jit(solution)/shard_map/experts_1/pallas_call | solution.py:474
  769.8 47.0 %experts_last_grads.1 = (bf16[2048,4096]{1,0:T(8,128)(2,1)}, f32[2048,128]{1,0:T(8,128)}) custom-call(bf16[512,2048]{1,0:T(8,128)(2,1)} %multiply_convert_fusion.n2_ref.refs_0_, bf16[512,2048]{1,0:T(8,128)(2,1)} %collective-permute-done.10.n2_ref.refs_1_, bf16[512,2048]{1,0:T(8,128)(2,1)} %collective-permute-done.14.n2_ref.refs_2_, ...), custom_call_target="tpu_custom_call" | custom-call | flops 549755813888 | bytes 33554432 | tf_op jit(solution)/shard_map/experts_last_grads/pallas_call | solution.py:592
  843.4 38.4 %rest_grads.1 = bf16[2048,4096]{1,0:T(8,128)(2,1)} custom-call(bf16[512,2048]{1,0:T(8,128)(2,1)} %copy-done.14, bf16[512,2048]{1,0:T(8,128)(2,1)} %collective-permute-done.6.c_ref.refs_7_.refs_1_, bf16[512,2048]{1,0:T(8,128)(2,1)} %collective-permute-done.15.c_ref.refs_8_.refs_2_, bf16[512,2048]{1,0:T(8,128)(2,1)} %collective-permute-done.17.c_ref.refs_9_.refs_3_, ...), custom_call_target="tpu_custom_call" | custom-call | flops 21474836480 | bytes 33554432 | tf_op jit(solution)/shard_map/rest_grads/pallas_call | solution.py:592
  888.3 38.6 %attend_back.1 = (bf16[4,2,256,512]{3,2,1,0:T(8,128)(2,1)}, bf16[4,2,256,512]{3,2,1,0:T(8,128)(2,1)}, bf16[4,2,256,512]{3,2,1,0:T(8,128)(2,1)}, f32[8,128]{1,0:T(8,128)}) custom-call(bf16[4,2,256,512]{3,2,1,0:T(8,128)(2,1)} %get-tuple-element.159.q_ref.refs_0_, bf16[4,2,256,512]{3,2,1,0:T(8,128)(2,1)} %get-tuple-element.160.k_ref.refs_1_, ...), custom_call_target="tpu_custom_call" | custom-call | flops 171798691840 | bytes 25165824 | tf_op jit(solution)/shard_map/attend_back/pallas_call | solution.py:275
  936.5 23.9 %qkv_grads.1 = (bf16[2048,1536]{1,0:T(8,128)(2,1)}, f32[2048,128]{1,0:T(8,128)}) custom-call(bf16[512,2048]{1,0:T(8,128)(2,1)} %multiply_convert_fusion.1.x_ref.refs_0_, bf16[512,2048]{1,0:T(8,128)(2,1)} %collective-permute-done.3.x_ref.refs_1_, bf16[512,2048]{1,0:T(8,128)(2,1)} %copy-done.12, bf16[512,2048]{1,0:T(8,128)(2,1)} %collective-permute-done.5.x_ref.refs_3_, ...), custom_call_target="tpu_custom_call" | custom-call | flops 12884901888 | bytes 23068672 | tf_op jit(solution)/shard_map/qkv_grads/pallas_call | solution.py:592
  990.3 31.1 %collective-permute-done.27 = bf16[512,2048]{1,0:T(8,128)(2,1)} collective-permute-done((bf16[512,2048]{1,0:T(8,128)(2,1)S(1)}, bf16[512,2048]{1,0:T(8,128)(2,1)}, u32[]{:S(2)}, u32[]{:S(2)}) %collective-permute-start.27) | collective-permute-done | bytes 2097184 | tf_op jit(solution)/shard_map/ppermute | solution.py:65
  1059.5 13.2 %collective-permute-done.36 = f32[290,128]{1,0:T(8,128)S(1)} collective-permute-done((f32[290,128]{1,0:T(8,128)S(1)}, f32[290,128]{1,0:T(8,128)S(1)}, u32[]{:S(2)}, u32[]{:S(2)}) %collective-permute-start.36) | collective-permute-done | bytes 148512 | tf_op jit(solution)/shard_map/ppermute | solution.py:809
  1110.1 28.0 %collective-permute-done.30 = bf16[256,512]{1,0:T(8,128)(2,1)S(1)} collective-permute-done((bf16[256,512]{1,0:T(8,128)(2,1)}, bf16[256,512]{1,0:T(8,128)(2,1)S(1)}, u32[]{:S(2)}, u32[]{:S(2)}) %collective-permute-start.30) | collective-permute-done | bytes 262176 | tf_op jit(solution)/shard_map/ppermute | solution.py:65
  (274 shorter events, 364.2 us)
Async XLA Ops:
  7.2 86.2 %all-gather.6.cloned.1.call-start = ((), (), s32[]{:S(2)}) async-start(), calls=%async_computation.4 | async-start | bytes 7667712 | tf_op jit(solution)/shard_map/all_gather | solution.py:650
  10.3 251.2 %all-gather.12.cloned.1.call-start = ((), (), s32[]{:S(2)}) async-start(), calls=%async_computation.11 | async-start | bytes 9437184 | tf_op jit(solution)/shard_map/all_gather | solution.py:669
  41.1 280.1 %all-gather.8.cloned.1.call-start = ((), (), s32[]{:S(2)}) async-start(), calls=%async_computation.5 | async-start | bytes 28311552 | tf_op jit(solution)/shard_map/all_gather | solution.py:669
  41.1 52.2 %collective-permute-start.3 = (bf16[512,2048]{1,0:T(8,128)(2,1)}, bf16[512,2048]{1,0:T(8,128)(2,1)}, u32[]{:S(2)}, u32[]{:S(2)}) collective-permute-start(bf16[512,2048]{1,0:T(8,128)(2,1)} %multiply_convert_fusion.1.x_ref.refs_0_), channel_id=1, source_target_pairs={{0,1},{1,2},{2,3},{3,0},{4,5},{5,6},{6,7},{7,4},{8,9},{9,10},{10,1... | collective-permute-start | bytes 6291464 | tf_op jit(solution)/shard_map/ppermute | solution.py:65
  93.4 315.1 %all-gather.10.cloned.1.call-start = ((), (), s32[]{:S(2)}) async-start(), calls=%async_computation.6 | async-start | bytes 28311552 | tf_op jit(solution)/shard_map/all_gather | solution.py:669
  93.5 48.8 %collective-permute-start.4 = (bf16[512,2048]{1,0:T(8,128)(2,1)}, bf16[512,2048]{1,0:T(8,128)(2,1)S(1)}, u32[]{:S(2)}, u32[]{:S(2)}) collective-permute-start(bf16[512,2048]{1,0:T(8,128)(2,1)} %collective-permute-done.3.x_ref.refs_1_), channel_id=1, source_target_pairs={{0,1},{1,2},{2,3},{3,0},{4,5},{5,6},{6,7},{7,4},{8,9},{9,10},{10,1... | collective-permute-start | bytes 6291464 | tf_op jit(solution)/shard_map/ppermute | solution.py:65
  142.3 59.5 %collective-permute-start.5 = (bf16[512,2048]{1,0:T(8,128)(2,1)S(1)}, bf16[512,2048]{1,0:T(8,128)(2,1)}, u32[]{:S(2)}, u32[]{:S(2)}) collective-permute-start(bf16[512,2048]{1,0:T(8,128)(2,1)S(1)} %collective-permute-done.4.x_ref.refs_2_), channel_id=1, source_target_pairs={{0,1},{1,2},{2,3},{3,0},{4,5},{5,6},{6,7},{7,4},{8,9},{9,10},{10,1... | collective-permute-start | bytes 6291464 | tf_op jit(solution)/shard_map/ppermute | solution.py:65
  201.7 49.7 %collective-permute-start.6 = (bf16[512,2048]{1,0:T(8,128)(2,1)S(1)}, bf16[512,2048]{1,0:T(8,128)(2,1)}, u32[]{:S(2)}, u32[]{:S(2)}) collective-permute-start(bf16[512,2048]{1,0:T(8,128)(2,1)S(1)} %bitcast_select_fusion.c_ref.refs_6_.refs_0_), channel_id=1, source_target_pairs={{0,1},{1,2},{2,3},{3,0},{4,5},{5,6},{6,7},{7,4},{8,9},{9,10},{10,1... | collective-permute-start | bytes 6291464 | tf_op jit(solution)/shard_map/ppermute | solution.py:65
  257.7 578.0 %reduce-scatter.5.cloned.1.call-start = ((), (), s32[]{:S(2)}) async-start(), calls=%async_computation.7 | async-start | bytes 28311552 | tf_op jit(solution)/shard_map/reduce_scatter | solution.py:756
  308.7 57.6 %collective-permute-start.10 = (bf16[512,2048]{1,0:T(8,128)(2,1)}, bf16[512,2048]{1,0:T(8,128)(2,1)}, u32[]{:S(2)}, u32[]{:S(2)}) collective-permute-start(bf16[512,2048]{1,0:T(8,128)(2,1)} %multiply_convert_fusion.n2_ref.refs_0_), channel_id=1, source_target_pairs={{0,1},{1,2},{2,3},{3,0},{4,5},{5,6},{6,7},{7,4},{8,9},{9,10},{10,1... | collective-permute-start | bytes 6291464 | tf_op jit(solution)/shard_map/ppermute | solution.py:65
  366.3 93.5 %collective-permute-start.14 = (bf16[512,2048]{1,0:T(8,128)(2,1)}, bf16[512,2048]{1,0:T(8,128)(2,1)}, u32[]{:S(2)}, u32[]{:S(2)}) collective-permute-start(bf16[512,2048]{1,0:T(8,128)(2,1)} %collective-permute-done.10.n2_ref.refs_1_), channel_id=1, source_target_pairs={{0,1},{1,2},{2,3},{3,0},{4,5},{5,6},{6,7},{7,4},{8,9},{9,10},{10,1... | collective-permute-start | bytes 6291464 | tf_op jit(solution)/shard_map/ppermute | solution.py:65
  368.8 91.0 %collective-permute-start.15 = (bf16[512,2048]{1,0:T(8,128)(2,1)}, bf16[512,2048]{1,0:T(8,128)(2,1)}, u32[]{:S(2)}, u32[]{:S(2)}) collective-permute-start(bf16[512,2048]{1,0:T(8,128)(2,1)} %collective-permute-done.6.c_ref.refs_7_.refs_1_), channel_id=1, source_target_pairs={{0,1},{1,2},{2,3},{3,0},{4,5},{5,6},{6,7},{7,4},{8,9},{9,10},{10,1... | collective-permute-start | bytes 6291464 | tf_op jit(solution)/shard_map/ppermute | solution.py:65
  459.8 81.1 %collective-permute-start.16 = (bf16[512,2048]{1,0:T(8,128)(2,1)}, bf16[512,2048]{1,0:T(8,128)(2,1)}, u32[]{:S(2)}, u32[]{:S(2)}) collective-permute-start(bf16[512,2048]{1,0:T(8,128)(2,1)} %collective-permute-done.14.n2_ref.refs_2_), channel_id=1, source_target_pairs={{0,1},{1,2},{2,3},{3,0},{4,5},{5,6},{6,7},{7,4},{8,9},{9,10},{10,1... | collective-permute-start | bytes 6291464 | tf_op jit(solution)/shard_map/ppermute | solution.py:65
  460.4 94.9 %collective-permute-start.17 = (bf16[512,2048]{1,0:T(8,128)(2,1)}, bf16[512,2048]{1,0:T(8,128)(2,1)}, u32[]{:S(2)}, u32[]{:S(2)}) collective-permute-start(bf16[512,2048]{1,0:T(8,128)(2,1)} %collective-permute-done.15.c_ref.refs_8_.refs_2_), channel_id=1, source_target_pairs={{0,1},{1,2},{2,3},{3,0},{4,5},{5,6},{6,7},{7,4},{8,9},{9,10},{10,1... | collective-permute-start | bytes 6291464 | tf_op jit(solution)/shard_map/ppermute | solution.py:65
  540.5 59.8 %collective-permute-start.19 = (bf16[512,2048]{1,0:T(8,128)(2,1)}, bf16[512,2048]{1,0:T(8,128)(2,1)}, u32[]{:S(2)}, u32[]{:S(2)}) collective-permute-start(bf16[512,2048]{1,0:T(8,128)(2,1)} %get-tuple-element.193), channel_id=1, source_target_pairs={{0,1},{1,2},{2,3},{3,0},{4,5},{5,6},{6,7},{7,4},{8,9},{9,10},{10,1... | collective-permute-start | bytes 6291464 | tf_op jit(solution)/shard_map/ppermute | solution.py:65
  594.6 77.6 %collective-permute-start.18 = (bf16[512,2048]{1,0:T(8,128)(2,1)}, bf16[512,2048]{1,0:T(8,128)(2,1)}, u32[]{:S(2)}, u32[]{:S(2)}) collective-permute-start(bf16[512,2048]{1,0:T(8,128)(2,1)} %get-tuple-element.200), channel_id=1, source_target_pairs={{0,1},{1,2},{2,3},{3,0},{4,5},{5,6},{6,7},{7,4},{8,9},{9,10},{10,1... | collective-permute-start | bytes 6291464 | tf_op jit(solution)/shard_map/ppermute | solution.py:65
  671.9 296.6 %reduce-scatter.7.cloned.1.call-start = ((), (), s32[]{:S(2)}) async-start(), calls=%async_computation.8 | async-start | bytes 18874368 | tf_op jit(solution)/shard_map/reduce_scatter | solution.py:776
  769.4 47.5 %collective-permute-start.21 = (bf16[512,2048]{1,0:T(8,128)(2,1)}, bf16[512,2048]{1,0:T(8,128)(2,1)}, u32[]{:S(2)}, u32[]{:S(2)}) collective-permute-start(bf16[512,2048]{1,0:T(8,128)(2,1)} %add_convert_fusion.5), channel_id=1, source_target_pairs={{0,1},{1,2},{2,3},{3,0},{4,5},{5,6},{6,7},{7,4},{8,9},{9,10},{10,1... | collective-permute-start | bytes 6291464 | tf_op jit(solution)/shard_map/ppermute | solution.py:65
  835.7 241.4 %reduce-scatter.9.cloned.1.call-start = ((), (), s32[]{:S(2)}) async-start(), calls=%async_computation.9 | async-start | bytes 18874368 | tf_op jit(solution)/shard_map/reduce_scatter | solution.py:785
  838.4 47.2 %collective-permute-start.24 = (bf16[512,512]{1,0:T(8,128)(2,1)}, bf16[512,512]{1,0:T(8,128)(2,1)}, u32[]{:S(2)}, u32[]{:S(2)}) collective-permute-start(bf16[512,512]{1,0:T(8,128)(2,1)} %get-tuple-element.342), channel_id=1, source_target_pairs={{0,3},{1,0},{2,1},{3,2},{4,7},{5,4},{6,5},{7,6},{8,11},{9,8},{10,9... | collective-permute-start | bytes 1572872 | tf_op jit(solution)/shard_map/ppermute | solution.py:65
  885.6 277.7 %reduce-scatter.11.cloned.1.call-start = ((), (), s32[]{:S(2)}) async-start(), calls=%async_computation.10 | async-start | bytes 7077888 | tf_op jit(solution)/shard_map/reduce_scatter | solution.py:800
  1026.1 46.6 %collective-permute-start.28 = (bf16[512,2048]{1,0:T(8,128)(2,1)}, bf16[512,2048]{1,0:T(8,128)(2,1)}, u32[]{:S(2)}, u32[]{:S(2)}) collective-permute-start(bf16[512,2048]{1,0:T(8,128)(2,1)} %add_convert_fusion.2), channel_id=1, source_target_pairs={{0,1},{1,2},{2,3},{3,0},{4,5},{5,6},{6,7},{7,4},{8,9},{9,10},{10,1... | collective-permute-start | bytes 6291464 | tf_op jit(solution)/shard_map/ppermute | solution.py:65
  1081.7 73.7 %collective-permute-start.29 = (bf16[512,2048]{1,0:T(8,128)(2,1)}, bf16[512,2048]{1,0:T(8,128)(2,1)}, u32[]{:S(2)}, u32[]{:S(2)}) collective-permute-start(bf16[512,2048]{1,0:T(8,128)(2,1)} %add_convert_fusion.1), channel_id=1, source_target_pairs={{0,1},{1,2},{2,3},{3,0},{4,5},{5,6},{6,7},{7,4},{8,9},{9,10},{10,1... | collective-permute-start | bytes 6291464 | tf_op jit(solution)/shard_map/ppermute | solution.py:65
  1103.0 50.3 %collective-permute-start.31 = (bf16[256,512]{1,0:T(8,128)(2,1)}, bf16[256,512]{1,0:T(8,128)(2,1)}, u32[]{:S(2)}, u32[]{:S(2)}) collective-permute-start(bf16[256,512]{1,0:T(8,128)(2,1)} %get-tuple-element.341), channel_id=1, source_target_pairs={{0,2},{1,3},{2,0},{3,1},{4,6},{5,7},{6,4},{7,5},{8,10},{9,11},{10,... | collective-permute-start | bytes 786440 | tf_op jit(solution)/shard_map/ppermute | solution.py:65
  (65 other events, 1262.4 us)
Sparse Core Ops, SparseCore 0:
  10.4 50.4 all-gather.5
  62.8 54.3 all-gather.11
  119.7 125.3 all-gather.7
  257.8 125.0 all-gather.9
  672.0 155.0 reduce-scatter.4
  835.8 117.6 reduce-scatter.6
  957.0 116.0 reduce-scatter.8
  1076.6 61.7 reduce-scatter.10
